TPU v7x, 32 devices: a whole 2x2x4 slice. The times are simulated.
32 devices in a mesh: grp: 2 (over x), ep: 16 (over z, y, core).
Axes of the slice: x: 2, y: 2, z: 4, core: 2. Of those that a mesh axis runs over, the one named last changes fastest.
Arguments:
- hidden_in: bfloat16 [2048, 4096], P(('grp', 'ep')), parts along dimension 0, may hold values from -3 to 3
- queries: bfloat16 [2048, 4096], P(('grp', 'ep')), parts along dimension 0, may hold values from -6 to 6
- token_keys: bfloat16 [2048, 256], P(('grp', 'ep')), parts along dimension 0, may hold values from -6 to 6
- token_values: bfloat16 [2048, 256], P(('grp', 'ep')), parts along dimension 0, may hold values from -15 to 15
- stored_keys: bfloat16 [32768, 256], P(('grp', 'ep')), parts along dimension 0, may hold values from -6 to 6
- stored_values: bfloat16 [32768, 256], P(('grp', 'ep')), parts along dimension 0, may hold values from -15 to 15
- cache_len: int32 [32], P(('grp', 'ep')), parts along dimension 0, may hold values from 1 to 1024, 8192 in all
- query_gain: float32 [128], replicated, may hold values from 0.5 to 2.5
- k_gain: float32 [128], replicated, may hold values from 0.25 to 1.75
- norm_gain: float32 [4096], replicated, may hold values from 0.25 to 1.75
- expert_ids: int32 [2048, 2], P(('grp', 'ep')), parts along dimension 0, may hold values from 0 to 7, as said below
- gate_weights: float32 [2048, 2], P(('grp', 'ep')), parts along dimension 0, may hold values from 0.05 to 0.6
- w_gate: bfloat16 [4096, 6144], P(None, 'ep'), may hold values from -0.09375 to 0.09375
- w_up: bfloat16 [4096, 6144], P(None, 'ep'), may hold values from -0.09375 to 0.09375
- w_down: bfloat16 [6144, 4096], P('ep'), may hold values from -0.21875 to 0.21875
Outputs:
- layer_out: bfloat16 [2048, 4096], P(('grp', 'ep')), parts along dimension 0
There are 2 independent parts, one for each index of `grp`. A program takes and returns all parts, laid end to end along the dimension named above; an argument that names none is the same for every part. Nothing has to cross between parts.
Inputs may be any that keep to these rules, and one draw needn't show every extreme that they name: `expert_ids`: each row names 2 different experts. In each aligned block of 32 rows no expert is named by more than 16 rows, and one expert, the same in every block, is named by exactly 16 rows in every block.
All inputs are finite; a program needn't handle non-finite values. No bound on the sum of `cache_len` on one device may be relied on, other than what follows from the above.
Results may differ from a plain program's by a relative error of at most 0.0095.
Values may be sent and summed in bfloat16 or wider, within the bound.
No kernel may reach another device: no remote copies, remote signals or barrier semaphores. Data moves between devices by JAX's collectives and lax.ppermute only.
A program may use at most 128 MiB of HBM per device.

v0:
```python
import math

import jax
import jax.numpy as jnp
from jax import lax
from jax.sharding import PartitionSpec as P

EPS = 1e-06


def swapped(value, axis, distance):
    return lax.ppermute(value, axis, [(i, i ^ 1 << distance) for i in range(lax.axis_size(axis))])


def normalized_rows(values_in, gain_vec):
    return (
        values_in
        * lax.rsqrt(jnp.mean(values_in * values_in, axis=-1, keepdims=True) + EPS)
        * gain_vec
    )


def attend_rows(query_slice, key_normed, joined_values, length, query_gain, cache_rows):
    row_count = query_slice.shape[0]
    heads_kv = key_normed.shape[1]
    head_dim = key_normed.shape[2]
    query_normalized = normalized_rows(
        query_slice.reshape(row_count, heads_kv, -1, head_dim).astype(jnp.float32), query_gain
    ).astype(jnp.bfloat16)
    scores = jnp.einsum(
        "tkgd,skd->ktgs", query_normalized, key_normed, preferred_element_type=jnp.float32
    ) / math.sqrt(head_dim)
    key_spots = jnp.arange(key_normed.shape[0], dtype=jnp.int32)
    query_rows = jnp.arange(row_count, dtype=jnp.int32)
    live_key = jnp.where(
        key_spots[None, :] < cache_rows,
        key_spots[None, :] < length,
        key_spots[None, :] - cache_rows <= query_rows[:, None],
    )
    raised = jnp.where(live_key[None, :, None, :], jnp.exp(scores), 0.0)
    probs = (raised / jnp.sum(raised, axis=-1, keepdims=True)).astype(jnp.bfloat16)
    attended = jnp.einsum(
        "ktgs,skd->tkgd", probs, joined_values, preferred_element_type=jnp.float32
    ).astype(jnp.bfloat16)
    return attended.reshape(row_count, -1)


def expert_apply(rows_in, w_gate, w_up, w_down):
    gate_pre = jnp.dot(rows_in, w_gate, preferred_element_type=jnp.float32)
    up_pre = jnp.dot(rows_in, w_up, preferred_element_type=jnp.float32)
    inner = (jax.nn.silu(gate_pre) * up_pre).astype(jnp.bfloat16)
    return jnp.dot(inner, w_down, preferred_element_type=jnp.float32)


def expert_block(normed_rows, route_ids, route_gates, residual, w_gate, w_up, w_down):
    row_count, top_count = route_ids.shape
    feat_width = normed_rows.shape[1]
    half_width = feat_width // 2
    ep_size = lax.axis_size("ep")
    experts = ep_size // 2
    slot_count = 2 * row_count * top_count // experts
    recv_rows = ep_size * slot_count
    flat_ids = route_ids.reshape(-1)
    one_hot = (flat_ids[:, None] == jnp.arange(experts, dtype=jnp.int32)[None, :]).astype(jnp.int32)
    earlier = jnp.cumsum(one_hot, axis=0) - one_hot
    rank_in = jnp.sum(earlier * one_hot, axis=1)
    slot_index = flat_ids * slot_count + rank_in
    source_row = (
        jnp.full((experts * slot_count,), row_count, jnp.int32)
        .at[slot_index]
        .set(jnp.arange(row_count * top_count, dtype=jnp.int32) // top_count)
    )
    padded_rows = jnp.concatenate([normed_rows, jnp.zeros((1, feat_width), jnp.bfloat16)], axis=0)
    outgoing = padded_rows[source_row].reshape(experts, slot_count, feat_width)
    parity = lax.axis_index("ep") % 2
    sendbuf = jnp.broadcast_to(outgoing[:, None], (experts, 2, slot_count, feat_width)).reshape(
        ep_size, slot_count, feat_width
    )
    arrived = lax.all_to_all(sendbuf, "ep", split_axis=0, concat_axis=0, tiled=True)
    gathered_rows = arrived.reshape(recv_rows, feat_width)
    partial_value = expert_apply(gathered_rows, w_gate, w_up, w_down)
    kept_half = lax.dynamic_slice_in_dim(partial_value, parity * half_width, half_width, 1).astype(
        jnp.bfloat16
    )
    sent_half = lax.dynamic_slice_in_dim(
        partial_value, (1 - parity) * half_width, half_width, 1
    ).astype(jnp.bfloat16)
    received = swapped(sent_half, "ep", 0)
    half_out = (kept_half.astype(jnp.float32) + received.astype(jnp.float32)).astype(jnp.bfloat16)
    returned = lax.all_to_all(
        half_out.reshape(ep_size, slot_count, half_width),
        "ep",
        split_axis=0,
        concat_axis=0,
        tiled=True,
    )
    expert_out = (
        returned.reshape(experts, 2, slot_count, half_width)
        .transpose(0, 2, 1, 3)
        .reshape(experts * slot_count, feat_width)
    )
    picked = expert_out[slot_index].reshape(row_count, top_count, feat_width)
    combined = jnp.einsum("tk,tkd->td", route_gates, picked.astype(jnp.float32))
    return (residual + combined).astype(jnp.bfloat16)


def local(
    hidden_in,
    queries,
    token_keys,
    token_values,
    stored_keys,
    stored_values,
    cache_len,
    query_gain,
    k_gain,
    norm_gain,
    expert_ids,
    gate_weights,
    w_gate,
    w_up,
    w_down,
):
    tokens_here = hidden_in.shape[0]
    cache_rows = stored_keys.shape[0]
    head_dim = query_gain.shape[0]
    heads_kv = token_keys.shape[1] // head_dim
    joined_keys = jnp.concatenate([stored_keys, token_keys], axis=0).reshape(
        cache_rows + tokens_here, heads_kv, head_dim
    )
    key_normed = normalized_rows(joined_keys.astype(jnp.float32), k_gain).astype(jnp.bfloat16)
    joined_values = jnp.concatenate([stored_values, token_values], axis=0).reshape(
        cache_rows + tokens_here, heads_kv, head_dim
    )
    length = cache_len[0]
    attended = attend_rows(queries, key_normed, joined_values, length, query_gain, cache_rows)
    residual = hidden_in.astype(jnp.float32) + attended.astype(jnp.float32)
    normed_rows = normalized_rows(residual, norm_gain).astype(jnp.bfloat16)
    return expert_block(normed_rows, expert_ids, gate_weights, residual, w_gate, w_up, w_down)


def solution(mesh):
    in_specs = (
        P(("grp", "ep"), None),
        P(("grp", "ep"), None),
        P(("grp", "ep"), None),
        P(("grp", "ep"), None),
        P(("grp", "ep"), None),
        P(("grp", "ep"), None),
        P(("grp", "ep")),
        P(),
        P(),
        P(),
        P(("grp", "ep"), None),
        P(("grp", "ep"), None),
        P(None, "ep"),
        P(None, "ep"),
        P("ep", None),
    )
    out_specs = P(("grp", "ep"), None)
    return jax.shard_map(local, mesh=mesh, in_specs=in_specs, out_specs=out_specs, check_vma=False)
```

profile of v0, /device:TPU:13, one launch (start us, length us, event | category | flops | bytes accessed | tf_op | source)
XLA Modules:
  0.0 244.7 jit_solution(9803694010693856453)
XLA Ops:
  0.0 0.9 copy.51
  2.3 2.2 maximum_convert_fusion
  4.5 2.7 %reshape.161 = f32[1088,2,128]{2,1,0:T(2,128)} reshape(f32[1088,256]{1,0:T(8,128)} %maximum_convert_fusion) | data formatting | bytes 2228224 | tf_op jit(solution)/shard_map/convert_element_type | solution.py:131
  7.2 3.0 %multiply_reduce_fusion = f32[1088,2]{1,0:T(8,128)S(1)} fusion(f32[1088,2,128]{2,1,0:T(2,128)} %reshape.161), kind=kLoop, calls=%fused_computation.18 | loop fusion | flops 554880 | bytes 1122816 | tf_op jit(solution)/shard_map/reduce_sum | solution.py:18
  10.3 0.9 add_rsqrt_fusion
  11.5 1.0 copy-done.5
  13.1 1.9 pad_maximum_fusion
  15.0 2.1 copy.40
  17.1 3.4 %fusion.20 = bf16[1088,2,128,1]{2,1,0,3:T(2,128)(2,1)S(1)} fusion(f32[1088,2,128]{2,1,0:T(2,128)} %reshape.161, f32[128]{0:T(128)S(1)} %copy-done.11, f32[1088,2]{1,0:T(8,128)} %add_rsqrt_fusion), kind=kLoop, calls=%fused_computation.32 | loop fusion | flops 835584 | bytes 1680384 | tf_op jit(solution)/shard_map/convert_element_type | solution.py:131
  20.6 4.2 %fusion = (f32[2,64,16]{2,1,0:T(8,128)S(1)}, f32[2,64,16,1088]{3,2,1,0:T(8,128)S(1)}) fusion(pred[64,1088]{1,0:T(8,128)(4,1)S(1)} %fusion.25, bf16[1088,2,128,1]{2,1,0,3:T(2,128)(2,1)S(1)} %fusion.20, f32[64,2,16,128]{3,2,1,0:T(8,128)} %bitcast.62, f32[128]{0:T(128)S(1)} %copy-done.12, f32[64,2,16]{2,1,0:T(2,128)S(1)} %copy.42), kind=kOutput, calls=%fused_computation.5 | convolution fusion | flops 577894400 | bytes 10605056 | tf_op jit(solution)/shard_map/tkgd,skd->ktgs/dot_general | solution.py:30
  24.8 2.6 %divide_convert_fusion = bf16[2,64,16,1088]{3,2,1,0:T(8,128)(2,1)S(1)} fusion(f32[2,64,16,1088]{3,2,1,0:T(8,128)S(1)} %get-tuple-element.6, f32[2,64,16]{2,1,0:T(8,128)S(1)} %get-tuple-element.5, pred[64,1088]{1,0:T(8,128)(4,1)S(1)} %fusion.25), kind=kLoop, calls=%fused_computation.3 | loop fusion | flops 8912896 | bytes 13447168 | tf_op jit(solution)/shard_map/convert_element_type | solution.py:41
  27.5 1.4 fusion.9
  29.5 1.1 copy-done.1
  32.3 1.2 scatter_custom_fusion
  33.5 2.0 multiply_convert_fusion.1
  36.3 6.3 %gather_fusion = bf16[256,4096]{1,0:T(8,128)(2,1)} fusion(bf16[65,4096]{1,0:T(8,128)(2,1)} %concatenate.11, s32[1024]{0:T(1024)S(1)} %pad_clamp_fusion.1), kind=kCustom, calls=%fused_computation | custom fusion | bytes 4195328 | tf_op jit(solution)/shard_map/gather | solution.py:74
  42.7 4.0 %broadcast_in_dim.64 = bf16[8,2,32,4096]{3,2,1,0:T(8,128)(2,1)} broadcast(bf16[8,32,4096]{2,1,0:T(8,128)(2,1)} %bitcast.58), dimensions={0,2,3} | broadcast | bytes 6291456 | tf_op jit(solution)/shard_map/broadcast_in_dim | solution.py:76
  46.7 6.6 %all-to-all-start = ((bf16[16,32,4096]{2,1,0:T(8,128)(2,1)}), bf16[16,32,4096]{2,1,0:T(8,128)(2,1)}, u32[]{:S(2)}, u32[]{:S(2)}) async-start(bf16[16,32,4096]{2,1,0:T(8,128)(2,1)} %bitcast.57), calls=%async_computation | async-start | bytes 8388608 | tf_op jit(solution)/shard_map/all_to_all | solution.py:79
  53.3 92.5 %all-to-all-done = bf16[16,32,4096]{2,1,0:T(8,128)(2,1)} async-done(((bf16[16,32,4096]{2,1,0:T(8,128)(2,1)}), bf16[16,32,4096]{2,1,0:T(8,128)(2,1)}, u32[]{:S(2)}, u32[]{:S(2)}) %all-to-all-start) | async-done | bytes 4194336 | tf_op jit(solution)/shard_map/all_to_all | solution.py:79
  145.7 6.4 %fusion.31 = f32[512,384]{1,0:T(8,128)} fusion(bf16[512,4096]{1,0:T(8,128)(2,1)} %bitcast.9, bf16[4096,384]{1,0:T(8,128)(2,1)} %param.27), kind=kOutput, calls=%fused_computation.64 | convolution fusion | flops 1610612736 | bytes 8126464 | tf_op jit(solution)/shard_map/dot_general | solution.py:49
  152.1 9.8 %fusion.13 = bf16[512,4096]{1,0:T(8,128)(2,1)} fusion(bf16[384,4096]{1,0:T(8,128)(2,1)S(1)} %copy-done, bf16[512,4096]{1,0:T(8,128)(2,1)} %bitcast.9, bf16[4096,384]{1,0:T(8,128)(2,1)} %param.28, f32[512,384]{1,0:T(8,128)} %fusion.31), kind=kOutput, calls=%fused_computation.16 | convolution fusion | flops 3222405120 | bytes 15466496 | tf_op jit(solution)/shard_map/dot_general | solution.py:52
  161.9 3.2 %dynamic-slice_convert_fusion = bf16[512,2048]{1,0:T(8,128)(2,1)} fusion(bf16[512,4096]{1,0:T(8,128)(2,1)} %fusion.13, s32[]{:T(128)S(6)} %select_n.51), kind=kLoop, calls=%fused_computation.9 | loop fusion | bytes 4194308 | tf_op jit(solution)/shard_map/convert_element_type | solution.py:87
  165.3 4.3 %collective-permute-done = bf16[512,2048]{1,0:T(8,128)(2,1)} collective-permute-done((bf16[512,2048]{1,0:T(8,128)(2,1)}, bf16[512,2048]{1,0:T(8,128)(2,1)}, u32[]{:S(2)}, u32[]{:S(2)}) %collective-permute-start) | collective-permute-done | bytes 2097184 | tf_op jit(solution)/shard_map/ppermute | solution.py:12
  169.6 4.5 %add_convert_fusion = bf16[512,2048]{1,0:T(8,128)(2,1)} fusion(bf16[512,2048]{1,0:T(8,128)(2,1)} %collective-permute-done, bf16[512,4096]{1,0:T(8,128)(2,1)} %fusion.13, s32[]{:T(128)S(6)} %select_n.50), kind=kLoop, calls=%fused_computation.8 | loop fusion | flops 4194304 | bytes 6291460 | tf_op jit(solution)/shard_map/convert_element_type | solution.py:89
  174.0 5.0 %all-to-all-start.1 = ((bf16[16,32,2048]{2,1,0:T(8,128)(2,1)}), bf16[16,32,2048]{2,1,0:T(8,128)(2,1)}, u32[]{:S(2)}, u32[]{:S(2)}) async-start(bf16[16,32,2048]{2,1,0:T(8,128)(2,1)} %bitcast.59), calls=%async_computation.1 | async-start | bytes 4194304 | tf_op jit(solution)/shard_map/all_to_all | solution.py:90
  179.2 47.4 %all-to-all-done.1 = bf16[16,32,2048]{2,1,0:T(8,128)(2,1)} async-done(((bf16[16,32,2048]{2,1,0:T(8,128)(2,1)}), bf16[16,32,2048]{2,1,0:T(8,128)(2,1)}, u32[]{:S(2)}, u32[]{:S(2)}) %all-to-all-start.1) | async-done | bytes 2097184 | tf_op jit(solution)/shard_map/all_to_all | solution.py:90
  226.6 3.8 %copy.52 = bf16[8,2,32,2048]{3,1,2,0:T(2,128)(2,1)S(1)} copy(bf16[8,2,32,2048]{3,2,1,0:T(8,128)(2,1)} %bitcast.11) | data formatting | bytes 4194304 | tf_op jit(solution)/shard_map/reshape | solution.py:98
  230.4 2.2 copy.63
  232.6 5.1 %gather_fusion.1 = bf16[128,4096]{1,0:T(8,128)(2,1)} fusion(bf16[256,4096]{1,0:T(8,128)(2,1)} %bitcast.53, s32[1024]{0:T(1024)S(1)} %pad_clamp_fusion), kind=kCustom, calls=%fused_computation.1 | custom fusion | bytes 2097664 | tf_op jit(solution)/shard_map/gather | solution.py:102
  237.7 2.5 %reshape.159 = bf16[64,2,4096]{2,1,0:T(2,128)(2,1)} reshape(bf16[128,4096]{1,0:T(8,128)(2,1)} %gather_fusion.1) | data formatting | bytes 2097152 | tf_op jit(solution)/shard_map/reshape | solution.py:102
  240.2 2.6 %fusion.32 = f32[64,1,4096]{2,1,0:T(1,128)S(1)} fusion(bf16[64,2,4096]{2,1,0:T(2,128)(2,1)} %reshape.159, bf16[64,2,1]{1,2,0:T(2,128)(2,1)S(1)} %copy.55), kind=kOutput, calls=%fused_computation.65 | convolution fusion | flops 1048576 | bytes 2097408 | tf_op jit(solution)/shard_map/tk,tkd->td/dot_general | solution.py:103
  242.8 1.9 fusion.14
  (51 shorter events, 5.2 us)
Async XLA Ops:
  0.0 152.1 %copy-start = (bf16[384,4096]{1,0:T(8,128)(2,1)S(1)}, bf16[384,4096]{1,0:T(8,128)(2,1)}, u32[]{:S(2)}) copy-start(bf16[384,4096]{1,0:T(8,128)(2,1)} %param.29) | copy-start | bytes 9437188
  7.2 3.9 %copy-start.7 = (bf16[64,4096]{1,0:T(8,128)(2,1)S(1)}, bf16[64,4096]{1,0:T(8,128)(2,1)}, u32[]{:S(2)}) copy-start(bf16[64,4096]{1,0:T(8,128)(2,1)} %param.16) | copy-start | bytes 1572868
  10.3 2.8 %copy-start.8 = (bf16[64,256]{1,0:T(8,128)(2,1)S(1)}, bf16[64,256]{1,0:T(8,128)(2,1)}, u32[]{:S(2)}) copy-start(bf16[64,256]{1,0:T(8,128)(2,1)} %param.18) | copy-start | bytes 98308
  11.2 5.9 %copy-start.11 = (f32[128]{0:T(128)S(1)}, f32[128]{0:T(128)}, u32[]{:S(2)}) copy-start(f32[128]{0:T(128)} %param.23) | copy-start | bytes 1540
  11.4 1.0 copy-start.5
  11.4 9.2 %copy-start.12 = (f32[128]{0:T(128)S(1)}, f32[128]{0:T(128)}, u32[]{:S(2)}) copy-start(f32[128]{0:T(128)} %param.22) | copy-start | bytes 1540
  24.8 2.6 %copy-start.6 = (bf16[1088,256]{0,1:T(8,128)(2,1)S(1)}, bf16[1088,256]{0,1:T(8,128)(2,1)}, u32[]{:S(2)}) copy-start(bf16[1088,256]{0,1:T(8,128)(2,1)} %copy.40) | copy-start | bytes 1671172
  27.5 3.1 %copy-start.3 = (bf16[64,4096]{1,0:T(8,128)(2,1)S(1)}, bf16[64,4096]{1,0:T(8,128)(2,1)}, u32[]{:S(2)}) copy-start(bf16[64,4096]{1,0:T(8,128)(2,1)} %param.15) | copy-start | bytes 1572868
  28.9 4.6 %copy-start.9 = (f32[4096]{0:T(1024)S(1)}, f32[4096]{0:T(1024)}, u32[]{:S(2)}) copy-start(f32[4096]{0:T(1024)} %param.24) | copy-start | bytes 49156
  29.5 1.1 copy-start.1
  46.7 99.0 %all-to-all-start = ((bf16[16,32,4096]{2,1,0:T(8,128)(2,1)}), bf16[16,32,4096]{2,1,0:T(8,128)(2,1)}, u32[]{:S(2)}, u32[]{:S(2)}) async-start(bf16[16,32,4096]{2,1,0:T(8,128)(2,1)} %bitcast.57), calls=%async_computation | async-start | bytes 8388608 | tf_op jit(solution)/shard_map/all_to_all | solution.py:79
  165.1 4.5 %collective-permute-start = (bf16[512,2048]{1,0:T(8,128)(2,1)}, bf16[512,2048]{1,0:T(8,128)(2,1)}, u32[]{:S(2)}, u32[]{:S(2)}) collective-permute-start(bf16[512,2048]{1,0:T(8,128)(2,1)} %dynamic-slice_convert_fusion), channel_id=1, source_target_pairs={{0,1},{1,0},{2,3},{3,2},{4,5},{5,4},{6,7},{7,6},{8,9},{9,8},{10,11... | collective-permute-start | bytes 6291464 | tf_op jit(solution)/shard_map/ppermute | solution.py:12
  174.0 5.0 %copy-start.10 = (f32[64,2]{0,1:T(2,128)S(1)}, f32[64,2]{0,1:T(2,128)}, u32[]{:S(2)}) copy-start(f32[64,2]{0,1:T(2,128)} %param.26) | copy-start | bytes 1540
  174.0 52.6 %all-to-all-start.1 = ((bf16[16,32,2048]{2,1,0:T(8,128)(2,1)}), bf16[16,32,2048]{2,1,0:T(8,128)(2,1)}, u32[]{:S(2)}, u32[]{:S(2)}) async-start(bf16[16,32,2048]{2,1,0:T(8,128)(2,1)} %bitcast.59), calls=%async_computation.1 | async-start | bytes 4194304 | tf_op jit(solution)/shard_map/all_to_all | solution.py:90
  240.2 2.6 %copy-start.2 = (f32[64,2,16,128]{3,2,1,0:T(8,128)S(1)}, f32[64,2,16,128]{3,2,1,0:T(8,128)}, u32[]{:S(2)}) copy-start(f32[64,2,16,128]{3,2,1,0:T(8,128)} %copy-done.1) | copy-start | bytes 3145732
  240.2 2.6 %copy-start.4 = (bf16[64,4096]{1,0:T(8,128)(2,1)S(1)}, bf16[64,4096]{1,0:T(8,128)(2,1)}, u32[]{:S(2)}) copy-start(bf16[64,4096]{1,0:T(8,128)(2,1)} %param.15) | copy-start | bytes 1572868
where the time goes:
time: 245 us
  waiting for transfers between devices  144 us (59%)
  local copies, waits for them, and re-layouts  38.5 us (16%)
  other arithmetic  25 us (10%)
  matrix products  24.3 us (10%)
  starting transfers between devices  11.8 us (5%)
    all_to_all x1, waiting for transfers between devices, expert_block(): lax.all_to_all(sendbuf, 'ep', split_axis=0, concat_axis=0, tiled=True)  92.5 us
    all_to_all x1, waiting for transfers between devices, expert_block(): lax.all_to_all(half_out.reshape(ep_size, slot_count, half_width), 'ep', s...  47.4 us
    dot_general x1, matrix products, expert_apply(): return jnp.dot(inner, w_down, preferred_element_type=jnp.float32)  9.75 us
    all_to_all x1, starting transfers between devices, expert_block(): lax.all_to_all(sendbuf, 'ep', split_axis=0, concat_axis=0, tiled=True)  6.56 us
    dot_general x1, matrix products, expert_apply(): gate_pre = jnp.dot(rows_in, w_gate, preferred_element_type=jnp.float32)  6.39 us
    gather x1, local copies, waits for them, and re-layouts, expert_block(): outgoing = padded_rows[source_row].reshape(experts, slot_count, feat_width)  6.35 us
    unnamed x30, local copies, waits for them, and re-layouts  5.56 us
    gather x1, local copies, waits for them, and re-layouts, expert_block(): picked = expert_out[slot_index].reshape(row_count, top_count, feat_width)  5.06 us
  transfers between devices with their start and end apart: 3, of which 3 were waited for; matrix products, arithmetic and copies ran while one was open for 0% of the time, Pallas kernels for 0%

commit v1 on v0

v1 whole, which is shorter than its diff:
```python
import math

import jax
import jax.numpy as jnp
from jax import lax
from jax.experimental import pallas as pl
from jax.experimental.pallas import tpu as pltpu
from jax.sharding import PartitionSpec as P

EPS = 1e-06
MIB = 1 << 20
VMEM = pltpu.VMEM
SMEM = pltpu.SMEM


def exchange(value, distance):
    return lax.ppermute(value, "ep", [(i, i ^ distance) for i in range(lax.axis_size("ep"))])


def whole(array):
    return pl.BlockSpec(array.shape, lambda: (0,) * array.ndim, memory_space=VMEM)


def params(mib):
    return pltpu.CompilerParams(vmem_limit_bytes=mib * MIB)


def cost(flops, moved):
    return pl.CostEstimate(flops=int(flops), bytes_accessed=int(moved), transcendentals=0)


def slots_of(chip, half, cap):
    lane = lax.broadcasted_iota(jnp.int32, (1, half * cap), 1)
    apart = lane // cap
    position = chip & (half - 1)
    expert = (chip - position) + (apart ^ position)
    return expert.astype(jnp.float32), (lane - apart * cap).astype(jnp.float32)


def slot_hits(info, expert, slot):
    rows, width = info.shape
    top = width // 2
    named = info[:, 0:1] == expert
    for k in range(1, top):
        named = jnp.logical_or(named, info[:, k : k + 1] == expert)
    row = lax.broadcasted_iota(jnp.int32, (rows, rows), 0)
    col = lax.broadcasted_iota(jnp.int32, (rows, rows), 1)
    earlier = jnp.where(col < row, 1.0, 0.0).astype(jnp.bfloat16)
    ones = jnp.where(named, 1.0, 0.0)
    rank = jnp.dot(earlier, ones.astype(jnp.bfloat16), preferred_element_type=jnp.float32)
    return jnp.where(rank == slot, ones, 0.0)


def spread_rows(chip, info, rows_bf16, out_refs, cap):
    half = len(out_refs)
    expert, slot = slots_of(chip, half, cap)
    hits = slot_hits(info, expert, slot).astype(jnp.bfloat16)
    for d in range(half):
        out_refs[d][...] = lax.dot_general(
            hits[:, d * cap : (d + 1) * cap],
            rows_bf16,
            (((0,), (0,)), ((), ())),
            preferred_element_type=jnp.float32,
        ).astype(jnp.bfloat16)


def weighted_rows(chip, info, in_refs, joined, cap):
    half = len(in_refs)
    top = info.shape[1] // 2
    expert, slot = slots_of(chip, half, cap)
    hits = slot_hits(info, expert, slot)
    weight = jnp.zeros_like(hits)
    for k in range(top):
        weight = weight + jnp.where(info[:, k : k + 1] == expert, info[:, top + k : top + k + 1], 0.0)
    weight = weight * hits
    high = weight.astype(jnp.bfloat16)
    low = (weight - high.astype(jnp.float32)).astype(jnp.bfloat16)
    for d in range(half):
        joined[d * cap : (d + 1) * cap, :] = in_refs[d][...]
    values = joined[...]
    return jnp.dot(high, values, preferred_element_type=jnp.float32) + jnp.dot(
        low, values, preferred_element_type=jnp.float32
    )


def unit_rows(values, gain):
    return values * lax.rsqrt(jnp.mean(values * values, axis=-1, keepdims=True) + EPS) * gain


def attend_kernel(cap, first_token, *refs):
    (meta, q_ref, hid_ref, sk_ref, tk_ref, sv_ref, tv_ref, qg_ref, kg_ref, ng_ref, info_ref) = refs[:11]
    (resid_ref, normed_ref, *out_refs) = refs[11:-3]
    kn_ref, vx_ref, qs_ref = refs[-3:]
    rows, width = resid_ref.shape
    mine = slice(first_token, first_token + rows)
    cache_rows = sk_ref.shape[0]
    token_rows = tk_ref.shape[0]
    head = qg_ref.shape[1]
    heads_kv = sk_ref.shape[1] // head
    heads = width // head
    group = heads // heads_kv
    length = meta[0]
    chip = meta[1]
    keys = cache_rows + token_rows
    q_gain = qg_ref[...] * (math.log2(math.e) / math.sqrt(head))
    k_gain = kg_ref[...]
    live = lax.broadcasted_iota(jnp.int32, (cache_rows, head), 0) < length
    live_ones = jnp.where(live, 1.0, 0.0).astype(jnp.bfloat16)
    for g in range(heads_kv):
        cols = slice(g * head, (g + 1) * head)
        kn_ref[g, :cache_rows, :] = unit_rows(sk_ref[:, cols].astype(jnp.float32), k_gain).astype(jnp.bfloat16)
        kn_ref[g, cache_rows:, :] = unit_rows(tk_ref[:, cols].astype(jnp.float32), k_gain).astype(jnp.bfloat16)
        vx_ref[g, :cache_rows, :head] = jnp.where(live, sv_ref[:, cols].astype(jnp.float32), 0.0).astype(jnp.bfloat16)
        vx_ref[g, :cache_rows, head:] = live_ones
        vx_ref[g, cache_rows:, :head] = tv_ref[:, cols]
        vx_ref[g, cache_rows:, head:] = jnp.ones((token_rows, head), jnp.bfloat16)
    for h in range(heads):
        x = q_ref[mine, h * head : (h + 1) * head].astype(jnp.float32)
        qs_ref[h * rows : (h + 1) * rows, :] = unit_rows(x, q_gain).astype(jnp.bfloat16)
    per = max(1, min(group, 256 // rows))
    block = per * rows
    own = lax.broadcasted_iota(jnp.int32, (block, token_rows), 0) % rows + first_token
    spot = lax.broadcasted_iota(jnp.int32, (block, token_rows), 1)
    causal = spot <= own
    square = jnp.zeros((rows, head), jnp.float32)
    for b in range(heads // per):
        g = b * per // group
        q_block = qs_ref[b * block : (b + 1) * block, :]
        scores = lax.dot_general(
            q_block, kn_ref[g, :cache_rows, :], (((1,), (1,)), ((), ())), preferred_element_type=jnp.float32
        )
        raised = jnp.exp2(scores).astype(jnp.bfloat16)
        scores_new = lax.dot_general(
            q_block, kn_ref[g, cache_rows:, :], (((1,), (1,)), ((), ())), preferred_element_type=jnp.float32
        )
        raised_new = jnp.where(causal, jnp.exp2(scores_new), 0.0).astype(jnp.bfloat16)
        summed = jnp.dot(raised, vx_ref[g, :cache_rows, :], preferred_element_type=jnp.float32) + jnp.dot(
            raised_new, vx_ref[g, cache_rows:, :], preferred_element_type=jnp.float32
        )
        attended = (summed[:, :head] / summed[:, head:]).astype(jnp.bfloat16).astype(jnp.float32)
        for i in range(per):
            cols = slice((b * per + i) * head, (b * per + i + 1) * head)
            resid = hid_ref[mine, cols].astype(jnp.float32) + attended[i * rows : (i + 1) * rows, :]
            resid_ref[:, cols] = resid
            square = square + resid * resid
    scale = lax.rsqrt(jnp.sum(square, axis=-1, keepdims=True) / width + EPS)
    normed = (resid_ref[...] * scale * ng_ref[...]).astype(jnp.bfloat16)
    normed_ref[...] = normed
    spread_rows(chip, info_ref[mine, :], normed, out_refs, cap)


def attend(meta, arrays, gains, info, chunk, chunks, half, cap):
    hidden_in, queries, token_keys, token_values, stored_keys, stored_values = arrays
    query_gain, k_gain, norm_gain = gains
    rows, width = hidden_in.shape[0] // chunks, hidden_in.shape[1]
    cache_rows, kv_width = stored_keys.shape
    token_rows = token_keys.shape[0]
    head = query_gain.shape[1]
    heads_kv = kv_width // head
    keys = cache_rows + token_rows
    out_shape = [
        jax.ShapeDtypeStruct((rows, width), jnp.float32),
        jax.ShapeDtypeStruct((rows, width), jnp.bfloat16),
    ] + [jax.ShapeDtypeStruct((cap, width), jnp.bfloat16)] * half

    def body(*refs):
        attend_kernel(cap, chunk * rows, *refs)

    results = pl.pallas_call(
        body,
        out_shape=out_shape,
        in_specs=[
            pl.BlockSpec(memory_space=SMEM),
            whole(queries),
            whole(hidden_in),
            whole(stored_keys),
            whole(token_keys),
            whole(stored_values),
            whole(token_values),
            whole(query_gain),
            whole(k_gain),
            whole(norm_gain),
            whole(info),
        ],
        out_specs=[pl.BlockSpec(o.shape, lambda: (0, 0), memory_space=VMEM) for o in out_shape],
        scratch_shapes=[
            VMEM((heads_kv, keys, head), jnp.bfloat16),
            VMEM((heads_kv, keys, 2 * head), jnp.bfloat16),
            VMEM((rows * width // head, head), jnp.bfloat16),
        ],
        compiler_params=params(32),
        cost_estimate=cost(4 * rows * width * keys, 6 * MIB),
        name="attend",
    )(meta, queries, hidden_in, stored_keys, token_keys, stored_values, token_values, query_gain, k_gain, norm_gain, info)
    return results[0], results[1], list(results[2:])


def relay(meta, rows_in, info, chunk, half, cap):
    rows, width = rows_in.shape
    out = jax.ShapeDtypeStruct((cap, width), jnp.bfloat16)

    def body(meta_ref, rows_ref, info_ref, *out_refs):
        spread_rows(meta_ref[1], info_ref[chunk * rows : (chunk + 1) * rows, :], rows_ref[...], out_refs, cap)

    return list(
        pl.pallas_call(
            body,
            out_shape=[out] * half,
            in_specs=[pl.BlockSpec(memory_space=SMEM), whole(rows_in), whole(info)],
            out_specs=[whole(out)] * half,
            compiler_params=params(32),
            cost_estimate=cost(2 * half * cap * rows * width, MIB),
            name="relay",
        )(meta, rows_in, info)
    )


def expert(own, other, w_gate, w_up, w_down):
    cap, width = own[0].shape
    count = len(own)
    hidden = w_gate.shape[1]
    total = 2 * count * cap
    block = min(total, 256)
    steps = 4
    k_part = width // steps
    out = jax.ShapeDtypeStruct((count * cap, width), jnp.bfloat16)

    def body(*refs):
        ins = refs[: 2 * count]
        wg_hbm, wu_hbm, wd_hbm = refs[2 * count : 2 * count + 3]
        out_own, out_other = refs[2 * count + 3 : 2 * count + 5]
        x_ref, y_ref, wgu, wd, sems = refs[2 * count + 5 :]
        up_copies, down_copies = [], []
        for s in range(steps):
            part = pl.ds(s * k_part, k_part)
            up_copies.append(
                (
                    pltpu.make_async_copy(wg_hbm.at[part, :], wgu.at[part, pl.ds(0, hidden)], sems.at[0, s]),
                    pltpu.make_async_copy(wu_hbm.at[part, :], wgu.at[part, pl.ds(hidden, hidden)], sems.at[1, s]),
                )
            )
            down_copies.append(pltpu.make_async_copy(wd_hbm.at[:, part], wd.at[:, part], sems.at[2, s]))
        for pair in up_copies:
            for copy in pair:
                copy.start()
        for copy in down_copies:
            copy.start()
        for i in range(2 * count):
            x_ref[i * cap : (i + 1) * cap, :] = ins[i][...]

        def rows_of(r, waiting):
            span = pl.ds(r * block, block) if isinstance(r, int) else pl.ds(pl.multiple_of(r * block, block), block)
            pre = jnp.zeros((block, 2 * hidden), jnp.float32)
            for s in range(steps):
                if waiting:
                    for copy in up_copies[s]:
                        copy.wait()
                pre = pre + jnp.dot(
                    x_ref[span, s * k_part : (s + 1) * k_part],
                    wgu[s * k_part : (s + 1) * k_part, :],
                    preferred_element_type=jnp.float32,
                )
            gate = pre[:, :hidden]
            inner = (gate / (1.0 + jnp.exp(-gate)) * pre[:, hidden:]).astype(jnp.bfloat16)
            for s in range(steps):
                if waiting:
                    down_copies[s].wait()
                y_ref[span, s * k_part : (s + 1) * k_part] = jnp.dot(
                    inner, wd[:, s * k_part : (s + 1) * k_part], preferred_element_type=jnp.float32
                ).astype(jnp.bfloat16)

        rows_of(0, True)
        if total > block:

            @pl.loop(1, total // block)
            def _(r):
                rows_of(r, False)

        out_own[...] = y_ref[: count * cap, :]
        out_other[...] = y_ref[count * cap :, :]

    return pl.pallas_call(
        body,
        out_shape=[out, out],
        in_specs=[whole(own[0])] * (2 * count) + [pl.BlockSpec(memory_space=pl.ANY)] * 3,
        out_specs=[whole(out)] * 2,
        scratch_shapes=[
            VMEM((total, width), jnp.bfloat16),
            VMEM((total, width), jnp.bfloat16),
            VMEM((width, 2 * hidden), jnp.bfloat16),
            VMEM((hidden, width), jnp.bfloat16),
            pltpu.SemaphoreType.DMA((3, steps)),
        ],
        compiler_params=params(52),
        cost_estimate=cost(6 * total * width * hidden, 6 * width * hidden),
        name="expert",
    )(*own, *other, w_gate, w_up, w_down)


def add_halves(mine, theirs, cap):
    rows, width = mine.shape
    count = rows // cap
    out = jax.ShapeDtypeStruct((cap, width), jnp.bfloat16)

    def body(a_ref, b_ref, *out_refs):
        for i in range(count):
            span = slice(i * cap, (i + 1) * cap)
            out_refs[i][...] = (a_ref[span, :].astype(jnp.float32) + b_ref[span, :].astype(jnp.float32)).astype(
                jnp.bfloat16
            )

    return list(
        pl.pallas_call(
            body,
            out_shape=[out] * count,
            in_specs=[whole(mine)] * 2,
            out_specs=[whole(out)] * count,
            compiler_params=params(32),
            cost_estimate=cost(rows * width, 6 * rows * width),
            name="add_halves",
        )(mine, theirs)
    )


def relay_back(meta, returned, info, chunk, rows, cap):
    half = len(returned)
    width = returned[0].shape[1]
    out = jax.ShapeDtypeStruct((rows, width), jnp.bfloat16)

    def body(meta_ref, info_ref, *refs):
        in_refs, out_ref, joined = refs[:half], refs[half], refs[half + 1]
        out_ref[...] = weighted_rows(meta_ref[1], info_ref[chunk * rows : (chunk + 1) * rows, :], in_refs, joined, cap).astype(jnp.bfloat16)

    return pl.pallas_call(
        body,
        out_shape=out,
        in_specs=[pl.BlockSpec(memory_space=SMEM), whole(info)]
        + [whole(returned[0])] * half,
        out_specs=whole(out),
        scratch_shapes=[VMEM((half * cap, width), jnp.bfloat16)],
        compiler_params=params(32),
        cost_estimate=cost(4 * half * cap * rows * width, MIB),
        name="relay_back",
    )(meta, info, *returned)


def finish(meta, resid, returned, far, info, chunk, chunks, cap, previous):
    half = len(returned)
    rows, width = resid.shape
    out = jax.ShapeDtypeStruct((rows * chunks, width), jnp.bfloat16)
    extra = [] if previous is None else [previous]

    def body(*refs):
        refs = refs[len(extra) :]
        meta_ref, info_ref, resid_ref, far_ref = refs[:4]
        in_refs, out_hbm, joined, out_ref, sem = refs[4 : 4 + half], *refs[4 + half :]
        near = weighted_rows(meta_ref[1], info_ref[chunk * rows : (chunk + 1) * rows, :], in_refs, joined, cap)
        out_ref[...] = (resid_ref[...] + (near + far_ref[...].astype(jnp.float32))).astype(jnp.bfloat16)
        copy = pltpu.make_async_copy(out_ref, out_hbm.at[pl.ds(chunk * rows, rows), :], sem)
        copy.start()
        copy.wait()

    return pl.pallas_call(
        body,
        out_shape=out,
        in_specs=[pl.BlockSpec(memory_space=pl.ANY)] * len(extra)
        + [
            pl.BlockSpec(memory_space=SMEM),
            whole(info),
            whole(resid),
            whole(far),
        ]
        + [whole(returned[0])] * half,
        out_specs=pl.BlockSpec(memory_space=pl.ANY),
        scratch_shapes=[
            VMEM((half * cap, width), jnp.bfloat16),
            VMEM((rows, width), jnp.bfloat16),
            pltpu.SemaphoreType.DMA,
        ],
        input_output_aliases={0: 0} if extra else {},
        compiler_params=params(32),
        cost_estimate=cost(4 * half * cap * rows * width, 2 * MIB),
        name="finish",
    )(*extra, meta, info, resid, far, *returned)


def local(
    hidden_in,
    queries,
    token_keys,
    token_values,
    stored_keys,
    stored_values,
    cache_len,
    query_gain,
    k_gain,
    norm_gain,
    expert_ids,
    gate_weights,
    w_gate,
    w_up,
    w_down,
):
    token_rows, top = expert_ids.shape
    ep = lax.axis_size("ep")
    experts = ep // 2
    half = experts // 2
    slots = 2 * token_rows * top // experts
    chunks = 2 if slots >= 32 else 1
    cap = slots // chunks
    rows = token_rows // chunks
    chip = lax.axis_index("ep") // 2
    meta = jnp.stack([cache_len[0], chip.astype(jnp.int32)])
    info = jnp.concatenate([expert_ids.astype(jnp.float32), gate_weights], axis=1)
    far_info = exchange(info, ep // 2)
    arrays = (hidden_in, queries, token_keys, token_values, stored_keys, stored_values)
    gains = (query_gain[None, :], k_gain[None, :], norm_gain[None, :])

    resid, far_rows, near_own = [], [], []
    for c in range(chunks):
        residual, normed, outgoing = attend(meta, arrays, gains, info, c, chunks, half, cap)
        resid.append(residual)
        far_rows.append(exchange(normed, ep // 2))
        near_own.append([outgoing[0]] + [exchange(outgoing[d], 2 * d) for d in range(1, half)])

    def run_experts(own):
        other = [exchange(x, 1) for x in own]
        mine, theirs = expert(own, other, w_gate, w_up, w_down)
        return add_halves(mine, exchange(theirs, 1), cap)

    def give_back(parts):
        return [parts[0]] + [exchange(parts[d], 2 * d) for d in range(1, half)]

    near_out = run_experts([x for own in near_own for x in own])
    near_back = [give_back(near_out[c * half : (c + 1) * half]) for c in range(chunks)]
    far_back = []
    for c in range(chunks):
        outgoing = relay(meta, far_rows[c], far_info, c, half, cap)
        own = [outgoing[0]] + [exchange(outgoing[d], 2 * d) for d in range(1, half)]
        returned = give_back(run_experts(own))
        far_back.append(exchange(relay_back(meta, returned, far_info, c, rows, cap), ep // 2))
    result = None
    for c in range(chunks):
        result = finish(meta, resid[c], near_back[c], far_back[c], info, c, chunks, cap, result)
    return result


def solution(mesh):
    in_specs = (
        P(("grp", "ep"), None),
        P(("grp", "ep"), None),
        P(("grp", "ep"), None),
        P(("grp", "ep"), None),
        P(("grp", "ep"), None),
        P(("grp", "ep"), None),
        P(("grp", "ep")),
        P(),
        P(),
        P(),
        P(("grp", "ep"), None),
        P(("grp", "ep"), None),
        P(None, "ep"),
        P(None, "ep"),
        P("ep", None),
    )
    out_specs = P(("grp", "ep"), None)
    return jax.shard_map(local, mesh=mesh, in_specs=in_specs, out_specs=out_specs, check_vma=False)
```

time: 245 us -> 130 us (0.53)
  the two profiles are of different devices: /device:TPU:13 before, /device:TPU:0 now
where the time goes in v1:
time: 130 us
  waiting for transfers between devices  45.3 us (35%)
  starting transfers between devices  39 us (30%)
  Pallas kernels  34.9 us (27%)
  local copies, waits for them, and re-layouts  7.81 us (6%)
  other arithmetic  1.44 us (1%)
    ppermute x48, waiting for transfers between devices, exchange(): lax.ppermute(value, 'ep', [(i, i ^ distance) for i in range(lax.axis_size...  45.3 us
    ppermute x48, starting transfers between devices, exchange(): lax.ppermute(value, 'ep', [(i, i ^ distance) for i in range(lax.axis_size...  39 us
    pallas_call x3, Pallas kernels, expert(): pl.pallas_call(body, out_shape=[out, out], in_specs=[whole(own[0])] * (2...  20.6 us
    unnamed x22, local copies, waits for them, and re-layouts  7.71 us
    pallas_call x2, Pallas kernels, attend(): pl.pallas_call(body, out_shape=out_shape, in_specs=[pl.BlockSpec(memory_s...  6.22 us
    pallas_call x2, Pallas kernels, finish(): pl.pallas_call(body, out_shape=out, in_specs=[pl.BlockSpec(memory_space=p...  3.46 us
  transfers between devices with their start and end apart: 48, of which 14 were waited for; matrix products, arithmetic and copies ran while one was open for 0% of the time, Pallas kernels for 26%

profile of v1, /device:TPU:0, one launch (start us, length us, event | category | flops | bytes accessed | tf_op | source)
XLA Modules:
  0.0 129.6 jit_solution(17645083195104179144)
XLA Ops:
  1.5 4.1 %collective-permute-start = (f32[64,4]{1,0:T(8,128)S(1)}, f32[64,4]{1,0:T(8,128)S(1)}, u32[]{:S(2)}, u32[]{:S(2)}) collective-permute-start(f32[64,4]{1,0:T(8,128)S(1)} %copy.22.refs_10_.refs_1_.refs_2_), channel_id=1, source_target_pairs={{0,8},{1,9},{2,10},{3,11},{4,12},{5,13},{6,14},{7,15},{8,0},{9,1},... | collective-permute-start | bytes 3080 | tf_op jit(solution)/shard_map/ppermute | solution.py:17
  14.0 3.1 %attend.3 = (f32[32,4096]{1,0:T(8,128)S(1)}, bf16[32,4096]{1,0:T(8,128)(2,1)S(1)}, bf16[16,4096]{1,0:T(8,128)(2,1)S(1)}, bf16[16,4096]{1,0:T(8,128)(2,1)S(1)}, b...) custom-call(s32[2]{0:T(128)S(1)} %pad_add_fusion.refs_0_.meta_ref.refs_1_, bf16[64,4096]{1,0:T(8,128)(2,1)S(1)} %copy-done, ...), custom_call_target="tpu_custom_call" | custom-call | flops 570425344 | bytes 6291456 | tf_op jit(solution)/shard_map/attend/pallas_call | solution.py:169
  17.1 1.6 %collective-permute-start.17 = (bf16[16,4096]{1,0:T(8,128)(2,1)S(1)}, bf16[16,4096]{1,0:T(8,128)(2,1)S(1)}, u32[]{:S(2)}, u32[]{:S(2)}) collective-permute-start(bf16[16,4096]{1,0:T(8,128)(2,1)S(1)} %get-tuple-element.64), channel_id=1, source_target_pairs={{0,2},{1,3},{2,0},{3,1},{4,6},{5,7},{6,4},{7,5},{8,10},{9,11},{10,... | collective-permute-start | bytes 393224 | tf_op jit(solution)/shard_map/ppermute | solution.py:17
  18.7 1.6 %collective-permute-start.18 = (bf16[16,4096]{1,0:T(8,128)(2,1)S(1)}, bf16[16,4096]{1,0:T(8,128)(2,1)S(1)}, u32[]{:S(2)}, u32[]{:S(2)}) collective-permute-start(bf16[16,4096]{1,0:T(8,128)(2,1)S(1)} %get-tuple-element.65), channel_id=1, source_target_pairs={{0,4},{1,5},{2,6},{3,7},{4,0},{5,1},{6,2},{7,3},{8,12},{9,13},{10,... | collective-permute-start | bytes 393224 | tf_op jit(solution)/shard_map/ppermute | solution.py:17
  20.6 3.1 %attend.2 = (f32[32,4096]{1,0:T(8,128)S(1)}, bf16[32,4096]{1,0:T(8,128)(2,1)S(1)}, bf16[16,4096]{1,0:T(8,128)(2,1)S(1)}, bf16[16,4096]{1,0:T(8,128)(2,1)S(1)}, b...) custom-call(s32[2]{0:T(128)S(1)} %pad_add_fusion.refs_0_.meta_ref.refs_1_, bf16[64,4096]{1,0:T(8,128)(2,1)S(1)} %copy-done, ...), custom_call_target="tpu_custom_call" | custom-call | flops 570425344 | bytes 6291456 | tf_op jit(solution)/shard_map/attend/pallas_call | solution.py:169
  23.8 1.6 %collective-permute-start.14 = (bf16[16,4096]{1,0:T(8,128)(2,1)S(1)}, bf16[16,4096]{1,0:T(8,128)(2,1)S(1)}, u32[]{:S(2)}, u32[]{:S(2)}) collective-permute-start(bf16[16,4096]{1,0:T(8,128)(2,1)S(1)} %get-tuple-element.60), channel_id=1, source_target_pairs={{0,2},{1,3},{2,0},{3,1},{4,6},{5,7},{6,4},{7,5},{8,10},{9,11},{10,... | collective-permute-start | bytes 393224 | tf_op jit(solution)/shard_map/ppermute | solution.py:17
  25.4 1.6 %collective-permute-start.15 = (bf16[16,4096]{1,0:T(8,128)(2,1)S(1)}, bf16[16,4096]{1,0:T(8,128)(2,1)S(1)}, u32[]{:S(2)}, u32[]{:S(2)}) collective-permute-start(bf16[16,4096]{1,0:T(8,128)(2,1)S(1)} %get-tuple-element.61), channel_id=1, source_target_pairs={{0,4},{1,5},{2,6},{3,7},{4,0},{5,1},{6,2},{7,3},{8,12},{9,13},{10,... | collective-permute-start | bytes 393224 | tf_op jit(solution)/shard_map/ppermute | solution.py:17
  30.3 1.9 %collective-permute-done.15.refs_2_ = bf16[16,4096]{1,0:T(8,128)(2,1)S(1)} collective-permute-done((bf16[16,4096]{1,0:T(8,128)(2,1)S(1)}, bf16[16,4096]{1,0:T(8,128)(2,1)S(1)}, u32[]{:S(2)}, u32[]{:S(2)}) %collective-permute-start.15) | collective-permute-done | bytes 131104 | tf_op jit(solution)/shard_map/ppermute | solution.py:17
  32.2 7.1 %collective-permute-done.16.refs_3_ = bf16[16,4096]{1,0:T(8,128)(2,1)S(1)} collective-permute-done((bf16[16,4096]{1,0:T(8,128)(2,1)S(1)}, bf16[16,4096]{1,0:T(8,128)(2,1)S(1)}, u32[]{:S(2)}, u32[]{:S(2)}) %collective-permute-start.16) | collective-permute-done | bytes 131104 | tf_op jit(solution)/shard_map/ppermute | solution.py:17
  39.8 7.9 %collective-permute-done.32.rows_ref = bf16[32,4096]{1,0:T(8,128)(2,1)S(1)} collective-permute-done((bf16[32,4096]{1,0:T(8,128)(2,1)S(1)}, bf16[32,4096]{1,0:T(8,128)(2,1)S(1)}, u32[]{:S(2)}, u32[]{:S(2)}) %collective-permute-start.32) | collective-permute-done | bytes 262176 | tf_op jit(solution)/shard_map/ppermute | solution.py:17
  49.8 3.0 %collective-permute-done.1.rows_ref = bf16[32,4096]{1,0:T(8,128)(2,1)S(1)} collective-permute-done((bf16[32,4096]{1,0:T(8,128)(2,1)S(1)}, bf16[32,4096]{1,0:T(8,128)(2,1)S(1)}, u32[]{:S(2)}, u32[]{:S(2)}) %collective-permute-start.1) | collective-permute-done | bytes 262176 | tf_op jit(solution)/shard_map/ppermute | solution.py:17
  53.9 2.0 %collective-permute-start.35 = (bf16[16,4096]{1,0:T(8,128)(2,1)S(1)}, bf16[16,4096]{1,0:T(8,128)(2,1)S(1)}, u32[]{:S(2)}, u32[]{:S(2)}) collective-permute-start(bf16[16,4096]{1,0:T(8,128)(2,1)S(1)} %get-tuple-element.78), channel_id=1, source_target_pairs={{0,6},{1,7},{2,4},{3,5},{4,2},{5,3},{6,0},{7,1},{8,14},{9,15},{10,... | collective-permute-start | bytes 393224 | tf_op jit(solution)/shard_map/ppermute | solution.py:17
  56.0 1.5 %collective-permute-start.2 = (bf16[16,4096]{1,0:T(8,128)(2,1)S(1)}, bf16[16,4096]{1,0:T(8,128)(2,1)S(1)}, u32[]{:S(2)}, u32[]{:S(2)}) collective-permute-start(bf16[16,4096]{1,0:T(8,128)(2,1)S(1)} %get-tuple-element.50), channel_id=1, source_target_pairs={{0,2},{1,3},{2,0},{3,1},{4,6},{5,7},{6,4},{7,5},{8,10},{9,11},{10,... | collective-permute-start | bytes 393224 | tf_op jit(solution)/shard_map/ppermute | solution.py:17
  57.5 2.0 %collective-permute-start.4 = (bf16[16,4096]{1,0:T(8,128)(2,1)S(1)}, bf16[16,4096]{1,0:T(8,128)(2,1)S(1)}, u32[]{:S(2)}, u32[]{:S(2)}) collective-permute-start(bf16[16,4096]{1,0:T(8,128)(2,1)S(1)} %get-tuple-element.52), channel_id=1, source_target_pairs={{0,6},{1,7},{2,4},{3,5},{4,2},{5,3},{6,0},{7,1},{8,14},{9,15},{10,... | collective-permute-start | bytes 393224 | tf_op jit(solution)/shard_map/ppermute | solution.py:17
  59.5 9.1 %expert.4 = (bf16[128,4096]{1,0:T(8,128)(2,1)}, bf16[128,4096]{1,0:T(8,128)(2,1)}) custom-call(bf16[16,4096]{1,0:T(8,128)(2,1)S(1)} %get-tuple-element.59.refs_0_, bf16[16,4096]{1,0:T(8,128)(2,1)S(1)} %collective-permute-done.14.refs_1_, bf16[16,4096]{1,0:T(8,128)(2,1)S(1)} %collective-permute-done.15.refs_2_, ...), custom_call_target="tpu_custom_call" | custom-call | flops 2415919104 | bytes 9437184 | tf_op jit(solution)/shard_map/expert/pallas_call | solution.py:282
  72.3 5.8 %expert.3 = (bf16[64,4096]{1,0:T(8,128)(2,1)S(1)}, bf16[64,4096]{1,0:T(8,128)(2,1)}) custom-call(bf16[16,4096]{1,0:T(8,128)(2,1)S(1)} %get-tuple-element.49.refs_0_, bf16[16,4096]{1,0:T(8,128)(2,1)S(1)} %collective-permute-done.2.refs_1_, bf16[16,4096]{1,0:T(8,128)(2,1)S(1)} %collective-permute-done.3.refs_2_, ...), custom_call_target="tpu_custom_call" | custom-call | flops 1207959552 | bytes 9437184 | tf_op jit(solution)/shard_map/expert/pallas_call | solution.py:282
  78.4 5.7 %expert.5 = (bf16[64,4096]{1,0:T(8,128)(2,1)S(1)}, bf16[64,4096]{1,0:T(8,128)(2,1)}) custom-call(bf16[16,4096]{1,0:T(8,128)(2,1)S(1)} %get-tuple-element.75.refs_0_, bf16[16,4096]{1,0:T(8,128)(2,1)S(1)} %collective-permute-done.33.refs_1_, bf16[16,4096]{1,0:T(8,128)(2,1)S(1)} %collective-permute-done.34.refs_2_, ...), custom_call_target="tpu_custom_call" | custom-call | flops 1207959552 | bytes 9437184 | tf_op jit(solution)/shard_map/expert/pallas_call | solution.py:282
  84.6 1.6 %collective-permute-start.10 = (bf16[16,4096]{1,0:T(8,128)(2,1)S(1)}, bf16[16,4096]{1,0:T(8,128)(2,1)S(1)}, u32[]{:S(2)}, u32[]{:S(2)}) collective-permute-start(bf16[16,4096]{1,0:T(8,128)(2,1)S(1)} %get-tuple-element.56), channel_id=1, source_target_pairs={{0,2},{1,3},{2,0},{3,1},{4,6},{5,7},{6,4},{7,5},{8,10},{9,11},{10,... | collective-permute-start | bytes 393224 | tf_op jit(solution)/shard_map/ppermute | solution.py:17
  86.3 1.9 %collective-permute-start.12 = (bf16[16,4096]{1,0:T(8,128)(2,1)S(1)}, bf16[16,4096]{1,0:T(8,128)(2,1)S(1)}, u32[]{:S(2)}, u32[]{:S(2)}) collective-permute-start(bf16[16,4096]{1,0:T(8,128)(2,1)S(1)} %get-tuple-element.58), channel_id=1, source_target_pairs={{0,6},{1,7},{2,4},{3,5},{4,2},{5,3},{6,0},{7,1},{8,14},{9,15},{10,... | collective-permute-start | bytes 393224 | tf_op jit(solution)/shard_map/ppermute | solution.py:17
  88.3 1.6 %collective-permute-start.41 = (bf16[16,4096]{1,0:T(8,128)(2,1)S(1)}, bf16[16,4096]{1,0:T(8,128)(2,1)S(1)}, u32[]{:S(2)}, u32[]{:S(2)}) collective-permute-start(bf16[16,4096]{1,0:T(8,128)(2,1)S(1)} %get-tuple-element.82), channel_id=1, source_target_pairs={{0,2},{1,3},{2,0},{3,1},{4,6},{5,7},{6,4},{7,5},{8,10},{9,11},{10,... | collective-permute-start | bytes 393224 | tf_op jit(solution)/shard_map/ppermute | solution.py:17
  90.4 2.1 %collective-permute-done.11.refs_2_ = bf16[16,4096]{1,0:T(8,128)(2,1)S(1)} collective-permute-done((bf16[16,4096]{1,0:T(8,128)(2,1)S(1)}, bf16[16,4096]{1,0:T(8,128)(2,1)S(1)}, u32[]{:S(2)}, u32[]{:S(2)}) %collective-permute-start.11) | collective-permute-done | bytes 131104 | tf_op jit(solution)/shard_map/ppermute | solution.py:17
  93.3 2.0 %collective-permute-done.12.refs_3_ = bf16[16,4096]{1,0:T(8,128)(2,1)S(1)} collective-permute-done((bf16[16,4096]{1,0:T(8,128)(2,1)S(1)}, bf16[16,4096]{1,0:T(8,128)(2,1)S(1)}, u32[]{:S(2)}, u32[]{:S(2)}) %collective-permute-start.12) | collective-permute-done | bytes 131104 | tf_op jit(solution)/shard_map/ppermute | solution.py:17
  96.4 2.0 %collective-permute-done.42.refs_2_ = bf16[16,4096]{1,0:T(8,128)(2,1)S(1)} collective-permute-done((bf16[16,4096]{1,0:T(8,128)(2,1)S(1)}, bf16[16,4096]{1,0:T(8,128)(2,1)S(1)}, u32[]{:S(2)}, u32[]{:S(2)}) %collective-permute-start.42) | collective-permute-done | bytes 131104 | tf_op jit(solution)/shard_map/ppermute | solution.py:17
  98.4 1.6 %collective-permute-done.43.refs_3_ = bf16[16,4096]{1,0:T(8,128)(2,1)S(1)} collective-permute-done((bf16[16,4096]{1,0:T(8,128)(2,1)S(1)}, bf16[16,4096]{1,0:T(8,128)(2,1)S(1)}, u32[]{:S(2)}, u32[]{:S(2)}) %collective-permute-start.43) | collective-permute-done | bytes 131104 | tf_op jit(solution)/shard_map/ppermute | solution.py:17
  101.3 2.6 %collective-permute-start.29 = (bf16[16,4096]{1,0:T(8,128)(2,1)S(1)}, bf16[16,4096]{1,0:T(8,128)(2,1)S(1)}, u32[]{:S(2)}, u32[]{:S(2)}) collective-permute-start(bf16[16,4096]{1,0:T(8,128)(2,1)S(1)} %get-tuple-element.70), channel_id=1, source_target_pairs={{0,2},{1,3},{2,0},{3,1},{4,6},{5,7},{6,4},{7,5},{8,10},{9,11},{10,... | collective-permute-start | bytes 393224 | tf_op jit(solution)/shard_map/ppermute | solution.py:17
  103.9 3.7 %collective-permute-start.30 = (bf16[16,4096]{1,0:T(8,128)(2,1)S(1)}, bf16[16,4096]{1,0:T(8,128)(2,1)S(1)}, u32[]{:S(2)}, u32[]{:S(2)}) collective-permute-start(bf16[16,4096]{1,0:T(8,128)(2,1)S(1)} %get-tuple-element.71), channel_id=1, source_target_pairs={{0,4},{1,5},{2,6},{3,7},{4,0},{5,1},{6,2},{7,3},{8,12},{9,13},{10,... | collective-permute-start | bytes 393224 | tf_op jit(solution)/shard_map/ppermute | solution.py:17
  107.6 8.4 %collective-permute-done.13.refs_3_ = bf16[32,4096]{1,0:T(8,128)(2,1)S(1)} collective-permute-done((bf16[32,4096]{1,0:T(8,128)(2,1)S(1)}, bf16[32,4096]{1,0:T(8,128)(2,1)S(1)}, u32[]{:S(2)}, u32[]{:S(2)}) %collective-permute-start.13) | collective-permute-done | bytes 262176 | tf_op jit(solution)/shard_map/ppermute | solution.py:17
  116.5 3.0 %collective-permute-start.47 = (bf16[16,4096]{1,0:T(8,128)(2,1)S(1)}, bf16[16,4096]{1,0:T(8,128)(2,1)S(1)}, u32[]{:S(2)}, u32[]{:S(2)}) collective-permute-start(bf16[16,4096]{1,0:T(8,128)(2,1)S(1)} %get-tuple-element.88), channel_id=1, source_target_pairs={{0,6},{1,7},{2,4},{3,5},{4,2},{5,3},{6,0},{7,1},{8,14},{9,15},{10,... | collective-permute-start | bytes 393224 | tf_op jit(solution)/shard_map/ppermute | solution.py:17
  119.6 3.0 %collective-permute-done.31.refs_7_ = bf16[16,4096]{1,0:T(8,128)(2,1)S(1)} collective-permute-done((bf16[16,4096]{1,0:T(8,128)(2,1)S(1)}, bf16[16,4096]{1,0:T(8,128)(2,1)S(1)}, u32[]{:S(2)}, u32[]{:S(2)}) %collective-permute-start.31) | collective-permute-done | bytes 131104 | tf_op jit(solution)/shard_map/ppermute | solution.py:17
  122.6 1.7 %finish.2.refs_0_ = bf16[64,4096]{1,0:T(8,128)(2,1)} custom-call(s32[2]{0:T(128)S(1)} %pad_add_fusion.refs_0_.meta_ref.refs_1_, f32[64,4]{1,0:T(8,128)S(1)} %copy.22.refs_10_.refs_1_.refs_2_, f32[32,4096]{1,0:T(8,128)S(1)} %get-tuple-element.47.refs_2_, bf16[32,4096]{1,0:T(8,128)(2,1)S(1)} %collective-permute-done.13.refs_3_, ...), custom_call_target="tpu_custom_call" | custom-call | flops 33554432 | bytes 2097152 | tf_op jit(solution)/shard_map/finish/pallas_call | solution.py:363
  124.4 3.3 %collective-permute-done.47.refs_8_ = bf16[16,4096]{1,0:T(8,128)(2,1)S(1)} collective-permute-done((bf16[16,4096]{1,0:T(8,128)(2,1)S(1)}, bf16[16,4096]{1,0:T(8,128)(2,1)S(1)}, u32[]{:S(2)}, u32[]{:S(2)}) %collective-permute-start.47) | collective-permute-done | bytes 131104 | tf_op jit(solution)/shard_map/ppermute | solution.py:17
  127.7 1.7 %finish.3 = bf16[64,4096]{1,0:T(8,128)(2,1)} custom-call(bf16[64,4096]{1,0:T(8,128)(2,1)} %finish.2.refs_0_, s32[2]{0:T(128)S(1)} %pad_add_fusion.refs_0_.meta_ref.refs_1_, f32[64,4]{1,0:T(8,128)S(1)} %copy.22.refs_10_.refs_1_.refs_2_, f32[32,4096]{1,0:T(8,128)S(1)} %get-tuple-element.73.refs_3_, ...), custom_call_target="tpu_custom_call", output_to_operand_aliasing={{}: (0, {})} | custom-call | flops 33554432 | bytes 2097152 | tf_op jit(solution)/shard_map/finish/pallas_call | solution.py:363
  (104 shorter events, 25.6 us)
Async XLA Ops:
  1.5 22.3 %collective-permute-start = (f32[64,4]{1,0:T(8,128)S(1)}, f32[64,4]{1,0:T(8,128)S(1)}, u32[]{:S(2)}, u32[]{:S(2)}) collective-permute-start(f32[64,4]{1,0:T(8,128)S(1)} %copy.22.refs_10_.refs_1_.refs_2_), channel_id=1, source_target_pairs={{0,8},{1,9},{2,10},{3,11},{4,12},{5,13},{6,14},{7,15},{8,0},{9,1},... | collective-permute-start | bytes 3080 | tf_op jit(solution)/shard_map/ppermute | solution.py:17
  17.1 8.3 %collective-permute-start.17 = (bf16[16,4096]{1,0:T(8,128)(2,1)S(1)}, bf16[16,4096]{1,0:T(8,128)(2,1)S(1)}, u32[]{:S(2)}, u32[]{:S(2)}) collective-permute-start(bf16[16,4096]{1,0:T(8,128)(2,1)S(1)} %get-tuple-element.64), channel_id=1, source_target_pairs={{0,2},{1,3},{2,0},{3,1},{4,6},{5,7},{6,4},{7,5},{8,10},{9,11},{10,... | collective-permute-start | bytes 393224 | tf_op jit(solution)/shard_map/ppermute | solution.py:17
  18.7 8.3 %collective-permute-start.18 = (bf16[16,4096]{1,0:T(8,128)(2,1)S(1)}, bf16[16,4096]{1,0:T(8,128)(2,1)S(1)}, u32[]{:S(2)}, u32[]{:S(2)}) collective-permute-start(bf16[16,4096]{1,0:T(8,128)(2,1)S(1)} %get-tuple-element.65), channel_id=1, source_target_pairs={{0,4},{1,5},{2,6},{3,7},{4,0},{5,1},{6,2},{7,3},{8,12},{9,13},{10,... | collective-permute-start | bytes 393224 | tf_op jit(solution)/shard_map/ppermute | solution.py:17
  20.6 8.0 %collective-permute-start.24 = (bf16[16,4096]{1,0:T(8,128)(2,1)S(1)}, bf16[16,4096]{1,0:T(8,128)(2,1)S(1)}, u32[]{:S(2)}, u32[]{:S(2)}) collective-permute-start(bf16[16,4096]{1,0:T(8,128)(2,1)S(1)} %get-tuple-element.63.refs_4_), channel_id=1, source_target_pairs={{0,1},{1,0},{2,3},{3,2},{4,5},{5,4},{6,7},{7,6},{8,9},{9,8},{10,11... | collective-permute-start | bytes 393224 | tf_op jit(solution)/shard_map/ppermute | solution.py:17
  26.9 20.8 %collective-permute-start.32 = (bf16[32,4096]{1,0:T(8,128)(2,1)S(1)}, bf16[32,4096]{1,0:T(8,128)(2,1)S(1)}, u32[]{:S(2)}, u32[]{:S(2)}) collective-permute-start(bf16[32,4096]{1,0:T(8,128)(2,1)S(1)} %get-tuple-element.74), channel_id=1, source_target_pairs={{0,8},{1,9},{2,10},{3,11},{4,12},{5,13},{6,14},{7,15},{8,0},{9,1},... | collective-permute-start | bytes 786440 | tf_op jit(solution)/shard_map/ppermute | solution.py:17
  27.3 12.0 %collective-permute-start.16 = (bf16[16,4096]{1,0:T(8,128)(2,1)S(1)}, bf16[16,4096]{1,0:T(8,128)(2,1)S(1)}, u32[]{:S(2)}, u32[]{:S(2)}) collective-permute-start(bf16[16,4096]{1,0:T(8,128)(2,1)S(1)} %get-tuple-element.62), channel_id=1, source_target_pairs={{0,6},{1,7},{2,4},{3,5},{4,2},{5,3},{6,0},{7,1},{8,14},{9,15},{10,... | collective-permute-start | bytes 393224 | tf_op jit(solution)/shard_map/ppermute | solution.py:17
  28.6 10.6 %collective-permute-start.20 = (bf16[16,4096]{1,0:T(8,128)(2,1)S(1)}, bf16[16,4096]{1,0:T(8,128)(2,1)S(1)}, u32[]{:S(2)}, u32[]{:S(2)}) collective-permute-start(bf16[16,4096]{1,0:T(8,128)(2,1)S(1)} %get-tuple-element.59.refs_0_), channel_id=1, source_target_pairs={{0,1},{1,0},{2,3},{3,2},{4,5},{5,4},{6,7},{7,6},{8,9},{9,8},{10,11... | collective-permute-start | bytes 393224 | tf_op jit(solution)/shard_map/ppermute | solution.py:17
  29.7 23.1 %collective-permute-start.1 = (bf16[32,4096]{1,0:T(8,128)(2,1)S(1)}, bf16[32,4096]{1,0:T(8,128)(2,1)S(1)}, u32[]{:S(2)}, u32[]{:S(2)}) collective-permute-start(bf16[32,4096]{1,0:T(8,128)(2,1)S(1)} %get-tuple-element.48), channel_id=1, source_target_pairs={{0,8},{1,9},{2,10},{3,11},{4,12},{5,13},{6,14},{7,15},{8,0},{9,1},... | collective-permute-start | bytes 786440 | tf_op jit(solution)/shard_map/ppermute | solution.py:17
  39.3 9.5 %collective-permute-start.26 = (bf16[16,4096]{1,0:T(8,128)(2,1)S(1)}, bf16[16,4096]{1,0:T(8,128)(2,1)S(1)}, u32[]{:S(2)}, u32[]{:S(2)}) collective-permute-start(bf16[16,4096]{1,0:T(8,128)(2,1)S(1)} %collective-permute-done.18.refs_6_), channel_id=1, source_target_pairs={{0,1},{1,0},{2,3},{3,2},{4,5},{5,4},{6,7},{7,6},{8,9},{9,8},{10,11... | collective-permute-start | bytes 393224 | tf_op jit(solution)/shard_map/ppermute | solution.py:17
  39.3 10.1 %collective-permute-start.27 = (bf16[16,4096]{1,0:T(8,128)(2,1)S(1)}, bf16[16,4096]{1,0:T(8,128)(2,1)S(1)}, u32[]{:S(2)}, u32[]{:S(2)}) collective-permute-start(bf16[16,4096]{1,0:T(8,128)(2,1)S(1)} %collective-permute-done.19.refs_7_), channel_id=1, source_target_pairs={{0,1},{1,0},{2,3},{3,2},{4,5},{5,4},{6,7},{7,6},{8,9},{9,8},{10,11... | collective-permute-start | bytes 393224 | tf_op jit(solution)/shard_map/ppermute | solution.py:17
  39.8 14.1 %collective-permute-start.21 = (bf16[16,4096]{1,0:T(8,128)(2,1)S(1)}, bf16[16,4096]{1,0:T(8,128)(2,1)S(1)}, u32[]{:S(2)}, u32[]{:S(2)}) collective-permute-start(bf16[16,4096]{1,0:T(8,128)(2,1)S(1)} %collective-permute-done.14.refs_1_), channel_id=1, source_target_pairs={{0,1},{1,0},{2,3},{3,2},{4,5},{5,4},{6,7},{7,6},{8,9},{9,8},{10,11... | collective-permute-start | bytes 393224 | tf_op jit(solution)/shard_map/ppermute | solution.py:17
  47.7 8.3 %collective-permute-start.22 = (bf16[16,4096]{1,0:T(8,128)(2,1)S(1)}, bf16[16,4096]{1,0:T(8,128)(2,1)S(1)}, u32[]{:S(2)}, u32[]{:S(2)}) collective-permute-start(bf16[16,4096]{1,0:T(8,128)(2,1)S(1)} %collective-permute-done.15.refs_2_), channel_id=1, source_target_pairs={{0,1},{1,0},{2,3},{3,2},{4,5},{5,4},{6,7},{7,6},{8,9},{9,8},{10,11... | collective-permute-start | bytes 393224 | tf_op jit(solution)/shard_map/ppermute | solution.py:17
  48.8 8.7 %collective-permute-start.23 = (bf16[16,4096]{1,0:T(8,128)(2,1)S(1)}, bf16[16,4096]{1,0:T(8,128)(2,1)S(1)}, u32[]{:S(2)}, u32[]{:S(2)}) collective-permute-start(bf16[16,4096]{1,0:T(8,128)(2,1)S(1)} %collective-permute-done.16.refs_3_), channel_id=1, source_target_pairs={{0,1},{1,0},{2,3},{3,2},{4,5},{5,4},{6,7},{7,6},{8,9},{9,8},{10,11... | collective-permute-start | bytes 393224 | tf_op jit(solution)/shard_map/ppermute | solution.py:17
  49.4 8.1 %collective-permute-start.33 = (bf16[16,4096]{1,0:T(8,128)(2,1)S(1)}, bf16[16,4096]{1,0:T(8,128)(2,1)S(1)}, u32[]{:S(2)}, u32[]{:S(2)}) collective-permute-start(bf16[16,4096]{1,0:T(8,128)(2,1)S(1)} %get-tuple-element.76), channel_id=1, source_target_pairs={{0,2},{1,3},{2,0},{3,1},{4,6},{5,7},{6,4},{7,5},{8,10},{9,11},{10,... | collective-permute-start | bytes 393224 | tf_op jit(solution)/shard_map/ppermute | solution.py:17
  53.9 14.7 %collective-permute-start.35 = (bf16[16,4096]{1,0:T(8,128)(2,1)S(1)}, bf16[16,4096]{1,0:T(8,128)(2,1)S(1)}, u32[]{:S(2)}, u32[]{:S(2)}) collective-permute-start(bf16[16,4096]{1,0:T(8,128)(2,1)S(1)} %get-tuple-element.78), channel_id=1, source_target_pairs={{0,6},{1,7},{2,4},{3,5},{4,2},{5,3},{6,0},{7,1},{8,14},{9,15},{10,... | collective-permute-start | bytes 393224 | tf_op jit(solution)/shard_map/ppermute | solution.py:17
  56.0 13.2 %collective-permute-start.2 = (bf16[16,4096]{1,0:T(8,128)(2,1)S(1)}, bf16[16,4096]{1,0:T(8,128)(2,1)S(1)}, u32[]{:S(2)}, u32[]{:S(2)}) collective-permute-start(bf16[16,4096]{1,0:T(8,128)(2,1)S(1)} %get-tuple-element.50), channel_id=1, source_target_pairs={{0,2},{1,3},{2,0},{3,1},{4,6},{5,7},{6,4},{7,5},{8,10},{9,11},{10,... | collective-permute-start | bytes 393224 | tf_op jit(solution)/shard_map/ppermute | solution.py:17
  57.5 11.8 %collective-permute-start.3 = (bf16[16,4096]{1,0:T(8,128)(2,1)S(1)}, bf16[16,4096]{1,0:T(8,128)(2,1)S(1)}, u32[]{:S(2)}, u32[]{:S(2)}) collective-permute-start(bf16[16,4096]{1,0:T(8,128)(2,1)S(1)} %get-tuple-element.51), channel_id=1, source_target_pairs={{0,4},{1,5},{2,6},{3,7},{4,0},{5,1},{6,2},{7,3},{8,12},{9,13},{10,... | collective-permute-start | bytes 393224 | tf_op jit(solution)/shard_map/ppermute | solution.py:17
  57.5 12.2 %collective-permute-start.4 = (bf16[16,4096]{1,0:T(8,128)(2,1)S(1)}, bf16[16,4096]{1,0:T(8,128)(2,1)S(1)}, u32[]{:S(2)}, u32[]{:S(2)}) collective-permute-start(bf16[16,4096]{1,0:T(8,128)(2,1)S(1)} %get-tuple-element.52), channel_id=1, source_target_pairs={{0,6},{1,7},{2,4},{3,5},{4,2},{5,3},{6,0},{7,1},{8,14},{9,15},{10,... | collective-permute-start | bytes 393224 | tf_op jit(solution)/shard_map/ppermute | solution.py:17
  59.5 10.3 %collective-permute-start.5 = (bf16[16,4096]{1,0:T(8,128)(2,1)S(1)}, bf16[16,4096]{1,0:T(8,128)(2,1)S(1)}, u32[]{:S(2)}, u32[]{:S(2)}) collective-permute-start(bf16[16,4096]{1,0:T(8,128)(2,1)S(1)} %get-tuple-element.49.refs_0_), channel_id=1, source_target_pairs={{0,1},{1,0},{2,3},{3,2},{4,5},{5,4},{6,7},{7,6},{8,9},{9,8},{10,11... | collective-permute-start | bytes 393224 | tf_op jit(solution)/shard_map/ppermute | solution.py:17
  68.6 32.4 %collective-permute-start.28 = (bf16[128,4096]{1,0:T(8,128)(2,1)}, bf16[128,4096]{1,0:T(8,128)(2,1)S(1)}, u32[]{:S(2)}, u32[]{:S(2)}) collective-permute-start(bf16[128,4096]{1,0:T(8,128)(2,1)} %get-tuple-element.68), channel_id=1, source_target_pairs={{0,1},{1,0},{2,3},{3,2},{4,5},{5,4},{6,7},{7,6},{8,9},{9,8},{10,11... | collective-permute-start | bytes 3145736 | tf_op jit(solution)/shard_map/ppermute | solution.py:17
  69.8 8.4 %collective-permute-start.36 = (bf16[16,4096]{1,0:T(8,128)(2,1)S(1)}, bf16[16,4096]{1,0:T(8,128)(2,1)S(1)}, u32[]{:S(2)}, u32[]{:S(2)}) collective-permute-start(bf16[16,4096]{1,0:T(8,128)(2,1)S(1)} %get-tuple-element.75.refs_0_), channel_id=1, source_target_pairs={{0,1},{1,0},{2,3},{3,2},{4,5},{5,4},{6,7},{7,6},{8,9},{9,8},{10,11... | collective-permute-start | bytes 393224 | tf_op jit(solution)/shard_map/ppermute | solution.py:17
  86.3 9.1 %collective-permute-start.12 = (bf16[16,4096]{1,0:T(8,128)(2,1)S(1)}, bf16[16,4096]{1,0:T(8,128)(2,1)S(1)}, u32[]{:S(2)}, u32[]{:S(2)}) collective-permute-start(bf16[16,4096]{1,0:T(8,128)(2,1)S(1)} %get-tuple-element.58), channel_id=1, source_target_pairs={{0,6},{1,7},{2,4},{3,5},{4,2},{5,3},{6,0},{7,1},{8,14},{9,15},{10,... | collective-permute-start | bytes 393224 | tf_op jit(solution)/shard_map/ppermute | solution.py:17
  88.3 8.1 %collective-permute-start.41 = (bf16[16,4096]{1,0:T(8,128)(2,1)S(1)}, bf16[16,4096]{1,0:T(8,128)(2,1)S(1)}, u32[]{:S(2)}, u32[]{:S(2)}) collective-permute-start(bf16[16,4096]{1,0:T(8,128)(2,1)S(1)} %get-tuple-element.82), channel_id=1, source_target_pairs={{0,2},{1,3},{2,0},{3,1},{4,6},{5,7},{6,4},{7,5},{8,10},{9,11},{10,... | collective-permute-start | bytes 393224 | tf_op jit(solution)/shard_map/ppermute | solution.py:17
  90.3 8.1 %collective-permute-start.42 = (bf16[16,4096]{1,0:T(8,128)(2,1)S(1)}, bf16[16,4096]{1,0:T(8,128)(2,1)S(1)}, u32[]{:S(2)}, u32[]{:S(2)}) collective-permute-start(bf16[16,4096]{1,0:T(8,128)(2,1)S(1)} %get-tuple-element.83), channel_id=1, source_target_pairs={{0,4},{1,5},{2,6},{3,7},{4,0},{5,1},{6,2},{7,3},{8,12},{9,13},{10,... | collective-permute-start | bytes 393224 | tf_op jit(solution)/shard_map/ppermute | solution.py:17
  96.3 19.7 %collective-permute-start.13 = (bf16[32,4096]{1,0:T(8,128)(2,1)S(1)}, bf16[32,4096]{1,0:T(8,128)(2,1)S(1)}, u32[]{:S(2)}, u32[]{:S(2)}) collective-permute-start(bf16[32,4096]{1,0:T(8,128)(2,1)S(1)} %relay_back.2), channel_id=1, source_target_pairs={{0,8},{1,9},{2,10},{3,11},{4,12},{5,13},{6,14},{7,15},{8,0},{9,1},... | collective-permute-start | bytes 786440 | tf_op jit(solution)/shard_map/ppermute | solution.py:17
  101.3 15.2 %collective-permute-start.29 = (bf16[16,4096]{1,0:T(8,128)(2,1)S(1)}, bf16[16,4096]{1,0:T(8,128)(2,1)S(1)}, u32[]{:S(2)}, u32[]{:S(2)}) collective-permute-start(bf16[16,4096]{1,0:T(8,128)(2,1)S(1)} %get-tuple-element.70), channel_id=1, source_target_pairs={{0,2},{1,3},{2,0},{3,1},{4,6},{5,7},{6,4},{7,5},{8,10},{9,11},{10,... | collective-permute-start | bytes 393224 | tf_op jit(solution)/shard_map/ppermute | solution.py:17
  103.9 20.4 %collective-permute-start.44 = (bf16[32,4096]{1,0:T(8,128)(2,1)S(1)}, bf16[32,4096]{1,0:T(8,128)(2,1)S(1)}, u32[]{:S(2)}, u32[]{:S(2)}) collective-permute-start(bf16[32,4096]{1,0:T(8,128)(2,1)S(1)} %relay_back.3), channel_id=1, source_target_pairs={{0,8},{1,9},{2,10},{3,11},{4,12},{5,13},{6,14},{7,15},{8,0},{9,1},... | collective-permute-start | bytes 786440 | tf_op jit(solution)/shard_map/ppermute | solution.py:17
  103.9 12.6 %collective-permute-start.30 = (bf16[16,4096]{1,0:T(8,128)(2,1)S(1)}, bf16[16,4096]{1,0:T(8,128)(2,1)S(1)}, u32[]{:S(2)}, u32[]{:S(2)}) collective-permute-start(bf16[16,4096]{1,0:T(8,128)(2,1)S(1)} %get-tuple-element.71), channel_id=1, source_target_pairs={{0,4},{1,5},{2,6},{3,7},{4,0},{5,1},{6,2},{7,3},{8,12},{9,13},{10,... | collective-permute-start | bytes 393224 | tf_op jit(solution)/shard_map/ppermute | solution.py:17
  107.6 15.0 %collective-permute-start.31 = (bf16[16,4096]{1,0:T(8,128)(2,1)S(1)}, bf16[16,4096]{1,0:T(8,128)(2,1)S(1)}, u32[]{:S(2)}, u32[]{:S(2)}) collective-permute-start(bf16[16,4096]{1,0:T(8,128)(2,1)S(1)} %get-tuple-element.72), channel_id=1, source_target_pairs={{0,6},{1,7},{2,4},{3,5},{4,2},{5,3},{6,0},{7,1},{8,14},{9,15},{10,... | collective-permute-start | bytes 393224 | tf_op jit(solution)/shard_map/ppermute | solution.py:17
  116.1 8.3 %collective-permute-start.45 = (bf16[16,4096]{1,0:T(8,128)(2,1)S(1)}, bf16[16,4096]{1,0:T(8,128)(2,1)S(1)}, u32[]{:S(2)}, u32[]{:S(2)}) collective-permute-start(bf16[16,4096]{1,0:T(8,128)(2,1)S(1)} %get-tuple-element.86), channel_id=1, source_target_pairs={{0,2},{1,3},{2,0},{3,1},{4,6},{5,7},{6,4},{7,5},{8,10},{9,11},{10,... | collective-permute-start | bytes 393224 | tf_op jit(solution)/shard_map/ppermute | solution.py:17
  116.5 7.8 %collective-permute-start.46 = (bf16[16,4096]{1,0:T(8,128)(2,1)S(1)}, bf16[16,4096]{1,0:T(8,128)(2,1)S(1)}, u32[]{:S(2)}, u32[]{:S(2)}) collective-permute-start(bf16[16,4096]{1,0:T(8,128)(2,1)S(1)} %get-tuple-element.87), channel_id=1, source_target_pairs={{0,4},{1,5},{2,6},{3,7},{4,0},{5,1},{6,2},{7,3},{8,12},{9,13},{10,... | collective-permute-start | bytes 393224 | tf_op jit(solution)/shard_map/ppermute | solution.py:17
  116.5 11.2 %collective-permute-start.47 = (bf16[16,4096]{1,0:T(8,128)(2,1)S(1)}, bf16[16,4096]{1,0:T(8,128)(2,1)S(1)}, u32[]{:S(2)}, u32[]{:S(2)}) collective-permute-start(bf16[16,4096]{1,0:T(8,128)(2,1)S(1)} %get-tuple-element.88), channel_id=1, source_target_pairs={{0,6},{1,7},{2,4},{3,5},{4,2},{5,3},{6,0},{7,1},{8,14},{9,15},{10,... | collective-permute-start | bytes 393224 | tf_op jit(solution)/shard_map/ppermute | solution.py:17
  (27 other events, 125.9 us)

commit v2 on v0

v2 whole, which is shorter than its diff:
```python
import math

import jax
import jax.numpy as jnp
from jax import lax
from jax.experimental import pallas as pl
from jax.experimental.pallas import tpu as pltpu
from jax.sharding import PartitionSpec as P

EPS = 1e-06
MIB = 1 << 20
VMEM = pltpu.VMEM
SMEM = pltpu.SMEM


def exchange(value, distance):
    return lax.ppermute(value, "ep", [(i, i ^ distance) for i in range(lax.axis_size("ep"))])


def whole(array):
    return pl.BlockSpec(array.shape, lambda: (0,) * array.ndim, memory_space=VMEM)


def params(mib):
    return pltpu.CompilerParams(vmem_limit_bytes=mib * MIB)


def cost(flops, moved):
    return pl.CostEstimate(flops=int(flops), bytes_accessed=int(moved), transcendentals=0)


def slots_of(half, cap):
    chip = lax.axis_index("ep") // 2
    lane = lax.broadcasted_iota(jnp.int32, (half * cap, 1), 0)
    apart = lane // cap
    position = chip & (half - 1)
    expert = (chip - position) + (apart ^ position)
    return expert.astype(jnp.float32), (lane - apart * cap).astype(jnp.float32)


def slot_hits(info, expert, slot):
    width, rows = info.shape
    named = info[0:1, :] == expert
    for k in range(1, width // 2):
        named = jnp.logical_or(named, info[k : k + 1, :] == expert)
    row = lax.broadcasted_iota(jnp.int32, (rows, rows), 0)
    col = lax.broadcasted_iota(jnp.int32, (rows, rows), 1)
    earlier = jnp.where(row < col, 1.0, 0.0).astype(jnp.bfloat16)
    ones = jnp.where(named, 1.0, 0.0)
    rank = jnp.dot(ones.astype(jnp.bfloat16), earlier, preferred_element_type=jnp.float32)
    return jnp.where(rank == slot, ones, 0.0)


def spread_rows(info, rows_bf16, out_refs, cap):
    half = len(out_refs)
    expert, slot = slots_of(half, cap)
    hits = slot_hits(info, expert, slot).astype(jnp.bfloat16)
    placed = jnp.dot(hits, rows_bf16, preferred_element_type=jnp.float32).astype(jnp.bfloat16)
    for d in range(half):
        out_refs[d][...] = placed[d * cap : (d + 1) * cap, :]


def weighted_rows(info, half, joined, cap):
    top = info.shape[0] // 2
    expert, slot = slots_of(half, cap)
    hits = slot_hits(info, expert, slot)
    weight = jnp.zeros_like(hits)
    for k in range(top):
        weight = weight + jnp.where(info[k : k + 1, :] == expert, info[top + k : top + k + 1, :], 0.0)
    weight = weight * hits
    high = weight.astype(jnp.bfloat16)
    low = (weight - high.astype(jnp.float32)).astype(jnp.bfloat16)
    values = joined[...]
    first = (((0,), (0,)), ((), ()))
    return lax.dot_general(high, values, first, preferred_element_type=jnp.float32) + lax.dot_general(
        low, values, first, preferred_element_type=jnp.float32
    )


def unit_rows(values, gain):
    return values * lax.rsqrt(jnp.mean(values * values, axis=-1, keepdims=True) + EPS) * gain


def attend(cache_len, arrays, before, chunk, chunks, half, cap):
    queries, hidden_in, stored_keys, stored_values, token_keys, token_values = arrays[:6]
    ids, gates = arrays[9:]
    rows, width = hidden_in.shape[0] // chunks, hidden_in.shape[1]
    cache_rows, kv_width = stored_keys.shape
    token_rows = token_keys.shape[0]
    head = arrays[6].shape[0]
    heads_kv = kv_width // head
    heads = width // head
    group = heads // heads_kv
    keys = cache_rows + token_rows
    top = ids.shape[0]
    first, last = chunk == 0, chunk == chunks - 1
    mine = pl.ds(chunk * rows, rows)
    per = max(1, min(group, 256 // rows))
    block = per * rows
    near_rows = cap * chunks if last else cap
    out_shape = [
        jax.ShapeDtypeStruct((rows, width), jnp.float32),
        jax.ShapeDtypeStruct((rows, width), jnp.bfloat16),
    ]
    out_shape += [jax.ShapeDtypeStruct((near_rows, width), jnp.bfloat16)] * half
    if first:
        out_shape.append(jax.ShapeDtypeStruct((2 * top, token_rows), jnp.float32))

    def body(len_ref, *refs):
        hbm, refs = refs[:11], refs[11:]
        carried, refs = refs[: len(before)], refs[len(before) :]
        outs, scratch = refs[: len(out_shape)], refs[len(out_shape) :]
        (q_ref, hid_ref, sk_ref, sv_ref, tk_ref, tv_ref, qg_ref, kg_ref, ng_ref, ids_ref, gates_ref) = scratch[:11]
        kn_ref, vx_ref, qs_ref, info_ref, sems = scratch[11:]
        resid_ref, normed_ref, out_refs = outs[0], outs[1], outs[2 : 2 + half]
        copies = []
        for i in range(11):
            source = hbm[i].at[mine, :] if i < 2 else hbm[i]
            target = scratch[i].at[0] if 6 <= i < 9 else scratch[i]
            copies.append(pltpu.make_async_copy(source, target, sems.at[i]))
        order = (2, 7, 4, 0, 6, 3, 5, 9, 10, 1, 8)
        for i in order:
            copies[i].start()
        length = len_ref[0]
        live = lax.broadcasted_iota(jnp.int32, (cache_rows, head), 0) < length
        live_ones = jnp.where(live, 1.0, 0.0).astype(jnp.bfloat16)
        for i in (2, 7, 4):
            copies[i].wait()
        k_gain = kg_ref[...]
        for g in range(heads_kv):
            cols = slice(g * head, (g + 1) * head)
            kn_ref[g, :cache_rows, :] = unit_rows(sk_ref[:, cols].astype(jnp.float32), k_gain).astype(jnp.bfloat16)
            kn_ref[g, cache_rows:, :] = unit_rows(tk_ref[:, cols].astype(jnp.float32), k_gain).astype(jnp.bfloat16)
        for i in (0, 6):
            copies[i].wait()
        q_gain = qg_ref[...] * (math.log2(math.e) / math.sqrt(head))
        for h in range(heads):
            x = q_ref[:, h * head : (h + 1) * head].astype(jnp.float32)
            qs_ref[h * rows : (h + 1) * rows, :] = unit_rows(x, q_gain).astype(jnp.bfloat16)
        for i in (3, 5):
            copies[i].wait()
        for g in range(heads_kv):
            cols = slice(g * head, (g + 1) * head)
            vx_ref[g, :cache_rows, :head] = jnp.where(live, sv_ref[:, cols].astype(jnp.float32), 0.0).astype(
                jnp.bfloat16
            )
            vx_ref[g, :cache_rows, head:] = live_ones
            vx_ref[g, cache_rows:, :head] = tv_ref[:, cols]
            vx_ref[g, cache_rows:, head:] = jnp.ones((token_rows, head), jnp.bfloat16)
        for i in (9, 10, 1, 8):
            copies[i].wait()
        info_ref[:top, :] = ids_ref[...].astype(jnp.float32)
        info_ref[top:, :] = gates_ref[...]
        if first:
            outs[-1][...] = info_ref[...]
        own = lax.broadcasted_iota(jnp.int32, (block, token_rows), 0) % rows + chunk * rows
        causal = lax.broadcasted_iota(jnp.int32, (block, token_rows), 1) <= own
        square = jnp.zeros((rows, head), jnp.float32)
        last_dims = (((1,), (1,)), ((), ()))
        for b in range(heads // per):
            g = b * per // group
            q_block = qs_ref[b * block : (b + 1) * block, :]
            scores = lax.dot_general(q_block, kn_ref[g, :cache_rows, :], last_dims, preferred_element_type=jnp.float32)
            raised = jnp.exp2(scores).astype(jnp.bfloat16)
            scores_new = lax.dot_general(
                q_block, kn_ref[g, cache_rows:, :], last_dims, preferred_element_type=jnp.float32
            )
            raised_new = jnp.where(causal, jnp.exp2(scores_new), 0.0).astype(jnp.bfloat16)
            summed = jnp.dot(raised, vx_ref[g, :cache_rows, :], preferred_element_type=jnp.float32) + jnp.dot(
                raised_new, vx_ref[g, cache_rows:, :], preferred_element_type=jnp.float32
            )
            attended = (summed[:, :head] / summed[:, head:]).astype(jnp.bfloat16).astype(jnp.float32)
            for i in range(per):
                cols = slice((b * per + i) * head, (b * per + i + 1) * head)
                resid = hid_ref[:, cols].astype(jnp.float32) + attended[i * rows : (i + 1) * rows, :]
                resid_ref[:, cols] = resid
                square = square + resid * resid
        scale = lax.rsqrt(jnp.sum(square, axis=-1, keepdims=True) / width + EPS)
        normed = (resid_ref[...] * scale * ng_ref[...]).astype(jnp.bfloat16)
        normed_ref[...] = normed
        tail = slice(near_rows - cap, near_rows)
        spread_rows(info_ref[:, chunk * rows : (chunk + 1) * rows], normed, [o.at[tail, :] for o in out_refs], cap)
        for i in range(len(before)):
            out_refs[i][: near_rows - cap, :] = carried[i][...]

    results = pl.pallas_call(
        body,
        out_shape=out_shape,
        in_specs=[pl.BlockSpec(memory_space=SMEM)]
        + [pl.BlockSpec(memory_space=pl.ANY)] * 11
        + [whole(b) for b in before],
        out_specs=[whole(o) for o in out_shape],
        scratch_shapes=[
            VMEM((rows, width), jnp.bfloat16),
            VMEM((rows, width), jnp.bfloat16),
            VMEM((cache_rows, kv_width), jnp.bfloat16),
            VMEM((cache_rows, kv_width), jnp.bfloat16),
            VMEM((token_rows, kv_width), jnp.bfloat16),
            VMEM((token_rows, kv_width), jnp.bfloat16),
            VMEM((1, head), jnp.float32),
            VMEM((1, head), jnp.float32),
            VMEM((1, width), jnp.float32),
            VMEM((top, token_rows), jnp.int32),
            VMEM((top, token_rows), jnp.float32),
            VMEM((heads_kv, keys, head), jnp.bfloat16),
            VMEM((heads_kv, keys, 2 * head), jnp.bfloat16),
            VMEM((rows * heads, head), jnp.bfloat16),
            VMEM((2 * top, token_rows), jnp.float32),
            pltpu.SemaphoreType.DMA((11,)),
        ],
        compiler_params=params(24),
        cost_estimate=cost(4 * rows * width * keys, 6 * MIB),
        name="attend",
    )(cache_len, *arrays, *before)
    return results[0], results[1], list(results[2 : 2 + half]), (results[-1] if first else None)


def relay(rows_in, info, chunk, half, cap):
    rows, width = rows_in.shape
    out = jax.ShapeDtypeStruct((cap, width), jnp.bfloat16)

    def body(rows_ref, info_ref, *out_refs):
        spread_rows(info_ref[:, chunk * rows : (chunk + 1) * rows], rows_ref[...], out_refs, cap)

    return list(
        pl.pallas_call(
            body,
            out_shape=[out] * half,
            in_specs=[whole(rows_in), whole(info)],
            out_specs=[whole(out)] * half,
            compiler_params=params(24),
            cost_estimate=cost(2 * half * cap * rows * width, MIB),
            name="relay",
        )(rows_in, info)
    )


def expert(own, weights):
    cap, width = own[0].shape
    count = len(own)
    hidden = weights[0].shape[1]
    total = count * cap
    block = min(total, 128)
    part = 512
    out = jax.ShapeDtypeStruct((cap, width), jnp.bfloat16)

    def body(*refs):
        ins, (wg0, wu0, wd0, wg1, wu1, wd1) = refs[:count], refs[count : count + 6]
        outs, (x_ref, y_ref) = refs[count + 6 : 2 * count + 6], refs[2 * count + 6 :]
        for i in range(count):
            x_ref[i * cap : (i + 1) * cap, :] = ins[i][...]

        def rows_of(span):
            inners = []
            for wg, wu in ((wg0, wu0), (wg1, wu1)):
                pre = jnp.zeros((block, 2 * hidden), jnp.float32)
                for k in range(0, width, part):
                    both = jnp.concatenate([wg[k : k + part, :], wu[k : k + part, :]], axis=1)
                    pre = pre + jnp.dot(x_ref[span, k : k + part], both, preferred_element_type=jnp.float32)
                gate = pre[:, :hidden]
                inners.append((gate / (1.0 + jnp.exp(-gate)) * pre[:, hidden:]).astype(jnp.bfloat16))
            inner = jnp.concatenate(inners, axis=1)
            for k in range(0, width, part):
                down = jnp.concatenate([wd0[:, k : k + part], wd1[:, k : k + part]], axis=0)
                y_ref[span, k : k + part] = jnp.dot(inner, down, preferred_element_type=jnp.float32).astype(
                    jnp.bfloat16
                )

        if total == block:
            rows_of(slice(0, block))
        else:

            @pl.loop(0, total // block)
            def _(r):
                rows_of(pl.ds(pl.multiple_of(r * block, block), block))

        for i in range(count):
            outs[i][...] = y_ref[i * cap : (i + 1) * cap, :]

    return list(
        pl.pallas_call(
            body,
            out_shape=[out] * count,
            in_specs=[whole(own[0])] * count + [whole(w) for w in weights],
            out_specs=[whole(out)] * count,
            scratch_shapes=[VMEM((total, width), jnp.bfloat16)] * 2,
            compiler_params=params(24),
            cost_estimate=cost(12 * total * width * hidden, 12 * width * hidden),
            name="expert",
        )(*own, *weights)
    )


def relay_back(returned, info, chunk, rows, cap):
    half = len(returned)
    width = returned[0].shape[1]
    out = jax.ShapeDtypeStruct((rows, width), jnp.bfloat16)

    def body(info_ref, *refs):
        in_refs, out_ref, joined = refs[:half], refs[half], refs[half + 1]
        for d in range(half):
            joined[d * cap : (d + 1) * cap, :] = in_refs[d][...]
        far = weighted_rows(info_ref[:, chunk * rows : (chunk + 1) * rows], half, joined, cap)
        out_ref[...] = far.astype(jnp.bfloat16)

    return pl.pallas_call(
        body,
        out_shape=out,
        in_specs=[whole(info)] + [whole(returned[0])] * half,
        out_specs=whole(out),
        scratch_shapes=[VMEM((half * cap, width), jnp.bfloat16)],
        compiler_params=params(24),
        cost_estimate=cost(4 * half * cap * rows * width, MIB),
        name="relay_back",
    )(info, *returned)


def finish(resid, returned, far, info, chunk, chunks, cap, previous):
    half = len(returned)
    rows, width = resid.shape
    out = jax.ShapeDtypeStruct((rows * chunks, width), jnp.bfloat16)
    extra = [] if previous is None else [previous]

    def body(*refs):
        info_ref, resid_ref, far_ref = refs[len(extra) : len(extra) + 3]
        refs = refs[len(extra) + 3 :]
        in_refs, out_hbm, joined, out_ref, sem = refs[:half], *refs[half:]
        for d in range(half):
            joined[d * cap : (d + 1) * cap, :] = in_refs[d][chunk * cap : (chunk + 1) * cap, :]
        near = weighted_rows(info_ref[:, chunk * rows : (chunk + 1) * rows], half, joined, cap)
        out_ref[...] = (resid_ref[...] + (near + far_ref[...].astype(jnp.float32))).astype(jnp.bfloat16)
        copy = pltpu.make_async_copy(out_ref, out_hbm.at[pl.ds(chunk * rows, rows), :], sem)
        copy.start()
        copy.wait()

    return pl.pallas_call(
        body,
        out_shape=out,
        in_specs=[pl.BlockSpec(memory_space=pl.ANY)] * len(extra)
        + [whole(info), whole(resid), whole(far)]
        + [whole(returned[0])] * half,
        out_specs=pl.BlockSpec(memory_space=pl.ANY),
        scratch_shapes=[
            VMEM((half * cap, width), jnp.bfloat16),
            VMEM((rows, width), jnp.bfloat16),
            pltpu.SemaphoreType.DMA,
        ],
        input_output_aliases={0: 0} if extra else {},
        compiler_params=params(24),
        cost_estimate=cost(4 * half * cap * rows * width, 2 * MIB),
        name="finish",
    )(*extra, info, resid, far, *returned)


def around(parts):
    return [parts[0]] + [exchange(parts[d], 2 * d) for d in range(1, len(parts))]


def local(
    hidden_in,
    queries,
    token_keys,
    token_values,
    stored_keys,
    stored_values,
    cache_len,
    query_gain,
    k_gain,
    norm_gain,
    expert_ids,
    gate_weights,
    w_gate,
    w_up,
    w_down,
):
    token_rows, top = expert_ids.shape
    ep = lax.axis_size("ep")
    experts = ep // 2
    half = experts // 2
    slots = 2 * token_rows * top // experts
    chunks = 2 if slots >= 32 else 1
    cap = slots // chunks
    rows = token_rows // chunks
    arrays = (
        queries,
        hidden_in,
        stored_keys,
        stored_values,
        token_keys,
        token_values,
        query_gain,
        k_gain,
        norm_gain,
        expert_ids.T,
        gate_weights.T,
    )
    weights = (w_gate, w_up, w_down)
    weights = weights + tuple(exchange(w, 1) for w in weights)

    resid, far_rows, outgoing, info = [], [], [], None
    for c in range(chunks):
        residual, normed, outgoing, packed = attend(cache_len, arrays, outgoing, c, chunks, half, cap)
        info = packed if c == 0 else info
        resid.append(residual)
        far_rows.append(exchange(normed, ep // 2))
    far_info = exchange(info, ep // 2)
    near_back = around(expert(around(outgoing), weights))
    far_back = []
    for c in range(chunks):
        placed = around(relay(far_rows[c], far_info, c, half, cap))
        returned = around(expert(placed, weights))
        far_back.append(exchange(relay_back(returned, far_info, c, rows, cap), ep // 2))
    result = None
    for c in range(chunks):
        result = finish(resid[c], near_back, far_back[c], info, c, chunks, cap, result)
    return result


def solution(mesh):
    in_specs = (
        P(("grp", "ep"), None),
        P(("grp", "ep"), None),
        P(("grp", "ep"), None),
        P(("grp", "ep"), None),
        P(("grp", "ep"), None),
        P(("grp", "ep"), None),
        P(("grp", "ep")),
        P(),
        P(),
        P(),
        P(("grp", "ep"), None),
        P(("grp", "ep"), None),
        P(None, "ep"),
        P(None, "ep"),
        P("ep", None),
    )
    out_specs = P(("grp", "ep"), None)
    return jax.shard_map(local, mesh=mesh, in_specs=in_specs, out_specs=out_specs, check_vma=False)
```

time: 245 us -> 116 us (0.47)
  the two profiles are of different devices: /device:TPU:13 before, /device:TPU:0 now
where the time goes in v2:
time: 116 us
  waiting for transfers between devices  44.5 us (38%)
  starting transfers between devices  33.1 us (29%)
  Pallas kernels  24.4 us (21%)
  local copies, waits for them, and re-layouts  12.8 us (11%)
    ppermute x26, waiting for transfers between devices, exchange(): lax.ppermute(value, 'ep', [(i, i ^ distance) for i in range(lax.axis_size...  44.5 us
    ppermute x26, starting transfers between devices, exchange(): lax.ppermute(value, 'ep', [(i, i ^ distance) for i in range(lax.axis_size...  33.1 us
    unnamed x28, local copies, waits for them, and re-layouts  12.8 us
    pallas_call x3, Pallas kernels, expert(): pl.pallas_call(body, out_shape=[out] * count, in_specs=[whole(own[0])] *...  12.4 us
    pallas_call x2, Pallas kernels, attend(): pl.pallas_call(body, out_shape=out_shape, in_specs=[pl.BlockSpec(memory_s...  7.45 us
    pallas_call x2, Pallas kernels, finish(): pl.pallas_call(body, out_shape=out, in_specs=[pl.BlockSpec(memory_space=p...  2.58 us
  transfers between devices with their start and end apart: 26, of which 11 were waited for; matrix products, arithmetic and copies ran while one was open for 0% of the time, Pallas kernels for 20%

profile of v2, /device:TPU:0, one launch (start us, length us, event | category | flops | bytes accessed | tf_op | source)
XLA Modules:
  0.0 115.8 jit_solution(216523367743124638)
XLA Ops:
  2.7 1.0 copy-done.4
  3.7 1.0 copy-done.5
  4.7 1.0 copy-done.6
  10.7 3.6 %attend.2 = (f32[32,4096]{1,0:T(8,128)S(1)}, bf16[32,4096]{1,0:T(8,128)(2,1)S(1)}, bf16[16,4096]{1,0:T(8,128)(2,1)S(1)}, bf16[16,4096]{1,0:T(8,128)(2,1)S(1)}, b...) custom-call(s32[1]{0:T(128)S(6)} %copy.18.len_ref, bf16[64,4096]{1,0:T(8,128)(2,1)S(1)} %copy-done.3, ...), custom_call_target="tpu_custom_call" | custom-call | flops 570425344 | bytes 6291456 | tf_op jit(solution)/shard_map/attend/pallas_call | solution.py:186
  14.3 4.0 %collective-permute-start = (f32[4,64]{1,0:T(4,128)S(1)}, f32[4,64]{1,0:T(4,128)S(1)}, u32[]{:S(2)}, u32[]{:S(2)}) collective-permute-start(f32[4,64]{1,0:T(4,128)S(1)} %get-tuple-element.38.refs_0_.refs_1_), channel_id=1, source_target_pairs={{0,8},{1,9},{2,10},{3,11},{4,12},{5,13},{6,14},{7,15},{8,0},{9,1},... | collective-permute-start | bytes 3080 | tf_op jit(solution)/shard_map/ppermute | solution.py:17
  18.4 3.8 %attend.3 = (f32[32,4096]{1,0:T(8,128)S(1)}, bf16[32,4096]{1,0:T(8,128)(2,1)S(1)}, bf16[32,4096]{1,0:T(8,128)(2,1)S(1)}, bf16[32,4096]{1,0:T(8,128)(2,1)S(1)}, b...) custom-call(s32[1]{0:T(128)S(6)} %copy.18.len_ref, bf16[64,4096]{1,0:T(8,128)(2,1)S(1)} %copy-done.3, ...), custom_call_target="tpu_custom_call" | custom-call | flops 570425344 | bytes 6291456 | tf_op jit(solution)/shard_map/attend/pallas_call | solution.py:186
  22.3 2.9 %collective-permute-start.18 = (bf16[32,4096]{1,0:T(8,128)(2,1)S(1)}, bf16[32,4096]{1,0:T(8,128)(2,1)S(1)}, u32[]{:S(2)}, u32[]{:S(2)}) collective-permute-start(bf16[32,4096]{1,0:T(8,128)(2,1)S(1)} %get-tuple-element.62), channel_id=1, source_target_pairs={{0,8},{1,9},{2,10},{3,11},{4,12},{5,13},{6,14},{7,15},{8,0},{9,1},... | collective-permute-start | bytes 786440 | tf_op jit(solution)/shard_map/ppermute | solution.py:17
  25.2 14.5 %collective-permute-done.1.rows_ref = bf16[32,4096]{1,0:T(8,128)(2,1)S(1)} collective-permute-done((bf16[32,4096]{1,0:T(8,128)(2,1)S(1)}, bf16[32,4096]{1,0:T(8,128)(2,1)S(1)}, u32[]{:S(2)}, u32[]{:S(2)}) %collective-permute-start.1) | collective-permute-done | bytes 262176 | tf_op jit(solution)/shard_map/ppermute | solution.py:17
  40.0 1.6 %collective-permute-start.2 = (bf16[16,4096]{1,0:T(8,128)(2,1)S(1)}, bf16[16,4096]{1,0:T(8,128)(2,1)S(1)}, u32[]{:S(2)}, u32[]{:S(2)}) collective-permute-start(bf16[16,4096]{1,0:T(8,128)(2,1)S(1)} %get-tuple-element.42), channel_id=1, source_target_pairs={{0,2},{1,3},{2,0},{3,1},{4,6},{5,7},{6,4},{7,5},{8,10},{9,11},{10,... | collective-permute-start | bytes 393224 | tf_op jit(solution)/shard_map/ppermute | solution.py:17
  41.6 2.5 %collective-permute-done.18.rows_ref = bf16[32,4096]{1,0:T(8,128)(2,1)S(1)} collective-permute-done((bf16[32,4096]{1,0:T(8,128)(2,1)S(1)}, bf16[32,4096]{1,0:T(8,128)(2,1)S(1)}, u32[]{:S(2)}, u32[]{:S(2)}) %collective-permute-start.18) | collective-permute-done | bytes 262176 | tf_op jit(solution)/shard_map/ppermute | solution.py:17
  45.1 2.6 %collective-permute-start.4 = (bf16[16,4096]{1,0:T(8,128)(2,1)S(1)}, bf16[16,4096]{1,0:T(8,128)(2,1)S(1)}, u32[]{:S(2)}, u32[]{:S(2)}) collective-permute-start(bf16[16,4096]{1,0:T(8,128)(2,1)S(1)} %get-tuple-element.44), channel_id=1, source_target_pairs={{0,6},{1,7},{2,4},{3,5},{4,2},{5,3},{6,0},{7,1},{8,14},{9,15},{10,... | collective-permute-start | bytes 393224 | tf_op jit(solution)/shard_map/ppermute | solution.py:17
  47.7 2.4 %collective-permute-done.3.refs_2_ = bf16[16,4096]{1,0:T(8,128)(2,1)S(1)} collective-permute-done((bf16[16,4096]{1,0:T(8,128)(2,1)S(1)}, bf16[16,4096]{1,0:T(8,128)(2,1)S(1)}, u32[]{:S(2)}, u32[]{:S(2)}) %collective-permute-start.3) | collective-permute-done | bytes 131104 | tf_op jit(solution)/shard_map/ppermute | solution.py:17
  50.1 1.4 %collective-permute-start.19 = (bf16[16,4096]{1,0:T(8,128)(2,1)S(1)}, bf16[16,4096]{1,0:T(8,128)(2,1)S(1)}, u32[]{:S(2)}, u32[]{:S(2)}) collective-permute-start(bf16[16,4096]{1,0:T(8,128)(2,1)S(1)} %get-tuple-element.64), channel_id=1, source_target_pairs={{0,2},{1,3},{2,0},{3,1},{4,6},{5,7},{6,4},{7,5},{8,10},{9,11},{10,... | collective-permute-start | bytes 393224 | tf_op jit(solution)/shard_map/ppermute | solution.py:17
  53.1 3.5 %collective-permute-done.19.refs_1_ = bf16[16,4096]{1,0:T(8,128)(2,1)S(1)} collective-permute-done((bf16[16,4096]{1,0:T(8,128)(2,1)S(1)}, bf16[16,4096]{1,0:T(8,128)(2,1)S(1)}, u32[]{:S(2)}, u32[]{:S(2)}) %collective-permute-start.19) | collective-permute-done | bytes 131104 | tf_op jit(solution)/shard_map/ppermute | solution.py:17
  56.5 2.9 %collective-permute-start.14 = (bf16[32,4096]{1,0:T(8,128)(2,1)S(1)}, bf16[32,4096]{1,0:T(8,128)(2,1)S(1)}, u32[]{:S(2)}, u32[]{:S(2)}) collective-permute-start(bf16[32,4096]{1,0:T(8,128)(2,1)S(1)} %get-tuple-element.56), channel_id=1, source_target_pairs={{0,6},{1,7},{2,4},{3,5},{4,2},{5,3},{6,0},{7,1},{8,14},{9,15},{10,... | collective-permute-start | bytes 786440 | tf_op jit(solution)/shard_map/ppermute | solution.py:17
  59.7 1.8 %collective-permute-start.21 = (bf16[16,4096]{1,0:T(8,128)(2,1)S(1)}, bf16[16,4096]{1,0:T(8,128)(2,1)S(1)}, u32[]{:S(2)}, u32[]{:S(2)}) collective-permute-start(bf16[16,4096]{1,0:T(8,128)(2,1)S(1)} %get-tuple-element.66), channel_id=1, source_target_pairs={{0,6},{1,7},{2,4},{3,5},{4,2},{5,3},{6,0},{7,1},{8,14},{9,15},{10,... | collective-permute-start | bytes 393224 | tf_op jit(solution)/shard_map/ppermute | solution.py:17
  61.5 1.9 %copy-done.1 = bf16[4096,384]{1,0:T(8,128)(2,1)S(1)} copy-done((bf16[4096,384]{1,0:T(8,128)(2,1)S(1)}, bf16[4096,384]{1,0:T(8,128)(2,1)}, u32[]{:S(2)}) %copy-start.1) | copy-done | bytes 3145752
  63.4 1.9 %copy-done.2 = bf16[384,4096]{1,0:T(8,128)(2,1)S(1)} copy-done((bf16[384,4096]{1,0:T(8,128)(2,1)S(1)}, bf16[384,4096]{1,0:T(8,128)(2,1)}, u32[]{:S(2)}) %copy-start.2) | copy-done | bytes 3145752
  65.3 4.2 %expert.3 = (bf16[16,4096]{1,0:T(8,128)(2,1)S(1)}, bf16[16,4096]{1,0:T(8,128)(2,1)S(1)}, bf16[16,4096]{1,0:T(8,128)(2,1)S(1)}, bf16[16,4096]{1,0:T(8,128)(2,1)S(1)}) custom-call(bf16[16,4096]{1,0:T(8,128)(2,1)S(1)} %get-tuple-element.41.refs_0_, bf16[16,4096]{1,0:T(8,128)(2,1)S(1)} %collective-permute-done.2.refs_1_, ...), custom_call_target="tpu_custom_call" | custom-call | flops 1207959552 | bytes 18874368 | tf_op jit(solution)/shard_map/expert/pallas_call | solution.py:281
  69.5 1.6 %collective-permute-done.20.refs_2_ = bf16[16,4096]{1,0:T(8,128)(2,1)S(1)} collective-permute-done((bf16[16,4096]{1,0:T(8,128)(2,1)S(1)}, bf16[16,4096]{1,0:T(8,128)(2,1)S(1)}, u32[]{:S(2)}, u32[]{:S(2)}) %collective-permute-start.20) | collective-permute-done | bytes 131104 | tf_op jit(solution)/shard_map/ppermute | solution.py:17
  71.9 1.8 %collective-permute-done.21.refs_3_ = bf16[16,4096]{1,0:T(8,128)(2,1)S(1)} collective-permute-done((bf16[16,4096]{1,0:T(8,128)(2,1)S(1)}, bf16[16,4096]{1,0:T(8,128)(2,1)S(1)}, u32[]{:S(2)}, u32[]{:S(2)}) %collective-permute-start.21) | collective-permute-done | bytes 131104 | tf_op jit(solution)/shard_map/ppermute | solution.py:17
  73.8 4.2 %expert.5 = (bf16[16,4096]{1,0:T(8,128)(2,1)S(1)}, bf16[16,4096]{1,0:T(8,128)(2,1)S(1)}, bf16[16,4096]{1,0:T(8,128)(2,1)S(1)}, bf16[16,4096]{1,0:T(8,128)(2,1)S(1)}) custom-call(bf16[16,4096]{1,0:T(8,128)(2,1)S(1)} %get-tuple-element.63.refs_0_, bf16[16,4096]{1,0:T(8,128)(2,1)S(1)} %collective-permute-done.19.refs_1_, ...), custom_call_target="tpu_custom_call" | custom-call | flops 1207959552 | bytes 18874368 | tf_op jit(solution)/shard_map/expert/pallas_call | solution.py:281
  78.0 2.8 %collective-permute-start.10 = (bf16[16,4096]{1,0:T(8,128)(2,1)S(1)}, bf16[16,4096]{1,0:T(8,128)(2,1)S(1)}, u32[]{:S(2)}, u32[]{:S(2)}) collective-permute-start(bf16[16,4096]{1,0:T(8,128)(2,1)S(1)} %get-tuple-element.48), channel_id=1, source_target_pairs={{0,6},{1,7},{2,4},{3,5},{4,2},{5,3},{6,0},{7,1},{8,14},{9,15},{10,... | collective-permute-start | bytes 393224 | tf_op jit(solution)/shard_map/ppermute | solution.py:17
  82.2 2.1 %collective-permute-start.24 = (bf16[16,4096]{1,0:T(8,128)(2,1)S(1)}, bf16[16,4096]{1,0:T(8,128)(2,1)S(1)}, u32[]{:S(2)}, u32[]{:S(2)}) collective-permute-start(bf16[16,4096]{1,0:T(8,128)(2,1)S(1)} %get-tuple-element.70), channel_id=1, source_target_pairs={{0,6},{1,7},{2,4},{3,5},{4,2},{5,3},{6,0},{7,1},{8,14},{9,15},{10,... | collective-permute-start | bytes 393224 | tf_op jit(solution)/shard_map/ppermute | solution.py:17
  84.3 3.9 %expert.4 = (bf16[32,4096]{1,0:T(8,128)(2,1)S(1)}, bf16[32,4096]{1,0:T(8,128)(2,1)S(1)}, bf16[32,4096]{1,0:T(8,128)(2,1)S(1)}, bf16[32,4096]{1,0:T(8,128)(2,1)S(1)}) custom-call(bf16[32,4096]{1,0:T(8,128)(2,1)S(1)} %get-tuple-element.53.refs_0_, bf16[32,4096]{1,0:T(8,128)(2,1)S(1)} %collective-permute-done.12.refs_1_, ...), custom_call_target="tpu_custom_call" | custom-call | flops 2415919104 | bytes 18874368 | tf_op jit(solution)/shard_map/expert/pallas_call | solution.py:281
  90.2 2.1 %collective-permute-start.17 = (bf16[32,4096]{1,0:T(8,128)(2,1)S(1)}, bf16[32,4096]{1,0:T(8,128)(2,1)S(1)}, u32[]{:S(2)}, u32[]{:S(2)}) collective-permute-start(bf16[32,4096]{1,0:T(8,128)(2,1)S(1)} %get-tuple-element.60), channel_id=1, source_target_pairs={{0,6},{1,7},{2,4},{3,5},{4,2},{5,3},{6,0},{7,1},{8,14},{9,15},{10,... | collective-permute-start | bytes 786440 | tf_op jit(solution)/shard_map/ppermute | solution.py:17
  92.3 3.2 %collective-permute-start.11 = (bf16[32,4096]{1,0:T(8,128)(2,1)S(1)}, bf16[32,4096]{1,0:T(8,128)(2,1)S(1)}, u32[]{:S(2)}, u32[]{:S(2)}) collective-permute-start(bf16[32,4096]{1,0:T(8,128)(2,1)S(1)} %relay_back.2), channel_id=1, source_target_pairs={{0,8},{1,9},{2,10},{3,11},{4,12},{5,13},{6,14},{7,15},{8,0},{9,1},... | collective-permute-start | bytes 786440 | tf_op jit(solution)/shard_map/ppermute | solution.py:17
  96.3 9.5 %collective-permute-done.16.refs_5_.refs_6_ = bf16[32,4096]{1,0:T(8,128)(2,1)S(1)} collective-permute-done((bf16[32,4096]{1,0:T(8,128)(2,1)S(1)}, bf16[32,4096]{1,0:T(8,128)(2,1)S(1)}, u32[]{:S(2)}, u32[]{:S(2)}) %collective-permute-start.16) | collective-permute-done | bytes 262176 | tf_op jit(solution)/shard_map/ppermute | solution.py:17
  105.8 4.7 %collective-permute-done.17.refs_6_.refs_7_ = bf16[32,4096]{1,0:T(8,128)(2,1)S(1)} collective-permute-done((bf16[32,4096]{1,0:T(8,128)(2,1)S(1)}, bf16[32,4096]{1,0:T(8,128)(2,1)S(1)}, u32[]{:S(2)}, u32[]{:S(2)}) %collective-permute-start.17) | collective-permute-done | bytes 262176 | tf_op jit(solution)/shard_map/ppermute | solution.py:17
  110.4 1.2 %finish.2.refs_0_ = bf16[64,4096]{1,0:T(8,128)(2,1)} custom-call(f32[4,64]{1,0:T(4,128)S(1)} %get-tuple-element.38.refs_0_.refs_1_, f32[32,4096]{1,0:T(8,128)S(1)} %get-tuple-element.39.refs_1_, bf16[32,4096]{1,0:T(8,128)(2,1)S(1)} %collective-permute-done.11.refs_2_, bf16[32,4096]{1,0:T(8,128)(2,1)S(1)} %get-tuple-element.57.refs_3_.refs_4_, ...), custom_call_target="tpu_custom_call" | custom-call | flops 33554432 | bytes 2097152 | tf_op jit(solution)/shard_map/finish/pallas_call | solution.py:336
  111.6 2.6 %collective-permute-done.25.refs_3_ = bf16[32,4096]{1,0:T(8,128)(2,1)S(1)} collective-permute-done((bf16[32,4096]{1,0:T(8,128)(2,1)S(1)}, bf16[32,4096]{1,0:T(8,128)(2,1)S(1)}, u32[]{:S(2)}, u32[]{:S(2)}) %collective-permute-start.25) | collective-permute-done | bytes 262176 | tf_op jit(solution)/shard_map/ppermute | solution.py:17
  114.2 1.4 %finish.3 = bf16[64,4096]{1,0:T(8,128)(2,1)} custom-call(bf16[64,4096]{1,0:T(8,128)(2,1)} %finish.2.refs_0_, f32[4,64]{1,0:T(4,128)S(1)} %get-tuple-element.38.refs_0_.refs_1_, f32[32,4096]{1,0:T(8,128)S(1)} %get-tuple-element.61.refs_2_, bf16[32,4096]{1,0:T(8,128)(2,1)S(1)} %collective-permute-done.25.refs_3_, ...), custom_call_target="tpu_custom_call", output_to_operand_aliasing={{}: (0, {})} | custom-call | flops 33554432 | bytes 2097152 | tf_op jit(solution)/shard_map/finish/pallas_call | solution.py:336
  (59 shorter events, 15.0 us)
Async XLA Ops:
  0.0 61.5 %copy-start = (bf16[4096,384]{1,0:T(8,128)(2,1)S(1)}, bf16[4096,384]{1,0:T(8,128)(2,1)}, u32[]{:S(2)}) copy-start(bf16[4096,384]{1,0:T(8,128)(2,1)} %refs_4_.9) | copy-start | bytes 9437188
  0.0 56.5 %collective-permute-start.5 = (bf16[4096,384]{1,0:T(8,128)(2,1)}, bf16[4096,384]{1,0:T(8,128)(2,1)S(1)}, u32[]{:S(2)}, u32[]{:S(2)}) collective-permute-start(bf16[4096,384]{1,0:T(8,128)(2,1)} %refs_4_.9), channel_id=1, source_target_pairs={{0,1},{1,0},{2,3},{3,2},{4,5},{5,4},{6,7},{7,6},{8,9},{9,8},{10,11... | collective-permute-start | bytes 9437192 | tf_op jit(solution)/shard_map/ppermute | solution.py:17
  0.5 59.0 %collective-permute-start.6 = (bf16[4096,384]{1,0:T(8,128)(2,1)}, bf16[4096,384]{1,0:T(8,128)(2,1)S(1)}, u32[]{:S(2)}, u32[]{:S(2)}) collective-permute-start(bf16[4096,384]{1,0:T(8,128)(2,1)} %refs_5_.9), channel_id=1, source_target_pairs={{0,1},{1,0},{2,3},{3,2},{4,5},{5,4},{6,7},{7,6},{8,9},{9,8},{10,11... | collective-permute-start | bytes 9437192 | tf_op jit(solution)/shard_map/ppermute | solution.py:17
  0.5 59.2 %collective-permute-start.7 = (bf16[384,4096]{1,0:T(8,128)(2,1)}, bf16[384,4096]{1,0:T(8,128)(2,1)S(1)}, u32[]{:S(2)}, u32[]{:S(2)}) collective-permute-start(bf16[384,4096]{1,0:T(8,128)(2,1)} %refs_6_.9), channel_id=1, source_target_pairs={{0,1},{1,0},{2,3},{3,2},{4,5},{5,4},{6,7},{7,6},{8,9},{9,8},{10,11... | collective-permute-start | bytes 9437192 | tf_op jit(solution)/shard_map/ppermute | solution.py:17
  1.6 1.0 copy-start.3
  2.7 1.0 copy-start.4
  3.7 1.0 copy-start.5
  14.3 7.9 %collective-permute-start = (f32[4,64]{1,0:T(4,128)S(1)}, f32[4,64]{1,0:T(4,128)S(1)}, u32[]{:S(2)}, u32[]{:S(2)}) collective-permute-start(f32[4,64]{1,0:T(4,128)S(1)} %get-tuple-element.38.refs_0_.refs_1_), channel_id=1, source_target_pairs={{0,8},{1,9},{2,10},{3,11},{4,12},{5,13},{6,14},{7,15},{8,0},{9,1},... | collective-permute-start | bytes 3080 | tf_op jit(solution)/shard_map/ppermute | solution.py:17
  18.3 21.3 %collective-permute-start.1 = (bf16[32,4096]{1,0:T(8,128)(2,1)S(1)}, bf16[32,4096]{1,0:T(8,128)(2,1)S(1)}, u32[]{:S(2)}, u32[]{:S(2)}) collective-permute-start(bf16[32,4096]{1,0:T(8,128)(2,1)S(1)} %get-tuple-element.40), channel_id=1, source_target_pairs={{0,8},{1,9},{2,10},{3,11},{4,12},{5,13},{6,14},{7,15},{8,0},{9,1},... | collective-permute-start | bytes 786440 | tf_op jit(solution)/shard_map/ppermute | solution.py:17
  22.3 21.9 %collective-permute-start.18 = (bf16[32,4096]{1,0:T(8,128)(2,1)S(1)}, bf16[32,4096]{1,0:T(8,128)(2,1)S(1)}, u32[]{:S(2)}, u32[]{:S(2)}) collective-permute-start(bf16[32,4096]{1,0:T(8,128)(2,1)S(1)} %get-tuple-element.62), channel_id=1, source_target_pairs={{0,8},{1,9},{2,10},{3,11},{4,12},{5,13},{6,14},{7,15},{8,0},{9,1},... | collective-permute-start | bytes 786440 | tf_op jit(solution)/shard_map/ppermute | solution.py:17
  40.0 5.0 %collective-permute-start.2 = (bf16[16,4096]{1,0:T(8,128)(2,1)S(1)}, bf16[16,4096]{1,0:T(8,128)(2,1)S(1)}, u32[]{:S(2)}, u32[]{:S(2)}) collective-permute-start(bf16[16,4096]{1,0:T(8,128)(2,1)S(1)} %get-tuple-element.42), channel_id=1, source_target_pairs={{0,2},{1,3},{2,0},{3,1},{4,6},{5,7},{6,4},{7,5},{8,10},{9,11},{10,... | collective-permute-start | bytes 393224 | tf_op jit(solution)/shard_map/ppermute | solution.py:17
  44.2 5.9 %collective-permute-start.3 = (bf16[16,4096]{1,0:T(8,128)(2,1)S(1)}, bf16[16,4096]{1,0:T(8,128)(2,1)S(1)}, u32[]{:S(2)}, u32[]{:S(2)}) collective-permute-start(bf16[16,4096]{1,0:T(8,128)(2,1)S(1)} %get-tuple-element.43), channel_id=1, source_target_pairs={{0,4},{1,5},{2,6},{3,7},{4,0},{5,1},{6,2},{7,3},{8,12},{9,13},{10,... | collective-permute-start | bytes 393224 | tf_op jit(solution)/shard_map/ppermute | solution.py:17
  45.1 7.4 %collective-permute-start.4 = (bf16[16,4096]{1,0:T(8,128)(2,1)S(1)}, bf16[16,4096]{1,0:T(8,128)(2,1)S(1)}, u32[]{:S(2)}, u32[]{:S(2)}) collective-permute-start(bf16[16,4096]{1,0:T(8,128)(2,1)S(1)} %get-tuple-element.44), channel_id=1, source_target_pairs={{0,6},{1,7},{2,4},{3,5},{4,2},{5,3},{6,0},{7,1},{8,14},{9,15},{10,... | collective-permute-start | bytes 393224 | tf_op jit(solution)/shard_map/ppermute | solution.py:17
  50.1 6.4 %collective-permute-start.19 = (bf16[16,4096]{1,0:T(8,128)(2,1)S(1)}, bf16[16,4096]{1,0:T(8,128)(2,1)S(1)}, u32[]{:S(2)}, u32[]{:S(2)}) collective-permute-start(bf16[16,4096]{1,0:T(8,128)(2,1)S(1)} %get-tuple-element.64), channel_id=1, source_target_pairs={{0,2},{1,3},{2,0},{3,1},{4,6},{5,7},{6,4},{7,5},{8,10},{9,11},{10,... | collective-permute-start | bytes 393224 | tf_op jit(solution)/shard_map/ppermute | solution.py:17
  52.4 25.6 %collective-permute-start.12 = (bf16[32,4096]{1,0:T(8,128)(2,1)S(1)}, bf16[32,4096]{1,0:T(8,128)(2,1)S(1)}, u32[]{:S(2)}, u32[]{:S(2)}) collective-permute-start(bf16[32,4096]{1,0:T(8,128)(2,1)S(1)} %get-tuple-element.54), channel_id=1, source_target_pairs={{0,2},{1,3},{2,0},{3,1},{4,6},{5,7},{6,4},{7,5},{8,10},{9,11},{10,... | collective-permute-start | bytes 786440 | tf_op jit(solution)/shard_map/ppermute | solution.py:17
  56.5 24.3 %collective-permute-start.13 = (bf16[32,4096]{1,0:T(8,128)(2,1)S(1)}, bf16[32,4096]{1,0:T(8,128)(2,1)S(1)}, u32[]{:S(2)}, u32[]{:S(2)}) collective-permute-start(bf16[32,4096]{1,0:T(8,128)(2,1)S(1)} %get-tuple-element.55), channel_id=1, source_target_pairs={{0,4},{1,5},{2,6},{3,7},{4,0},{5,1},{6,2},{7,3},{8,12},{9,13},{10,... | collective-permute-start | bytes 786440 | tf_op jit(solution)/shard_map/ppermute | solution.py:17
  56.5 25.0 %collective-permute-start.14 = (bf16[32,4096]{1,0:T(8,128)(2,1)S(1)}, bf16[32,4096]{1,0:T(8,128)(2,1)S(1)}, u32[]{:S(2)}, u32[]{:S(2)}) collective-permute-start(bf16[32,4096]{1,0:T(8,128)(2,1)S(1)} %get-tuple-element.56), channel_id=1, source_target_pairs={{0,6},{1,7},{2,4},{3,5},{4,2},{5,3},{6,0},{7,1},{8,14},{9,15},{10,... | collective-permute-start | bytes 786440 | tf_op jit(solution)/shard_map/ppermute | solution.py:17
  59.4 11.7 %collective-permute-start.20 = (bf16[16,4096]{1,0:T(8,128)(2,1)S(1)}, bf16[16,4096]{1,0:T(8,128)(2,1)S(1)}, u32[]{:S(2)}, u32[]{:S(2)}) collective-permute-start(bf16[16,4096]{1,0:T(8,128)(2,1)S(1)} %get-tuple-element.65), channel_id=1, source_target_pairs={{0,4},{1,5},{2,6},{3,7},{4,0},{5,1},{6,2},{7,3},{8,12},{9,13},{10,... | collective-permute-start | bytes 393224 | tf_op jit(solution)/shard_map/ppermute | solution.py:17
  59.7 14.1 %collective-permute-start.21 = (bf16[16,4096]{1,0:T(8,128)(2,1)S(1)}, bf16[16,4096]{1,0:T(8,128)(2,1)S(1)}, u32[]{:S(2)}, u32[]{:S(2)}) collective-permute-start(bf16[16,4096]{1,0:T(8,128)(2,1)S(1)} %get-tuple-element.66), channel_id=1, source_target_pairs={{0,6},{1,7},{2,4},{3,5},{4,2},{5,3},{6,0},{7,1},{8,14},{9,15},{10,... | collective-permute-start | bytes 393224 | tf_op jit(solution)/shard_map/ppermute | solution.py:17
  61.5 1.9 %copy-start.1 = (bf16[4096,384]{1,0:T(8,128)(2,1)S(1)}, bf16[4096,384]{1,0:T(8,128)(2,1)}, u32[]{:S(2)}) copy-start(bf16[4096,384]{1,0:T(8,128)(2,1)} %refs_5_.9) | copy-start | bytes 9437188
  63.4 1.9 %copy-start.2 = (bf16[384,4096]{1,0:T(8,128)(2,1)S(1)}, bf16[384,4096]{1,0:T(8,128)(2,1)}, u32[]{:S(2)}) copy-start(bf16[384,4096]{1,0:T(8,128)(2,1)} %refs_6_.9) | copy-start | bytes 9437188
  71.1 11.1 %collective-permute-start.8 = (bf16[16,4096]{1,0:T(8,128)(2,1)S(1)}, bf16[16,4096]{1,0:T(8,128)(2,1)S(1)}, u32[]{:S(2)}, u32[]{:S(2)}) collective-permute-start(bf16[16,4096]{1,0:T(8,128)(2,1)S(1)} %get-tuple-element.46), channel_id=1, source_target_pairs={{0,2},{1,3},{2,0},{3,1},{4,6},{5,7},{6,4},{7,5},{8,10},{9,11},{10,... | collective-permute-start | bytes 393224 | tf_op jit(solution)/shard_map/ppermute | solution.py:17
  73.7 14.4 %collective-permute-start.9 = (bf16[16,4096]{1,0:T(8,128)(2,1)S(1)}, bf16[16,4096]{1,0:T(8,128)(2,1)S(1)}, u32[]{:S(2)}, u32[]{:S(2)}) collective-permute-start(bf16[16,4096]{1,0:T(8,128)(2,1)S(1)} %get-tuple-element.47), channel_id=1, source_target_pairs={{0,4},{1,5},{2,6},{3,7},{4,0},{5,1},{6,2},{7,3},{8,12},{9,13},{10,... | collective-permute-start | bytes 393224 | tf_op jit(solution)/shard_map/ppermute | solution.py:17
  78.0 11.0 %collective-permute-start.10 = (bf16[16,4096]{1,0:T(8,128)(2,1)S(1)}, bf16[16,4096]{1,0:T(8,128)(2,1)S(1)}, u32[]{:S(2)}, u32[]{:S(2)}) collective-permute-start(bf16[16,4096]{1,0:T(8,128)(2,1)S(1)} %get-tuple-element.48), channel_id=1, source_target_pairs={{0,6},{1,7},{2,4},{3,5},{4,2},{5,3},{6,0},{7,1},{8,14},{9,15},{10,... | collective-permute-start | bytes 393224 | tf_op jit(solution)/shard_map/ppermute | solution.py:17
  80.8 9.4 %collective-permute-start.22 = (bf16[16,4096]{1,0:T(8,128)(2,1)S(1)}, bf16[16,4096]{1,0:T(8,128)(2,1)S(1)}, u32[]{:S(2)}, u32[]{:S(2)}) collective-permute-start(bf16[16,4096]{1,0:T(8,128)(2,1)S(1)} %get-tuple-element.68), channel_id=1, source_target_pairs={{0,2},{1,3},{2,0},{3,1},{4,6},{5,7},{6,4},{7,5},{8,10},{9,11},{10,... | collective-permute-start | bytes 393224 | tf_op jit(solution)/shard_map/ppermute | solution.py:17
  81.6 10.7 %collective-permute-start.23 = (bf16[16,4096]{1,0:T(8,128)(2,1)S(1)}, bf16[16,4096]{1,0:T(8,128)(2,1)S(1)}, u32[]{:S(2)}, u32[]{:S(2)}) collective-permute-start(bf16[16,4096]{1,0:T(8,128)(2,1)S(1)} %get-tuple-element.69), channel_id=1, source_target_pairs={{0,4},{1,5},{2,6},{3,7},{4,0},{5,1},{6,2},{7,3},{8,12},{9,13},{10,... | collective-permute-start | bytes 393224 | tf_op jit(solution)/shard_map/ppermute | solution.py:17
  82.2 13.3 %collective-permute-start.24 = (bf16[16,4096]{1,0:T(8,128)(2,1)S(1)}, bf16[16,4096]{1,0:T(8,128)(2,1)S(1)}, u32[]{:S(2)}, u32[]{:S(2)}) collective-permute-start(bf16[16,4096]{1,0:T(8,128)(2,1)S(1)} %get-tuple-element.70), channel_id=1, source_target_pairs={{0,6},{1,7},{2,4},{3,5},{4,2},{5,3},{6,0},{7,1},{8,14},{9,15},{10,... | collective-permute-start | bytes 393224 | tf_op jit(solution)/shard_map/ppermute | solution.py:17
  88.2 8.1 %collective-permute-start.15 = (bf16[32,4096]{1,0:T(8,128)(2,1)S(1)}, bf16[32,4096]{1,0:T(8,128)(2,1)S(1)}, u32[]{:S(2)}, u32[]{:S(2)}) collective-permute-start(bf16[32,4096]{1,0:T(8,128)(2,1)S(1)} %get-tuple-element.58), channel_id=1, source_target_pairs={{0,2},{1,3},{2,0},{3,1},{4,6},{5,7},{6,4},{7,5},{8,10},{9,11},{10,... | collective-permute-start | bytes 786440 | tf_op jit(solution)/shard_map/ppermute | solution.py:17
  89.0 16.7 %collective-permute-start.16 = (bf16[32,4096]{1,0:T(8,128)(2,1)S(1)}, bf16[32,4096]{1,0:T(8,128)(2,1)S(1)}, u32[]{:S(2)}, u32[]{:S(2)}) collective-permute-start(bf16[32,4096]{1,0:T(8,128)(2,1)S(1)} %get-tuple-element.59), channel_id=1, source_target_pairs={{0,4},{1,5},{2,6},{3,7},{4,0},{5,1},{6,2},{7,3},{8,12},{9,13},{10,... | collective-permute-start | bytes 786440 | tf_op jit(solution)/shard_map/ppermute | solution.py:17
  90.2 20.3 %collective-permute-start.17 = (bf16[32,4096]{1,0:T(8,128)(2,1)S(1)}, bf16[32,4096]{1,0:T(8,128)(2,1)S(1)}, u32[]{:S(2)}, u32[]{:S(2)}) collective-permute-start(bf16[32,4096]{1,0:T(8,128)(2,1)S(1)} %get-tuple-element.60), channel_id=1, source_target_pairs={{0,6},{1,7},{2,4},{3,5},{4,2},{5,3},{6,0},{7,1},{8,14},{9,15},{10,... | collective-permute-start | bytes 786440 | tf_op jit(solution)/shard_map/ppermute | solution.py:17
  92.3 18.1 %collective-permute-start.11 = (bf16[32,4096]{1,0:T(8,128)(2,1)S(1)}, bf16[32,4096]{1,0:T(8,128)(2,1)S(1)}, u32[]{:S(2)}, u32[]{:S(2)}) collective-permute-start(bf16[32,4096]{1,0:T(8,128)(2,1)S(1)} %relay_back.2), channel_id=1, source_target_pairs={{0,8},{1,9},{2,10},{3,11},{4,12},{5,13},{6,14},{7,15},{8,0},{9,1},... | collective-permute-start | bytes 786440 | tf_op jit(solution)/shard_map/ppermute | solution.py:17
  96.2 18.1 %collective-permute-start.25 = (bf16[32,4096]{1,0:T(8,128)(2,1)S(1)}, bf16[32,4096]{1,0:T(8,128)(2,1)S(1)}, u32[]{:S(2)}, u32[]{:S(2)}) collective-permute-start(bf16[32,4096]{1,0:T(8,128)(2,1)S(1)} %relay_back.3), channel_id=1, source_target_pairs={{0,8},{1,9},{2,10},{3,11},{4,12},{5,13},{6,14},{7,15},{8,0},{9,1},... | collective-permute-start | bytes 786440 | tf_op jit(solution)/shard_map/ppermute | solution.py:17
  (8 other events, 5.9 us)

commit v3 on v2

--- a/solution.py
+++ b/solution.py
@@ -8,6 +8,7 @@
 from jax.sharding import PartitionSpec as P
 
 EPS = 1e-06
+ROUTE = 128
 MIB = 1 << 20
 VMEM = pltpu.VMEM
 SMEM = pltpu.SMEM
@@ -25,8 +26,12 @@
     return pltpu.CompilerParams(vmem_limit_bytes=mib * MIB)
 
 
-def cost(flops, moved):
-    return pl.CostEstimate(flops=int(flops), bytes_accessed=int(moved), transcendentals=0)
+def unread(arrays):
+    return [pl.BlockSpec(memory_space=pl.ANY)] * len(arrays)
+
+
+def taking(microseconds):
+    return pl.CostEstimate(flops=1, bytes_accessed=int(microseconds * 3.5e6), transcendentals=0)
 
 
 def slots_of(half, cap):
@@ -49,6 +54,36 @@
     ones = jnp.where(named, 1.0, 0.0)
     rank = jnp.dot(ones.astype(jnp.bfloat16), earlier, preferred_element_type=jnp.float32)
     return jnp.where(rank == slot, ones, 0.0)
+
+
+def route_lanes(top, width):
+    row = lax.broadcasted_iota(jnp.int32, (2 * top, width), 0)
+    lane = lax.broadcasted_iota(jnp.int32, (2 * top, width), 1)
+    apart = lane - row
+    gate = row >= top
+    later = jnp.logical_and(gate, jnp.logical_or(apart == top, apart == 2 * top))
+    return jnp.where(jnp.logical_or(apart == 0, later), 1.0, 0.0).astype(jnp.bfloat16)
+
+
+def pack_route(info, width):
+    top = info.shape[0] // 2
+    gates = info[top:, :]
+    high = gates.astype(jnp.bfloat16).astype(jnp.float32)
+    middle = (gates - high).astype(jnp.bfloat16).astype(jnp.float32)
+    low = gates - high - middle
+    parts = jnp.concatenate([info[:top, :], high, middle, low], axis=0).astype(jnp.bfloat16)
+    row = lax.broadcasted_iota(jnp.int32, (4 * top, width), 0)
+    lane = lax.broadcasted_iota(jnp.int32, (4 * top, width), 1)
+    place = jnp.where(row == lane, 1.0, 0.0).astype(jnp.bfloat16)
+    return lax.dot_general(parts, place, (((0,), (0,)), ((), ())), preferred_element_type=jnp.float32).astype(
+        jnp.bfloat16
+    )
+
+
+def unpack_route(lanes, top):
+    return lax.dot_general(
+        route_lanes(top, lanes.shape[1]), lanes, (((1,), (1,)), ((), ())), preferred_element_type=jnp.float32
+    )
 
 
 def spread_rows(info, rows_bf16, out_refs, cap):
@@ -100,7 +135,7 @@
     near_rows = cap * chunks if last else cap
     out_shape = [
         jax.ShapeDtypeStruct((rows, width), jnp.float32),
-        jax.ShapeDtypeStruct((rows, width), jnp.bfloat16),
+        jax.ShapeDtypeStruct((rows, width + ROUTE), jnp.bfloat16),
     ]
     out_shape += [jax.ShapeDtypeStruct((near_rows, width), jnp.bfloat16)] * half
     if first:
@@ -177,9 +212,11 @@
                 square = square + resid * resid
         scale = lax.rsqrt(jnp.sum(square, axis=-1, keepdims=True) / width + EPS)
         normed = (resid_ref[...] * scale * ng_ref[...]).astype(jnp.bfloat16)
-        normed_ref[...] = normed
+        route = info_ref[:, chunk * rows : (chunk + 1) * rows]
+        normed_ref[:, :width] = normed
+        normed_ref[:, width:] = pack_route(route, ROUTE)
         tail = slice(near_rows - cap, near_rows)
-        spread_rows(info_ref[:, chunk * rows : (chunk + 1) * rows], normed, [o.at[tail, :] for o in out_refs], cap)
+        spread_rows(route, normed, [o.at[tail, :] for o in out_refs], cap)
         for i in range(len(before)):
             out_refs[i][: near_rows - cap, :] = carried[i][...]
 
@@ -187,7 +224,7 @@
         body,
         out_shape=out_shape,
         in_specs=[pl.BlockSpec(memory_space=SMEM)]
-        + [pl.BlockSpec(memory_space=pl.ANY)] * 11
+        + [pl.BlockSpec(memory_space=pltpu.HBM)] * 11
         + [whole(b) for b in before],
         out_specs=[whole(o) for o in out_shape],
         scratch_shapes=[
@@ -209,46 +246,75 @@
             pltpu.SemaphoreType.DMA((11,)),
         ],
         compiler_params=params(24),
-        cost_estimate=cost(4 * rows * width * keys, 6 * MIB),
+        cost_estimate=taking(4),
         name="attend",
     )(cache_len, *arrays, *before)
     return results[0], results[1], list(results[2 : 2 + half]), (results[-1] if first else None)
 
 
-def relay(rows_in, info, chunk, half, cap):
-    rows, width = rows_in.shape
-    out = jax.ShapeDtypeStruct((cap, width), jnp.bfloat16)
-
-    def body(rows_ref, info_ref, *out_refs):
-        spread_rows(info_ref[:, chunk * rows : (chunk + 1) * rows], rows_ref[...], out_refs, cap)
+def relay(rows_in, top, half, cap, carried, after):
+    width = rows_in.shape[1] - ROUTE
+    out = [jax.ShapeDtypeStruct((cap, width), jnp.bfloat16)] * half
+    out += [jax.ShapeDtypeStruct(x.shape, x.dtype) for x in carried]
+
+    def body(rows_ref, *refs):
+        outs = refs[len(carried) + len(after) :]
+        spread_rows(unpack_route(rows_ref[:, width:], top), rows_ref[:, :width], outs[:half], cap)
+        for i in range(len(carried)):
+            outs[half + i][...] = refs[i][...]
+
+    results = pl.pallas_call(
+        body,
+        out_shape=out,
+        in_specs=[whole(rows_in)] + [whole(x) for x in carried] + unread(after),
+        out_specs=[whole(o) for o in out],
+        compiler_params=params(24),
+        cost_estimate=taking(0.5),
+        name="relay",
+    )(rows_in, *carried, *after)
+    return list(results[:half]), list(results[half:])
+
+
+def arrange(arrays, plan, after):
+    width = arrays[0].shape[1]
+    out = [jax.ShapeDtypeStruct((sum(piece[2] for piece in pieces), width), arrays[0].dtype) for pieces in plan]
+
+    def body(*refs):
+        outs = refs[len(arrays) + len(after) :]
+        for out_ref, pieces in zip(outs, plan):
+            at = 0
+            for index, start, count in pieces:
+                out_ref[at : at + count, :] = refs[index][start : start + count, :]
+                at += count
 
     return list(
         pl.pallas_call(
             body,
-            out_shape=[out] * half,
-            in_specs=[whole(rows_in), whole(info)],
-            out_specs=[whole(out)] * half,
+            out_shape=out,
+            in_specs=[whole(x) for x in arrays] + unread(after),
+            out_specs=[whole(x) for x in out],
             compiler_params=params(24),
-            cost_estimate=cost(2 * half * cap * rows * width, MIB),
-            name="relay",
-        )(rows_in, info)
-    )
-
-
-def expert(own, weights):
-    cap, width = own[0].shape
-    count = len(own)
+            cost_estimate=taking(0.3),
+            name="arrange",
+        )(*arrays, *after)
+    )
+
+
+def expert(ins, weights, outs, after, microseconds):
+    rows, width = ins[0].shape
+    total = len(ins) * rows
     hidden = weights[0].shape[1]
-    total = count * cap
     block = min(total, 128)
     part = 512
-    out = jax.ShapeDtypeStruct((cap, width), jnp.bfloat16)
+    back = total // outs
+    out = [jax.ShapeDtypeStruct((back, width), jnp.bfloat16)] * outs
 
     def body(*refs):
-        ins, (wg0, wu0, wd0, wg1, wu1, wd1) = refs[:count], refs[count : count + 6]
-        outs, (x_ref, y_ref) = refs[count + 6 : 2 * count + 6], refs[2 * count + 6 :]
-        for i in range(count):
-            x_ref[i * cap : (i + 1) * cap, :] = ins[i][...]
+        in_refs, refs = refs[: len(ins)], refs[len(ins) :]
+        (wg0, wu0, wd0, wg1, wu1, wd1), refs = refs[:6], refs[6 + len(after) :]
+        out_refs, (x_ref, y_ref) = refs[:outs], refs[outs:]
+        for i in range(len(ins)):
+            x_ref[i * rows : (i + 1) * rows, :] = in_refs[i][...]
 
         def rows_of(span):
             inners = []
@@ -274,86 +340,79 @@
             def _(r):
                 rows_of(pl.ds(pl.multiple_of(r * block, block), block))
 
-        for i in range(count):
-            outs[i][...] = y_ref[i * cap : (i + 1) * cap, :]
+        for i in range(outs):
+            out_refs[i][...] = y_ref[i * back : (i + 1) * back, :]
 
     return list(
         pl.pallas_call(
             body,
-            out_shape=[out] * count,
-            in_specs=[whole(own[0])] * count + [whole(w) for w in weights],
-            out_specs=[whole(out)] * count,
+            out_shape=out,
+            in_specs=[whole(x) for x in ins] + [whole(w) for w in weights] + unread(after),
+            out_specs=[whole(o) for o in out],
             scratch_shapes=[VMEM((total, width), jnp.bfloat16)] * 2,
             compiler_params=params(24),
-            cost_estimate=cost(12 * total * width * hidden, 12 * width * hidden),
+            cost_estimate=taking(microseconds),
             name="expert",
-        )(*own, *weights)
-    )
-
-
-def relay_back(returned, info, chunk, rows, cap):
+        )(*ins, *weights, *after)
+    )
+
+
+def relay_back(returned, rows_in, top, cap, after):
     half = len(returned)
-    width = returned[0].shape[1]
+    rows, width = rows_in.shape[0], returned[0].shape[1]
     out = jax.ShapeDtypeStruct((rows, width), jnp.bfloat16)
 
-    def body(info_ref, *refs):
-        in_refs, out_ref, joined = refs[:half], refs[half], refs[half + 1]
+    def body(rows_ref, *refs):
+        in_refs, (out_ref, joined) = refs[:half], refs[half + len(after) :]
         for d in range(half):
             joined[d * cap : (d + 1) * cap, :] = in_refs[d][...]
-        far = weighted_rows(info_ref[:, chunk * rows : (chunk + 1) * rows], half, joined, cap)
+        far = weighted_rows(unpack_route(rows_ref[:, width:], top), half, joined, cap)
         out_ref[...] = far.astype(jnp.bfloat16)
 
     return pl.pallas_call(
         body,
         out_shape=out,
-        in_specs=[whole(info)] + [whole(returned[0])] * half,
+        in_specs=[whole(rows_in)] + [whole(returned[0])] * half + unread(after),
         out_specs=whole(out),
         scratch_shapes=[VMEM((half * cap, width), jnp.bfloat16)],
         compiler_params=params(24),
-        cost_estimate=cost(4 * half * cap * rows * width, MIB),
+        cost_estimate=taking(0.6),
         name="relay_back",
-    )(info, *returned)
-
-
-def finish(resid, returned, far, info, chunk, chunks, cap, previous):
+    )(rows_in, *returned, *after)
+
+
+def finish(resid, far, returned, info, cap):
     half = len(returned)
-    rows, width = resid.shape
+    chunks = len(resid)
+    rows, width = resid[0].shape
     out = jax.ShapeDtypeStruct((rows * chunks, width), jnp.bfloat16)
-    extra = [] if previous is None else [previous]
-
-    def body(*refs):
-        info_ref, resid_ref, far_ref = refs[len(extra) : len(extra) + 3]
-        refs = refs[len(extra) + 3 :]
-        in_refs, out_hbm, joined, out_ref, sem = refs[:half], *refs[half:]
-        for d in range(half):
-            joined[d * cap : (d + 1) * cap, :] = in_refs[d][chunk * cap : (chunk + 1) * cap, :]
-        near = weighted_rows(info_ref[:, chunk * rows : (chunk + 1) * rows], half, joined, cap)
-        out_ref[...] = (resid_ref[...] + (near + far_ref[...].astype(jnp.float32))).astype(jnp.bfloat16)
-        copy = pltpu.make_async_copy(out_ref, out_hbm.at[pl.ds(chunk * rows, rows), :], sem)
-        copy.start()
-        copy.wait()
+
+    def body(info_ref, *refs):
+        resid_refs, far_refs, refs = refs[:chunks], refs[chunks : 2 * chunks], refs[2 * chunks :]
+        in_refs, (out_ref, joined) = refs[:half], refs[half:]
+        for c in range(chunks):
+            for d in range(half):
+                joined[d * cap : (d + 1) * cap, :] = in_refs[d][c * cap : (c + 1) * cap, :]
+            near = weighted_rows(info_ref[:, c * rows : (c + 1) * rows], half, joined, cap)
+            out_ref[c * rows : (c + 1) * rows, :] = (
+                resid_refs[c][...] + (near + far_refs[c][...].astype(jnp.float32))
+            ).astype(jnp.bfloat16)
 
     return pl.pallas_call(
         body,
         out_shape=out,
-        in_specs=[pl.BlockSpec(memory_space=pl.ANY)] * len(extra)
-        + [whole(info), whole(resid), whole(far)]
-        + [whole(returned[0])] * half,
-        out_specs=pl.BlockSpec(memory_space=pl.ANY),
-        scratch_shapes=[
-            VMEM((half * cap, width), jnp.bfloat16),
-            VMEM((rows, width), jnp.bfloat16),
-            pltpu.SemaphoreType.DMA,
-        ],
-        input_output_aliases={0: 0} if extra else {},
+        in_specs=[whole(x) for x in (info, *resid, *far, *returned)],
+        out_specs=whole(out),
+        scratch_shapes=[VMEM((half * cap, width), jnp.bfloat16)],
         compiler_params=params(24),
-        cost_estimate=cost(4 * half * cap * rows * width, 2 * MIB),
+        cost_estimate=taking(2),
         name="finish",
-    )(*extra, info, resid, far, *returned)
+    )(info, *resid, *far, *returned)
 
 
 def around(parts):
-    return [parts[0]] + [exchange(parts[d], 2 * d) for d in range(1, len(parts))]
+    moved = {d: exchange(parts[d], 2 * d) for d in reversed(range(1, len(parts)))}
+    return [parts[0]] + [moved[d] for d in range(1, len(parts))]
 
 
 def local(
@@ -394,26 +453,36 @@
         expert_ids.T,
         gate_weights.T,
     )
+    arrays = tuple(pltpu.with_memory_space_constraint(x, pltpu.HBM) for x in arrays)
     weights = (w_gate, w_up, w_down)
     weights = weights + tuple(exchange(w, 1) for w in weights)
 
-    resid, far_rows, outgoing, info = [], [], [], None
+    resid, normed, outgoing, info = [], [], [], None
     for c in range(chunks):
-        residual, normed, outgoing, packed = attend(cache_len, arrays, outgoing, c, chunks, half, cap)
+        residual, rows_c, outgoing, packed = attend(cache_len, arrays, outgoing, c, chunks, half, cap)
         info = packed if c == 0 else info
         resid.append(residual)
-        far_rows.append(exchange(normed, ep // 2))
-    far_info = exchange(info, ep // 2)
-    near_back = around(expert(around(outgoing), weights))
-    far_back = []
+        normed.append(rows_c)
+    far_rows = [exchange(x, ep // 2) for x in normed]
+    near = around(arrange(outgoing, [[(d, 0, slots)] for d in range(half)], list(weights[3:])))
+    placed = [around(relay(far_rows[0], top, half, cap, [], [])[0])]
+    after = near[1:]
+    for c in range(1, chunks):
+        arrived, _ = relay(far_rows[c], top, half, cap, [], after)
+        placed.append(around(arrived))
+        after = [arrived[0]]
+    near_out = expert(near, weights, half, after, 4)
+    after = near_out[0]
+    returned, far_back = [], []
     for c in range(chunks):
-        placed = around(relay(far_rows[c], far_info, c, half, cap))
-        returned = around(expert(placed, weights))
-        far_back.append(exchange(relay_back(returned, far_info, c, rows, cap), ep // 2))
-    result = None
+        far_out = expert(placed[c], weights, half, [after], 0.01)
+        returned.append(around(far_out))
+        after = far_out[0]
     for c in range(chunks):
-        result = finish(resid[c], near_back, far_back[c], info, c, chunks, cap, result)
-    return result
+        back = relay_back(returned[c], far_rows[c], top, cap, [after] + far_back)
+        far_back.append(exchange(back, ep // 2))
+        after = back
+    return finish(resid, far_back, around(near_out), info, cap)
 
 
 def solution(mesh):

time: 116 us -> 97.8 us (0.84)
  local copies, waits for them, and re-layouts: 12.8 us -> 0.01 us
  waiting for transfers between devices: 44.5 us -> 37.4 us
  starting transfers between devices: 33.1 us -> 34.3 us
    unnamed x28 -> x6, local copies, waits for them, and re-layouts: 12.8 us -> 0.01 us
    ppermute x26 -> x25, waiting for transfers between devices: 44.5 us -> 37.4 us  [exchange(): lax.ppermute(value, 'ep', [(i, i ^ distance) for i in range(lax.axis_size...]
    ppermute x26 -> x25, starting transfers between devices: 33.1 us -> 34.3 us  [exchange(): lax.ppermute(value, 'ep', [(i, i ^ distance) for i in range(lax.axis_size...]
    pallas_call x2, Pallas kernels: 7.45 us -> 8.68 us  [attend(): pl.pallas_call(body, out_shape=out_shape, in_specs=[pl.BlockSpec(memory_s...]
  transfers between devices with their start and end apart: 26 -> 25, of which waited for: 11 -> 10; matrix products, arithmetic and copies ran while one was open for 0% -> 0% of each run, Pallas kernels for 20% -> 23%
where the time goes in v3:
time: 97.8 us; the launch traced here: 97.7 us
  waiting for transfers between devices  37.4 us (38%)
  starting transfers between devices  34.3 us (35%)
  Pallas kernels  25.1 us (26%)
    ppermute x25, waiting for transfers between devices, exchange(): lax.ppermute(value, 'ep', [(i, i ^ distance) for i in range(lax.axis_size...  37.4 us
    ppermute x25, starting transfers between devices, exchange(): lax.ppermute(value, 'ep', [(i, i ^ distance) for i in range(lax.axis_size...  34.3 us
    pallas_call x3, Pallas kernels, expert(): pl.pallas_call(body, out_shape=out, in_specs=[whole(x) for x in ins] + [w...  12.5 us
    pallas_call x2, Pallas kernels, attend(): pl.pallas_call(body, out_shape=out_shape, in_specs=[pl.BlockSpec(memory_s...  8.68 us
  transfers between devices with their start and end apart: 25, of which 10 were waited for; matrix products, arithmetic and copies ran while one was open for 0% of the time, Pallas kernels for 23%

profile of v3, /device:TPU:0, one launch (start us, length us, event | category | flops | bytes accessed | tf_op | source)
XLA Modules:
  0.0 97.7 jit_solution(6966109528265272422)
XLA Ops:
  1.6 4.3 %attend.2 = (f32[32,4096]{1,0:T(8,128)S(1)}, bf16[32,4224]{1,0:T(8,128)(2,1)S(1)}, bf16[16,4096]{1,0:T(8,128)(2,1)S(1)}, bf16[16,4096]{1,0:T(8,128)(2,1)S(1)}, b...) custom-call(s32[1]{0:T(128)S(6)} %copy.16.len_ref, bf16[64,4096]{1,0:T(8,128)(2,1)} %refs_0_.3, ...), custom_call_target="tpu_custom_call" | custom-call | flops 1 | bytes 14000000 | tf_op jit(solution)/shard_map/attend/pallas_call | solution.py:223
  6.0 3.7 %collective-permute-start = (bf16[32,4224]{1,0:T(8,128)(2,1)S(1)}, bf16[32,4224]{1,0:T(8,128)(2,1)S(1)}, u32[]{:S(2)}, u32[]{:S(2)}) collective-permute-start(bf16[32,4224]{1,0:T(8,128)(2,1)S(1)} %get-tuple-element.49), channel_id=1, source_target_pairs={{0,8},{1,9},{2,10},{3,11},{4,12},{5,13},{6,14},{7,15},{8,0},{9,1},... | collective-permute-start | bytes 811016 | tf_op jit(solution)/shard_map/ppermute | solution.py:18
  9.6 4.3 %attend.3 = (f32[32,4096]{1,0:T(8,128)S(1)}, bf16[32,4224]{1,0:T(8,128)(2,1)S(1)}, bf16[32,4096]{1,0:T(8,128)(2,1)S(1)}, bf16[32,4096]{1,0:T(8,128)(2,1)S(1)}, b...) custom-call(s32[1]{0:T(128)S(6)} %copy.16.len_ref, bf16[64,4096]{1,0:T(8,128)(2,1)} %refs_0_.3, ...), custom_call_target="tpu_custom_call" | custom-call | flops 1 | bytes 14000000 | tf_op jit(solution)/shard_map/attend/pallas_call | solution.py:223
  14.1 0.9 collective-permute-done.6.refs_6_.refs_9_
  15.0 3.0 %collective-permute-start.7 = (bf16[32,4096]{1,0:T(8,128)(2,1)S(1)}, bf16[32,4096]{1,0:T(8,128)(2,1)S(1)}, u32[]{:S(2)}, u32[]{:S(2)}) collective-permute-start(bf16[32,4096]{1,0:T(8,128)(2,1)S(1)} %get-tuple-element.59), channel_id=1, source_target_pairs={{0,2},{1,3},{2,0},{3,1},{4,6},{5,7},{6,4},{7,5},{8,10},{9,11},{10,... | collective-permute-start | bytes 786440 | tf_op jit(solution)/shard_map/ppermute | solution.py:18
  18.0 1.6 %collective-permute-start.8 = (bf16[32,4096]{1,0:T(8,128)(2,1)S(1)}, bf16[32,4096]{1,0:T(8,128)(2,1)S(1)}, u32[]{:S(2)}, u32[]{:S(2)}) collective-permute-start(bf16[32,4096]{1,0:T(8,128)(2,1)S(1)} %get-tuple-element.60), channel_id=1, source_target_pairs={{0,4},{1,5},{2,6},{3,7},{4,0},{5,1},{6,2},{7,3},{8,12},{9,13},{10,... | collective-permute-start | bytes 786440 | tf_op jit(solution)/shard_map/ppermute | solution.py:18
  19.6 9.1 %collective-permute-done.rows_ref = bf16[32,4224]{1,0:T(8,128)(2,1)S(1)} collective-permute-done((bf16[32,4224]{1,0:T(8,128)(2,1)S(1)}, bf16[32,4224]{1,0:T(8,128)(2,1)S(1)}, u32[]{:S(2)}, u32[]{:S(2)}) %collective-permute-start) | collective-permute-done | bytes 270368 | tf_op jit(solution)/shard_map/ppermute | solution.py:18
  29.1 1.8 %collective-permute-start.1 = (bf16[16,4096]{1,0:T(8,128)(2,1)S(1)}, bf16[16,4096]{1,0:T(8,128)(2,1)S(1)}, u32[]{:S(2)}, u32[]{:S(2)}) collective-permute-start(bf16[16,4096]{1,0:T(8,128)(2,1)S(1)} %get-tuple-element.51), channel_id=1, source_target_pairs={{0,2},{1,3},{2,0},{3,1},{4,6},{5,7},{6,4},{7,5},{8,10},{9,11},{10,... | collective-permute-start | bytes 393224 | tf_op jit(solution)/shard_map/ppermute | solution.py:18
  31.0 3.3 %collective-permute-done.10.rows_ref = bf16[32,4224]{1,0:T(8,128)(2,1)S(1)} collective-permute-done((bf16[32,4224]{1,0:T(8,128)(2,1)S(1)}, bf16[32,4224]{1,0:T(8,128)(2,1)S(1)}, u32[]{:S(2)}, u32[]{:S(2)}) %collective-permute-start.10) | collective-permute-done | bytes 270368 | tf_op jit(solution)/shard_map/ppermute | solution.py:18
  34.2 0.7 collective-permute-start.2
  34.9 2.3 %collective-permute-start.3 = (bf16[16,4096]{1,0:T(8,128)(2,1)S(1)}, bf16[16,4096]{1,0:T(8,128)(2,1)S(1)}, u32[]{:S(2)}, u32[]{:S(2)}) collective-permute-start(bf16[16,4096]{1,0:T(8,128)(2,1)S(1)} %get-tuple-element.53), channel_id=1, source_target_pairs={{0,6},{1,7},{2,4},{3,5},{4,2},{5,3},{6,0},{7,1},{8,14},{9,15},{10,... | collective-permute-start | bytes 393224 | tf_op jit(solution)/shard_map/ppermute | solution.py:18
  37.3 4.5 %collective-permute-done.9.refs_2_.refs_3_ = bf16[32,4096]{1,0:T(8,128)(2,1)S(1)} collective-permute-done((bf16[32,4096]{1,0:T(8,128)(2,1)S(1)}, bf16[32,4096]{1,0:T(8,128)(2,1)S(1)}, u32[]{:S(2)}, u32[]{:S(2)}) %collective-permute-start.9) | collective-permute-done | bytes 262176 | tf_op jit(solution)/shard_map/ppermute | solution.py:18
  42.3 2.0 %collective-permute-start.14 = (bf16[16,4096]{1,0:T(8,128)(2,1)S(1)}, bf16[16,4096]{1,0:T(8,128)(2,1)S(1)}, u32[]{:S(2)}, u32[]{:S(2)}) collective-permute-start(bf16[16,4096]{1,0:T(8,128)(2,1)S(1)} %get-tuple-element.69), channel_id=1, source_target_pairs={{0,2},{1,3},{2,0},{3,1},{4,6},{5,7},{6,4},{7,5},{8,10},{9,11},{10,... | collective-permute-start | bytes 393224 | tf_op jit(solution)/shard_map/ppermute | solution.py:18
  44.3 3.8 %expert.3 = (bf16[32,4096]{1,0:T(8,128)(2,1)S(1)}, bf16[32,4096]{1,0:T(8,128)(2,1)S(1)}, bf16[32,4096]{1,0:T(8,128)(2,1)S(1)}, bf16[32,4096]{1,0:T(8,128)(2,1)S(1)}) custom-call(bf16[32,4096]{1,0:T(8,128)(2,1)S(1)} %get-tuple-element.58.refs_0_, bf16[32,4096]{1,0:T(8,128)(2,1)S(1)} %collective-permute-done.7.refs_0_.refs_1_, ...), custom_call_target="tpu_custom_call" | custom-call | flops 1 | bytes 14000000 | tf_op jit(solution)/shard_map/expert/pallas_call | solution.py:347
  48.1 1.6 %collective-permute-start.16 = (bf16[16,4096]{1,0:T(8,128)(2,1)S(1)}, bf16[16,4096]{1,0:T(8,128)(2,1)S(1)}, u32[]{:S(2)}, u32[]{:S(2)}) collective-permute-start(bf16[16,4096]{1,0:T(8,128)(2,1)S(1)} %get-tuple-element.71), channel_id=1, source_target_pairs={{0,6},{1,7},{2,4},{3,5},{4,2},{5,3},{6,0},{7,1},{8,14},{9,15},{10,... | collective-permute-start | bytes 393224 | tf_op jit(solution)/shard_map/ppermute | solution.py:18
  49.7 4.4 %expert.4 = (bf16[16,4096]{1,0:T(8,128)(2,1)S(1)}, bf16[16,4096]{1,0:T(8,128)(2,1)S(1)}, bf16[16,4096]{1,0:T(8,128)(2,1)S(1)}, bf16[16,4096]{1,0:T(8,128)(2,1)S(1)}) custom-call(bf16[16,4096]{1,0:T(8,128)(2,1)S(1)} %get-tuple-element.50.refs_0_, bf16[16,4096]{1,0:T(8,128)(2,1)S(1)} %collective-permute-done.1.refs_1_, ...), custom_call_target="tpu_custom_call" | custom-call | flops 1 | bytes 35000 | tf_op jit(solution)/shard_map/expert/pallas_call | solution.py:347
  54.2 2.0 %collective-permute-start.11 = (bf16[16,4096]{1,0:T(8,128)(2,1)S(1)}, bf16[16,4096]{1,0:T(8,128)(2,1)S(1)}, u32[]{:S(2)}, u32[]{:S(2)}) collective-permute-start(bf16[16,4096]{1,0:T(8,128)(2,1)S(1)} %get-tuple-element.66), channel_id=1, source_target_pairs={{0,2},{1,3},{2,0},{3,1},{4,6},{5,7},{6,4},{7,5},{8,10},{9,11},{10,... | collective-permute-start | bytes 393224 | tf_op jit(solution)/shard_map/ppermute | solution.py:18
  56.2 1.5 %collective-permute-start.13 = (bf16[16,4096]{1,0:T(8,128)(2,1)S(1)}, bf16[16,4096]{1,0:T(8,128)(2,1)S(1)}, u32[]{:S(2)}, u32[]{:S(2)}) collective-permute-start(bf16[16,4096]{1,0:T(8,128)(2,1)S(1)} %get-tuple-element.68), channel_id=1, source_target_pairs={{0,6},{1,7},{2,4},{3,5},{4,2},{5,3},{6,0},{7,1},{8,14},{9,15},{10,... | collective-permute-start | bytes 393224 | tf_op jit(solution)/shard_map/ppermute | solution.py:18
  57.7 4.3 %expert.5 = (bf16[16,4096]{1,0:T(8,128)(2,1)S(1)}, bf16[16,4096]{1,0:T(8,128)(2,1)S(1)}, bf16[16,4096]{1,0:T(8,128)(2,1)S(1)}, bf16[16,4096]{1,0:T(8,128)(2,1)S(1)}) custom-call(bf16[16,4096]{1,0:T(8,128)(2,1)S(1)} %get-tuple-element.63.refs_10_.refs_0_, bf16[16,4096]{1,0:T(8,128)(2,1)S(1)} %collective-permute-done.14.refs_1_, ...), custom_call_target="tpu_custom_call" | custom-call | flops 1 | bytes 35000 | tf_op jit(solution)/shard_map/expert/pallas_call | solution.py:347
  62.1 0.6 relay_back.2.refs_4_
  62.7 7.2 %collective-permute-start.17 = (bf16[32,4096]{1,0:T(8,128)(2,1)S(1)}, bf16[32,4096]{1,0:T(8,128)(2,1)S(1)}, u32[]{:S(2)}, u32[]{:S(2)}) collective-permute-start(bf16[32,4096]{1,0:T(8,128)(2,1)S(1)} %relay_back.2.refs_4_), channel_id=1, source_target_pairs={{0,8},{1,9},{2,10},{3,11},{4,12},{5,13},{6,14},{7,15},{8,0},{9,1},... | collective-permute-start | bytes 786440 | tf_op jit(solution)/shard_map/ppermute | solution.py:18
  70.9 2.5 %collective-permute-start.20 = (bf16[16,4096]{1,0:T(8,128)(2,1)S(1)}, bf16[16,4096]{1,0:T(8,128)(2,1)S(1)}, u32[]{:S(2)}, u32[]{:S(2)}) collective-permute-start(bf16[16,4096]{1,0:T(8,128)(2,1)S(1)} %get-tuple-element.75), channel_id=1, source_target_pairs={{0,6},{1,7},{2,4},{3,5},{4,2},{5,3},{6,0},{7,1},{8,14},{9,15},{10,... | collective-permute-start | bytes 393224 | tf_op jit(solution)/shard_map/ppermute | solution.py:18
  73.9 1.0 %collective-permute-done.18.refs_1_ = bf16[16,4096]{1,0:T(8,128)(2,1)S(1)} collective-permute-done((bf16[16,4096]{1,0:T(8,128)(2,1)S(1)}, bf16[16,4096]{1,0:T(8,128)(2,1)S(1)}, u32[]{:S(2)}, u32[]{:S(2)}) %collective-permute-start.18) | collective-permute-done | bytes 131104 | tf_op jit(solution)/shard_map/ppermute | solution.py:18
  74.9 1.1 %collective-permute-start.23 = (bf16[32,4096]{1,0:T(8,128)(2,1)S(1)}, bf16[32,4096]{1,0:T(8,128)(2,1)S(1)}, u32[]{:S(2)}, u32[]{:S(2)}) collective-permute-start(bf16[32,4096]{1,0:T(8,128)(2,1)S(1)} %get-tuple-element.77), channel_id=1, source_target_pairs={{0,4},{1,5},{2,6},{3,7},{4,0},{5,1},{6,2},{7,3},{8,12},{9,13},{10,... | collective-permute-start | bytes 786440 | tf_op jit(solution)/shard_map/ppermute | solution.py:18
  75.9 5.2 %collective-permute-done.19.refs_2_ = bf16[16,4096]{1,0:T(8,128)(2,1)S(1)} collective-permute-done((bf16[16,4096]{1,0:T(8,128)(2,1)S(1)}, bf16[16,4096]{1,0:T(8,128)(2,1)S(1)}, u32[]{:S(2)}, u32[]{:S(2)}) %collective-permute-start.19) | collective-permute-done | bytes 131104 | tf_op jit(solution)/shard_map/ppermute | solution.py:18
  81.2 0.7 collective-permute-start.24
  81.9 2.6 %collective-permute-done.20.refs_3_ = bf16[16,4096]{1,0:T(8,128)(2,1)S(1)} collective-permute-done((bf16[16,4096]{1,0:T(8,128)(2,1)S(1)}, bf16[16,4096]{1,0:T(8,128)(2,1)S(1)}, u32[]{:S(2)}, u32[]{:S(2)}) %collective-permute-start.20) | collective-permute-done | bytes 131104 | tf_op jit(solution)/shard_map/ppermute | solution.py:18
  84.4 0.6 relay_back.3
  85.1 3.3 %collective-permute-done.23.refs_6_ = bf16[32,4096]{1,0:T(8,128)(2,1)S(1)} collective-permute-done((bf16[32,4096]{1,0:T(8,128)(2,1)S(1)}, bf16[32,4096]{1,0:T(8,128)(2,1)S(1)}, u32[]{:S(2)}, u32[]{:S(2)}) %collective-permute-start.23) | collective-permute-done | bytes 262176 | tf_op jit(solution)/shard_map/ppermute | solution.py:18
  88.4 5.1 %collective-permute-done.24.refs_7_ = bf16[32,4096]{1,0:T(8,128)(2,1)S(1)} collective-permute-done((bf16[32,4096]{1,0:T(8,128)(2,1)S(1)}, bf16[32,4096]{1,0:T(8,128)(2,1)S(1)}, u32[]{:S(2)}, u32[]{:S(2)}) %collective-permute-start.24) | collective-permute-done | bytes 262176 | tf_op jit(solution)/shard_map/ppermute | solution.py:18
  93.5 2.5 %collective-permute-done.21.refs_3_ = bf16[32,4096]{1,0:T(8,128)(2,1)S(1)} collective-permute-done((bf16[32,4096]{1,0:T(8,128)(2,1)S(1)}, bf16[32,4096]{1,0:T(8,128)(2,1)S(1)}, u32[]{:S(2)}, u32[]{:S(2)}) %collective-permute-start.21) | collective-permute-done | bytes 262176 | tf_op jit(solution)/shard_map/ppermute | solution.py:18
  95.9 1.7 %finish.1 = bf16[64,4096]{1,0:T(8,128)(2,1)} custom-call(f32[4,64]{1,0:T(4,128)S(1)} %get-tuple-element.42.info_ref, f32[32,4096]{1,0:T(8,128)S(1)} %get-tuple-element.43.refs_0_, f32[32,4096]{1,0:T(8,128)S(1)} %get-tuple-element.48.refs_1_, bf16[32,4096]{1,0:T(8,128)(2,1)S(1)} %collective-permute-done.17.refs_5_.refs_2_, ...), custom_call_target="tpu_custom_call" | custom-call | flops 1 | bytes 7000000 | tf_op jit(solution)/shard_map/finish/pallas_call | solution.py:401
  (35 shorter events, 3.8 us)
Async XLA Ops:
  0.0 14.1 %collective-permute-start.4 = (bf16[4096,384]{1,0:T(8,128)(2,1)}, bf16[4096,384]{1,0:T(8,128)(2,1)S(1)}, u32[]{:S(2)}, u32[]{:S(2)}) collective-permute-start(bf16[4096,384]{1,0:T(8,128)(2,1)} %refs_4_.9), channel_id=1, source_target_pairs={{0,1},{1,0},{2,3},{3,2},{4,5},{5,4},{6,7},{7,6},{8,9},{9,8},{10,11... | collective-permute-start | bytes 9437192 | tf_op jit(solution)/shard_map/ppermute | solution.py:18
  0.5 13.6 %collective-permute-start.5 = (bf16[4096,384]{1,0:T(8,128)(2,1)}, bf16[4096,384]{1,0:T(8,128)(2,1)S(1)}, u32[]{:S(2)}, u32[]{:S(2)}) collective-permute-start(bf16[4096,384]{1,0:T(8,128)(2,1)} %refs_5_.9), channel_id=1, source_target_pairs={{0,1},{1,0},{2,3},{3,2},{4,5},{5,4},{6,7},{7,6},{8,9},{9,8},{10,11... | collective-permute-start | bytes 9437192 | tf_op jit(solution)/shard_map/ppermute | solution.py:18
  0.5 14.4 %collective-permute-start.6 = (bf16[384,4096]{1,0:T(8,128)(2,1)}, bf16[384,4096]{1,0:T(8,128)(2,1)S(1)}, u32[]{:S(2)}, u32[]{:S(2)}) collective-permute-start(bf16[384,4096]{1,0:T(8,128)(2,1)} %refs_6_.9), channel_id=1, source_target_pairs={{0,1},{1,0},{2,3},{3,2},{4,5},{5,4},{6,7},{7,6},{8,9},{9,8},{10,11... | collective-permute-start | bytes 9437192 | tf_op jit(solution)/shard_map/ppermute | solution.py:18
  6.0 22.7 %collective-permute-start = (bf16[32,4224]{1,0:T(8,128)(2,1)S(1)}, bf16[32,4224]{1,0:T(8,128)(2,1)S(1)}, u32[]{:S(2)}, u32[]{:S(2)}) collective-permute-start(bf16[32,4224]{1,0:T(8,128)(2,1)S(1)} %get-tuple-element.49), channel_id=1, source_target_pairs={{0,8},{1,9},{2,10},{3,11},{4,12},{5,13},{6,14},{7,15},{8,0},{9,1},... | collective-permute-start | bytes 811016 | tf_op jit(solution)/shard_map/ppermute | solution.py:18
  14.0 20.3 %collective-permute-start.10 = (bf16[32,4224]{1,0:T(8,128)(2,1)S(1)}, bf16[32,4224]{1,0:T(8,128)(2,1)S(1)}, u32[]{:S(2)}, u32[]{:S(2)}) collective-permute-start(bf16[32,4224]{1,0:T(8,128)(2,1)S(1)} %get-tuple-element.62), channel_id=1, source_target_pairs={{0,8},{1,9},{2,10},{3,11},{4,12},{5,13},{6,14},{7,15},{8,0},{9,1},... | collective-permute-start | bytes 811016 | tf_op jit(solution)/shard_map/ppermute | solution.py:18
  14.9 29.4 %copy-start = (bf16[4096,384]{1,0:T(8,128)(2,1)S(1)}, bf16[4096,384]{1,0:T(8,128)(2,1)}, u32[]{:S(2)}) copy-start(bf16[4096,384]{1,0:T(8,128)(2,1)} %refs_4_.9) | copy-start | bytes 9437188
  15.0 29.4 %copy-start.1 = (bf16[4096,384]{1,0:T(8,128)(2,1)S(1)}, bf16[4096,384]{1,0:T(8,128)(2,1)}, u32[]{:S(2)}) copy-start(bf16[4096,384]{1,0:T(8,128)(2,1)} %refs_5_.9) | copy-start | bytes 9437188
  15.0 29.4 %copy-start.2 = (bf16[384,4096]{1,0:T(8,128)(2,1)S(1)}, bf16[384,4096]{1,0:T(8,128)(2,1)}, u32[]{:S(2)}) copy-start(bf16[384,4096]{1,0:T(8,128)(2,1)} %refs_6_.9) | copy-start | bytes 9437188
  15.0 19.9 %collective-permute-start.7 = (bf16[32,4096]{1,0:T(8,128)(2,1)S(1)}, bf16[32,4096]{1,0:T(8,128)(2,1)S(1)}, u32[]{:S(2)}, u32[]{:S(2)}) collective-permute-start(bf16[32,4096]{1,0:T(8,128)(2,1)S(1)} %get-tuple-element.59), channel_id=1, source_target_pairs={{0,2},{1,3},{2,0},{3,1},{4,6},{5,7},{6,4},{7,5},{8,10},{9,11},{10,... | collective-permute-start | bytes 786440 | tf_op jit(solution)/shard_map/ppermute | solution.py:18
  18.0 19.3 %collective-permute-start.8 = (bf16[32,4096]{1,0:T(8,128)(2,1)S(1)}, bf16[32,4096]{1,0:T(8,128)(2,1)S(1)}, u32[]{:S(2)}, u32[]{:S(2)}) collective-permute-start(bf16[32,4096]{1,0:T(8,128)(2,1)S(1)} %get-tuple-element.60), channel_id=1, source_target_pairs={{0,4},{1,5},{2,6},{3,7},{4,0},{5,1},{6,2},{7,3},{8,12},{9,13},{10,... | collective-permute-start | bytes 786440 | tf_op jit(solution)/shard_map/ppermute | solution.py:18
  19.6 22.2 %collective-permute-start.9 = (bf16[32,4096]{1,0:T(8,128)(2,1)S(1)}, bf16[32,4096]{1,0:T(8,128)(2,1)S(1)}, u32[]{:S(2)}, u32[]{:S(2)}) collective-permute-start(bf16[32,4096]{1,0:T(8,128)(2,1)S(1)} %get-tuple-element.61), channel_id=1, source_target_pairs={{0,6},{1,7},{2,4},{3,5},{4,2},{5,3},{6,0},{7,1},{8,14},{9,15},{10,... | collective-permute-start | bytes 786440 | tf_op jit(solution)/shard_map/ppermute | solution.py:18
  29.1 19.0 %collective-permute-start.1 = (bf16[16,4096]{1,0:T(8,128)(2,1)S(1)}, bf16[16,4096]{1,0:T(8,128)(2,1)S(1)}, u32[]{:S(2)}, u32[]{:S(2)}) collective-permute-start(bf16[16,4096]{1,0:T(8,128)(2,1)S(1)} %get-tuple-element.51), channel_id=1, source_target_pairs={{0,2},{1,3},{2,0},{3,1},{4,6},{5,7},{6,4},{7,5},{8,10},{9,11},{10,... | collective-permute-start | bytes 393224 | tf_op jit(solution)/shard_map/ppermute | solution.py:18
  34.2 15.5 %collective-permute-start.2 = (bf16[16,4096]{1,0:T(8,128)(2,1)S(1)}, bf16[16,4096]{1,0:T(8,128)(2,1)S(1)}, u32[]{:S(2)}, u32[]{:S(2)}) collective-permute-start(bf16[16,4096]{1,0:T(8,128)(2,1)S(1)} %get-tuple-element.52), channel_id=1, source_target_pairs={{0,4},{1,5},{2,6},{3,7},{4,0},{5,1},{6,2},{7,3},{8,12},{9,13},{10,... | collective-permute-start | bytes 393224 | tf_op jit(solution)/shard_map/ppermute | solution.py:18
  34.9 14.8 %collective-permute-start.3 = (bf16[16,4096]{1,0:T(8,128)(2,1)S(1)}, bf16[16,4096]{1,0:T(8,128)(2,1)S(1)}, u32[]{:S(2)}, u32[]{:S(2)}) collective-permute-start(bf16[16,4096]{1,0:T(8,128)(2,1)S(1)} %get-tuple-element.53), channel_id=1, source_target_pairs={{0,6},{1,7},{2,4},{3,5},{4,2},{5,3},{6,0},{7,1},{8,14},{9,15},{10,... | collective-permute-start | bytes 393224 | tf_op jit(solution)/shard_map/ppermute | solution.py:18
  42.3 13.9 %collective-permute-start.14 = (bf16[16,4096]{1,0:T(8,128)(2,1)S(1)}, bf16[16,4096]{1,0:T(8,128)(2,1)S(1)}, u32[]{:S(2)}, u32[]{:S(2)}) collective-permute-start(bf16[16,4096]{1,0:T(8,128)(2,1)S(1)} %get-tuple-element.69), channel_id=1, source_target_pairs={{0,2},{1,3},{2,0},{3,1},{4,6},{5,7},{6,4},{7,5},{8,10},{9,11},{10,... | collective-permute-start | bytes 393224 | tf_op jit(solution)/shard_map/ppermute | solution.py:18
  44.3 13.4 %collective-permute-start.15 = (bf16[16,4096]{1,0:T(8,128)(2,1)S(1)}, bf16[16,4096]{1,0:T(8,128)(2,1)S(1)}, u32[]{:S(2)}, u32[]{:S(2)}) collective-permute-start(bf16[16,4096]{1,0:T(8,128)(2,1)S(1)} %get-tuple-element.70), channel_id=1, source_target_pairs={{0,4},{1,5},{2,6},{3,7},{4,0},{5,1},{6,2},{7,3},{8,12},{9,13},{10,... | collective-permute-start | bytes 393224 | tf_op jit(solution)/shard_map/ppermute | solution.py:18
  48.1 9.6 %collective-permute-start.16 = (bf16[16,4096]{1,0:T(8,128)(2,1)S(1)}, bf16[16,4096]{1,0:T(8,128)(2,1)S(1)}, u32[]{:S(2)}, u32[]{:S(2)}) collective-permute-start(bf16[16,4096]{1,0:T(8,128)(2,1)S(1)} %get-tuple-element.71), channel_id=1, source_target_pairs={{0,6},{1,7},{2,4},{3,5},{4,2},{5,3},{6,0},{7,1},{8,14},{9,15},{10,... | collective-permute-start | bytes 393224 | tf_op jit(solution)/shard_map/ppermute | solution.py:18
  54.2 7.9 %collective-permute-start.11 = (bf16[16,4096]{1,0:T(8,128)(2,1)S(1)}, bf16[16,4096]{1,0:T(8,128)(2,1)S(1)}, u32[]{:S(2)}, u32[]{:S(2)}) collective-permute-start(bf16[16,4096]{1,0:T(8,128)(2,1)S(1)} %get-tuple-element.66), channel_id=1, source_target_pairs={{0,2},{1,3},{2,0},{3,1},{4,6},{5,7},{6,4},{7,5},{8,10},{9,11},{10,... | collective-permute-start | bytes 393224 | tf_op jit(solution)/shard_map/ppermute | solution.py:18
  56.2 5.9 %collective-permute-start.12 = (bf16[16,4096]{1,0:T(8,128)(2,1)S(1)}, bf16[16,4096]{1,0:T(8,128)(2,1)S(1)}, u32[]{:S(2)}, u32[]{:S(2)}) collective-permute-start(bf16[16,4096]{1,0:T(8,128)(2,1)S(1)} %get-tuple-element.67), channel_id=1, source_target_pairs={{0,4},{1,5},{2,6},{3,7},{4,0},{5,1},{6,2},{7,3},{8,12},{9,13},{10,... | collective-permute-start | bytes 393224 | tf_op jit(solution)/shard_map/ppermute | solution.py:18
  56.2 5.9 %collective-permute-start.13 = (bf16[16,4096]{1,0:T(8,128)(2,1)S(1)}, bf16[16,4096]{1,0:T(8,128)(2,1)S(1)}, u32[]{:S(2)}, u32[]{:S(2)}) collective-permute-start(bf16[16,4096]{1,0:T(8,128)(2,1)S(1)} %get-tuple-element.68), channel_id=1, source_target_pairs={{0,6},{1,7},{2,4},{3,5},{4,2},{5,3},{6,0},{7,1},{8,14},{9,15},{10,... | collective-permute-start | bytes 393224 | tf_op jit(solution)/shard_map/ppermute | solution.py:18
  62.7 21.8 %collective-permute-start.17 = (bf16[32,4096]{1,0:T(8,128)(2,1)S(1)}, bf16[32,4096]{1,0:T(8,128)(2,1)S(1)}, u32[]{:S(2)}, u32[]{:S(2)}) collective-permute-start(bf16[32,4096]{1,0:T(8,128)(2,1)S(1)} %relay_back.2.refs_4_), channel_id=1, source_target_pairs={{0,8},{1,9},{2,10},{3,11},{4,12},{5,13},{6,14},{7,15},{8,0},{9,1},... | collective-permute-start | bytes 786440 | tf_op jit(solution)/shard_map/ppermute | solution.py:18
  69.9 5.0 %collective-permute-start.18 = (bf16[16,4096]{1,0:T(8,128)(2,1)S(1)}, bf16[16,4096]{1,0:T(8,128)(2,1)S(1)}, u32[]{:S(2)}, u32[]{:S(2)}) collective-permute-start(bf16[16,4096]{1,0:T(8,128)(2,1)S(1)} %get-tuple-element.73), channel_id=1, source_target_pairs={{0,2},{1,3},{2,0},{3,1},{4,6},{5,7},{6,4},{7,5},{8,10},{9,11},{10,... | collective-permute-start | bytes 393224 | tf_op jit(solution)/shard_map/ppermute | solution.py:18
  70.4 10.8 %collective-permute-start.19 = (bf16[16,4096]{1,0:T(8,128)(2,1)S(1)}, bf16[16,4096]{1,0:T(8,128)(2,1)S(1)}, u32[]{:S(2)}, u32[]{:S(2)}) collective-permute-start(bf16[16,4096]{1,0:T(8,128)(2,1)S(1)} %get-tuple-element.74), channel_id=1, source_target_pairs={{0,4},{1,5},{2,6},{3,7},{4,0},{5,1},{6,2},{7,3},{8,12},{9,13},{10,... | collective-permute-start | bytes 393224 | tf_op jit(solution)/shard_map/ppermute | solution.py:18
  70.9 13.5 %collective-permute-start.20 = (bf16[16,4096]{1,0:T(8,128)(2,1)S(1)}, bf16[16,4096]{1,0:T(8,128)(2,1)S(1)}, u32[]{:S(2)}, u32[]{:S(2)}) collective-permute-start(bf16[16,4096]{1,0:T(8,128)(2,1)S(1)} %get-tuple-element.75), channel_id=1, source_target_pairs={{0,6},{1,7},{2,4},{3,5},{4,2},{5,3},{6,0},{7,1},{8,14},{9,15},{10,... | collective-permute-start | bytes 393224 | tf_op jit(solution)/shard_map/ppermute | solution.py:18
  73.4 11.7 %collective-permute-start.22 = (bf16[32,4096]{1,0:T(8,128)(2,1)S(1)}, bf16[32,4096]{1,0:T(8,128)(2,1)S(1)}, u32[]{:S(2)}, u32[]{:S(2)}) collective-permute-start(bf16[32,4096]{1,0:T(8,128)(2,1)S(1)} %get-tuple-element.76), channel_id=1, source_target_pairs={{0,2},{1,3},{2,0},{3,1},{4,6},{5,7},{6,4},{7,5},{8,10},{9,11},{10,... | collective-permute-start | bytes 786440 | tf_op jit(solution)/shard_map/ppermute | solution.py:18
  74.9 13.5 %collective-permute-start.23 = (bf16[32,4096]{1,0:T(8,128)(2,1)S(1)}, bf16[32,4096]{1,0:T(8,128)(2,1)S(1)}, u32[]{:S(2)}, u32[]{:S(2)}) collective-permute-start(bf16[32,4096]{1,0:T(8,128)(2,1)S(1)} %get-tuple-element.77), channel_id=1, source_target_pairs={{0,4},{1,5},{2,6},{3,7},{4,0},{5,1},{6,2},{7,3},{8,12},{9,13},{10,... | collective-permute-start | bytes 786440 | tf_op jit(solution)/shard_map/ppermute | solution.py:18
  81.2 12.3 %collective-permute-start.24 = (bf16[32,4096]{1,0:T(8,128)(2,1)S(1)}, bf16[32,4096]{1,0:T(8,128)(2,1)S(1)}, u32[]{:S(2)}, u32[]{:S(2)}) collective-permute-start(bf16[32,4096]{1,0:T(8,128)(2,1)S(1)} %get-tuple-element.78), channel_id=1, source_target_pairs={{0,6},{1,7},{2,4},{3,5},{4,2},{5,3},{6,0},{7,1},{8,14},{9,15},{10,... | collective-permute-start | bytes 786440 | tf_op jit(solution)/shard_map/ppermute | solution.py:18
  85.0 10.9 %collective-permute-start.21 = (bf16[32,4096]{1,0:T(8,128)(2,1)S(1)}, bf16[32,4096]{1,0:T(8,128)(2,1)S(1)}, u32[]{:S(2)}, u32[]{:S(2)}) collective-permute-start(bf16[32,4096]{1,0:T(8,128)(2,1)S(1)} %relay_back.3), channel_id=1, source_target_pairs={{0,8},{1,9},{2,10},{3,11},{4,12},{5,13},{6,14},{7,15},{8,0},{9,1},... | collective-permute-start | bytes 786440 | tf_op jit(solution)/shard_map/ppermute | solution.py:18

commit v4 on v3

--- a/solution.py
+++ b/solution.py
@@ -112,8 +112,9 @@
     )
 
 
-def unit_rows(values, gain):
-    return values * lax.rsqrt(jnp.mean(values * values, axis=-1, keepdims=True) + EPS) * gain
+def unit_rows(values, gain, ones):
+    square = jnp.dot((values * values).astype(jnp.bfloat16), ones, preferred_element_type=jnp.float32)
+    return values * lax.rsqrt(square / values.shape[-1] + EPS) * gain
 
 
 def attend(cache_len, arrays, before, chunk, chunks, half, cap):
@@ -141,44 +142,46 @@
     if first:
         out_shape.append(jax.ShapeDtypeStruct((2 * top, token_rows), jnp.float32))
 
-    def body(len_ref, *refs):
+    def body(len_hbm, *refs):
         hbm, refs = refs[:11], refs[11:]
         carried, refs = refs[: len(before)], refs[len(before) :]
         outs, scratch = refs[: len(out_shape)], refs[len(out_shape) :]
         (q_ref, hid_ref, sk_ref, sv_ref, tk_ref, tv_ref, qg_ref, kg_ref, ng_ref, ids_ref, gates_ref) = scratch[:11]
-        kn_ref, vx_ref, qs_ref, info_ref, sems = scratch[11:]
+        kn_ref, vx_ref, qs_ref, info_ref, len_ref, sems = scratch[11:]
         resid_ref, normed_ref, out_refs = outs[0], outs[1], outs[2 : 2 + half]
         copies = []
         for i in range(11):
             source = hbm[i].at[mine, :] if i < 2 else hbm[i]
             target = scratch[i].at[0] if 6 <= i < 9 else scratch[i]
             copies.append(pltpu.make_async_copy(source, target, sems.at[i]))
-        order = (2, 7, 4, 0, 6, 3, 5, 9, 10, 1, 8)
-        for i in order:
+        copies.append(pltpu.make_async_copy(len_hbm, len_ref, sems.at[11]))
+        for i in (0, 6, 11, 2, 7, 4, 3, 5, 9, 10, 1, 8):
             copies[i].start()
-        length = len_ref[0]
-        live = lax.broadcasted_iota(jnp.int32, (cache_rows, head), 0) < length
-        live_ones = jnp.where(live, 1.0, 0.0).astype(jnp.bfloat16)
+        ones = jnp.ones((head, head), jnp.bfloat16)
+        for i in (0, 6):
+            copies[i].wait()
+        q_gain = qg_ref[...] * (math.log2(math.e) / math.sqrt(head))
+        for h in range(heads):
+            x = q_ref[:, h * head : (h + 1) * head].astype(jnp.float32)
+            qs_ref[h * rows : (h + 1) * rows, :] = unit_rows(x, q_gain, ones).astype(jnp.bfloat16)
         for i in (2, 7, 4):
             copies[i].wait()
         k_gain = kg_ref[...]
         for g in range(heads_kv):
             cols = slice(g * head, (g + 1) * head)
-            kn_ref[g, :cache_rows, :] = unit_rows(sk_ref[:, cols].astype(jnp.float32), k_gain).astype(jnp.bfloat16)
-            kn_ref[g, cache_rows:, :] = unit_rows(tk_ref[:, cols].astype(jnp.float32), k_gain).astype(jnp.bfloat16)
-        for i in (0, 6):
+            kn_ref[g, :cache_rows, :] = unit_rows(sk_ref[:, cols].astype(jnp.float32), k_gain, ones).astype(
+                jnp.bfloat16
+            )
+            kn_ref[g, cache_rows:, :] = unit_rows(tk_ref[:, cols].astype(jnp.float32), k_gain, ones).astype(
+                jnp.bfloat16
+            )
+        for i in (11, 3, 5):
             copies[i].wait()
-        q_gain = qg_ref[...] * (math.log2(math.e) / math.sqrt(head))
-        for h in range(heads):
-            x = q_ref[:, h * head : (h + 1) * head].astype(jnp.float32)
-            qs_ref[h * rows : (h + 1) * rows, :] = unit_rows(x, q_gain).astype(jnp.bfloat16)
-        for i in (3, 5):
-            copies[i].wait()
+        live = lax.broadcasted_iota(jnp.int32, (cache_rows, head), 0) < len_ref[0]
+        live_ones = jnp.where(live, 1.0, 0.0).astype(jnp.bfloat16)
         for g in range(heads_kv):
             cols = slice(g * head, (g + 1) * head)
-            vx_ref[g, :cache_rows, :head] = jnp.where(live, sv_ref[:, cols].astype(jnp.float32), 0.0).astype(
-                jnp.bfloat16
-            )
+            vx_ref[g, :cache_rows, :head] = sv_ref[:, cols] * live_ones
             vx_ref[g, :cache_rows, head:] = live_ones
             vx_ref[g, cache_rows:, :head] = tv_ref[:, cols]
             vx_ref[g, cache_rows:, head:] = jnp.ones((token_rows, head), jnp.bfloat16)
@@ -223,7 +226,7 @@
     results = pl.pallas_call(
         body,
         out_shape=out_shape,
-        in_specs=[pl.BlockSpec(memory_space=SMEM)]
+        in_specs=[pl.BlockSpec(memory_space=pl.ANY)]
         + [pl.BlockSpec(memory_space=pltpu.HBM)] * 11
         + [whole(b) for b in before],
         out_specs=[whole(o) for o in out_shape],
@@ -243,7 +246,8 @@
             VMEM((heads_kv, keys, 2 * head), jnp.bfloat16),
             VMEM((rows * heads, head), jnp.bfloat16),
             VMEM((2 * top, token_rows), jnp.float32),
-            pltpu.SemaphoreType.DMA((11,)),
+            SMEM((1,), jnp.int32),
+            pltpu.SemaphoreType.DMA((12,)),
         ],
         compiler_params=params(24),
         cost_estimate=taking(4),
@@ -252,7 +256,7 @@
     return results[0], results[1], list(results[2 : 2 + half]), (results[-1] if first else None)
 
 
-def relay(rows_in, top, half, cap, carried, after):
+def relay(rows_in, top, half, cap, carried, after, microseconds):
     width = rows_in.shape[1] - ROUTE
     out = [jax.ShapeDtypeStruct((cap, width), jnp.bfloat16)] * half
     out += [jax.ShapeDtypeStruct(x.shape, x.dtype) for x in carried]
@@ -269,33 +273,27 @@
         in_specs=[whole(rows_in)] + [whole(x) for x in carried] + unread(after),
         out_specs=[whole(o) for o in out],
         compiler_params=params(24),
-        cost_estimate=taking(0.5),
+        cost_estimate=taking(microseconds),
         name="relay",
     )(rows_in, *carried, *after)
     return list(results[:half]), list(results[half:])
 
 
-def arrange(arrays, plan, after):
-    width = arrays[0].shape[1]
-    out = [jax.ShapeDtypeStruct((sum(piece[2] for piece in pieces), width), arrays[0].dtype) for pieces in plan]
-
+def passed(arrays, after, microseconds):
     def body(*refs):
         outs = refs[len(arrays) + len(after) :]
-        for out_ref, pieces in zip(outs, plan):
-            at = 0
-            for index, start, count in pieces:
-                out_ref[at : at + count, :] = refs[index][start : start + count, :]
-                at += count
+        for i in range(len(arrays)):
+            outs[i][...] = refs[i][...]
 
     return list(
         pl.pallas_call(
             body,
-            out_shape=out,
+            out_shape=[jax.ShapeDtypeStruct(x.shape, x.dtype) for x in arrays],
             in_specs=[whole(x) for x in arrays] + unread(after),
-            out_specs=[whole(x) for x in out],
+            out_specs=[whole(x) for x in arrays],
             compiler_params=params(24),
-            cost_estimate=taking(0.3),
-            name="arrange",
+            cost_estimate=taking(microseconds),
+            name="passed",
         )(*arrays, *after)
     )
 
@@ -305,7 +303,7 @@
     total = len(ins) * rows
     hidden = weights[0].shape[1]
     block = min(total, 128)
-    part = 512
+    part = 1024
     back = total // outs
     out = [jax.ShapeDtypeStruct((back, width), jnp.bfloat16)] * outs
 
@@ -319,10 +317,8 @@
         def rows_of(span):
             inners = []
             for wg, wu in ((wg0, wu0), (wg1, wu1)):
-                pre = jnp.zeros((block, 2 * hidden), jnp.float32)
-                for k in range(0, width, part):
-                    both = jnp.concatenate([wg[k : k + part, :], wu[k : k + part, :]], axis=1)
-                    pre = pre + jnp.dot(x_ref[span, k : k + part], both, preferred_element_type=jnp.float32)
+                both = jnp.concatenate([wg[...], wu[...]], axis=1)
+                pre = jnp.dot(x_ref[span, :], both, preferred_element_type=jnp.float32)
                 gate = pre[:, :hidden]
                 inners.append((gate / (1.0 + jnp.exp(-gate)) * pre[:, hidden:]).astype(jnp.bfloat16))
             inner = jnp.concatenate(inners, axis=1)
@@ -357,7 +353,7 @@
     )
 
 
-def relay_back(returned, rows_in, top, cap, after):
+def relay_back(returned, rows_in, top, cap, after, microseconds):
     half = len(returned)
     rows, width = rows_in.shape[0], returned[0].shape[1]
     out = jax.ShapeDtypeStruct((rows, width), jnp.bfloat16)
@@ -376,38 +372,59 @@
         out_specs=whole(out),
         scratch_shapes=[VMEM((half * cap, width), jnp.bfloat16)],
         compiler_params=params(24),
-        cost_estimate=taking(0.6),
+        cost_estimate=taking(microseconds),
         name="relay_back",
     )(rows_in, *returned, *after)
 
 
-def finish(resid, far, returned, info, cap):
+def add_near(resid, far, returned, info, cap, after, microseconds):
     half = len(returned)
     chunks = len(resid)
     rows, width = resid[0].shape
-    out = jax.ShapeDtypeStruct((rows * chunks, width), jnp.bfloat16)
+    out = jax.ShapeDtypeStruct((rows * chunks, width), jnp.float32)
 
     def body(info_ref, *refs):
-        resid_refs, far_refs, refs = refs[:chunks], refs[chunks : 2 * chunks], refs[2 * chunks :]
-        in_refs, (out_ref, joined) = refs[:half], refs[half:]
+        resid_refs, far_refs, refs = refs[:chunks], refs[chunks : chunks + len(far)], refs[chunks + len(far) :]
+        in_refs, (out_ref, joined) = refs[:half], refs[half + len(after) :]
         for c in range(chunks):
             for d in range(half):
                 joined[d * cap : (d + 1) * cap, :] = in_refs[d][c * cap : (c + 1) * cap, :]
-            near = weighted_rows(info_ref[:, c * rows : (c + 1) * rows], half, joined, cap)
-            out_ref[c * rows : (c + 1) * rows, :] = (
-                resid_refs[c][...] + (near + far_refs[c][...].astype(jnp.float32))
-            ).astype(jnp.bfloat16)
+            total = resid_refs[c][...] + weighted_rows(info_ref[:, c * rows : (c + 1) * rows], half, joined, cap)
+            if c < len(far):
+                total = total + far_refs[c][...].astype(jnp.float32)
+            out_ref[c * rows : (c + 1) * rows, :] = total
 
     return pl.pallas_call(
         body,
         out_shape=out,
-        in_specs=[whole(x) for x in (info, *resid, *far, *returned)],
+        in_specs=[whole(x) for x in (info, *resid, *far, *returned)] + unread(after),
         out_specs=whole(out),
         scratch_shapes=[VMEM((half * cap, width), jnp.bfloat16)],
         compiler_params=params(24),
-        cost_estimate=taking(2),
-        name="finish",
-    )(info, *resid, *far, *returned)
+        cost_estimate=taking(microseconds),
+        name="add_near",
+    )(info, *resid, *far, *returned, *after)
+
+
+def add_far(base, far):
+    total, width = base.shape
+    first = total - far.shape[0]
+    out = jax.ShapeDtypeStruct(base.shape, jnp.bfloat16)
+
+    def body(base_ref, far_ref, out_ref):
+        if first:
+            out_ref[:first, :] = base_ref[:first, :].astype(jnp.bfloat16)
+        out_ref[first:, :] = (base_ref[first:, :] + far_ref[...].astype(jnp.float32)).astype(jnp.bfloat16)
+
+    return pl.pallas_call(
+        body,
+        out_shape=out,
+        in_specs=[whole(base), whole(far)],
+        out_specs=whole(out),
+        compiler_params=params(24),
+        cost_estimate=taking(1),
+        name="add_far",
+    )(base, far)
 
 
 def around(parts):
@@ -463,26 +480,33 @@
         info = packed if c == 0 else info
         resid.append(residual)
         normed.append(rows_c)
-    far_rows = [exchange(x, ep // 2) for x in normed]
-    near = around(arrange(outgoing, [[(d, 0, slots)] for d in range(half)], list(weights[3:])))
-    placed = [around(relay(far_rows[0], top, half, cap, [], [])[0])]
-    after = near[1:]
-    for c in range(1, chunks):
-        arrived, _ = relay(far_rows[c], top, half, cap, [], after)
-        placed.append(around(arrived))
-        after = [arrived[0]]
-    near_out = expert(near, weights, half, after, 4)
-    after = near_out[0]
-    returned, far_back = [], []
+    far_rows = [exchange(normed[0], ep // 2)]
+    gate = passed(outgoing + normed[1:], list(weights[3:]), 0.3)
+    near = around(gate[:half])
+    far_rows += [exchange(x, ep // 2) for x in gate[half:]]
+
+    placed = []
+    after = [gate[0]]
     for c in range(chunks):
-        far_out = expert(placed[c], weights, half, [after], 0.01)
-        returned.append(around(far_out))
-        after = far_out[0]
+        slotted, _ = relay(far_rows[c], top, half, cap, [], after, 0.5)
+        placed.append(around(slotted))
+        after = [slotted[0], *near, placed[0][1]]
+    returned, after = [], after[:1]
     for c in range(chunks):
-        back = relay_back(returned[c], far_rows[c], top, cap, [after] + far_back)
+        outs = expert(placed[c], weights, half, after, 0.01)
+        returned.append(around(outs))
+        after = outs[:1]
+    far_back, near_out = [], None
+    for c in range(chunks):
+        if c == chunks - 1:
+            near_out = expert(near, weights, half, after, 4)
+            after = near_out[:1]
+        back = relay_back(returned[c], far_rows[c], top, cap, after, 0.6)
         far_back.append(exchange(back, ep // 2))
-        after = back
-    return finish(resid, far_back, around(near_out), info, cap)
+        after = [back]
+    near_back = around(passed(near_out, after, 0.1))
+    base = add_near(resid, far_back[:-1], near_back, info, cap, [], 4)
+    return add_far(base, far_back[-1])
 
 
 def solution(mesh):

time: 97.8 us -> 90.6 us (0.926)
  waiting for transfers between devices: 37.4 us -> 28.4 us
  starting transfers between devices: 34.3 us -> 38.7 us
  Pallas kernels: 25.1 us -> 22.5 us
    ppermute x25, waiting for transfers between devices: 37.4 us -> 28.4 us  [exchange(): lax.ppermute(value, 'ep', [(i, i ^ distance) for i in range(lax.axis_size...]
    ppermute x25, starting transfers between devices: 34.3 us -> 38.7 us  [exchange(): lax.ppermute(value, 'ep', [(i, i ^ distance) for i in range(lax.axis_size...]
    pallas_call x3, Pallas kernels: 12.5 us -> 9.62 us  [expert(): pl.pallas_call(body, out_shape=out, in_specs=[whole(x) for x in ins] + [w...]
    pallas_call x2 -> x4, Pallas kernels: 1.81 us -> 1.96 us  [the longest x1 0.94 us: add_near(): pl.pallas_call(body, out_shape=out, in_specs=[whole(x) for x in (info, *r...]
  transfers between devices with their start and end apart: 25 -> 25, of which waited for: 10 -> 9; matrix products, arithmetic and copies ran while one was open for 0% -> 0% of each run, Pallas kernels for 23% -> 24%
where the time goes in v4:
time: 90.6 us; the launch traced here: 90.4 us
  starting transfers between devices  38.7 us (43%)
  waiting for transfers between devices  28.4 us (31%)
  Pallas kernels  22.5 us (25%)
    ppermute x25, starting transfers between devices, exchange(): lax.ppermute(value, 'ep', [(i, i ^ distance) for i in range(lax.axis_size...  38.7 us
    ppermute x25, waiting for transfers between devices, exchange(): lax.ppermute(value, 'ep', [(i, i ^ distance) for i in range(lax.axis_size...  28.4 us
    pallas_call x3, Pallas kernels, expert(): pl.pallas_call(body, out_shape=out, in_specs=[whole(x) for x in ins] + [w...  9.62 us
    pallas_call x2, Pallas kernels, attend(): pl.pallas_call(body, out_shape=out_shape, in_specs=[pl.BlockSpec(memory_s...  8.77 us
  transfers between devices with their start and end apart: 25, of which 9 were waited for; matrix products, arithmetic and copies ran while one was open for 0% of the time, Pallas kernels for 24%

profile of v4, /device:TPU:0, one launch (start us, length us, event | category | flops | bytes accessed | tf_op | source)
XLA Modules:
  0.0 90.4 jit_solution(9089169895020216189)
XLA Ops:
  1.6 4.4 %attend.2 = (f32[32,4096]{1,0:T(8,128)S(1)}, bf16[32,4224]{1,0:T(8,128)(2,1)S(1)}, bf16[16,4096]{1,0:T(8,128)(2,1)S(1)}, bf16[16,4096]{1,0:T(8,128)(2,1)S(1)}, b...) custom-call(s32[1]{0:T(128)S(6)} %copy.16.len_hbm, bf16[64,4096]{1,0:T(8,128)(2,1)} %refs_0_.3, ...), custom_call_target="tpu_custom_call" | custom-call | flops 1 | bytes 14000000 | tf_op jit(solution)/shard_map/attend/pallas_call | solution.py:226
  6.0 3.7 %collective-permute-start = (bf16[32,4224]{1,0:T(8,128)(2,1)S(1)}, bf16[32,4224]{1,0:T(8,128)(2,1)S(1)}, u32[]{:S(2)}, u32[]{:S(2)}) collective-permute-start(bf16[32,4224]{1,0:T(8,128)(2,1)S(1)} %get-tuple-element.54), channel_id=1, source_target_pairs={{0,8},{1,9},{2,10},{3,11},{4,12},{5,13},{6,14},{7,15},{8,0},{9,1},... | collective-permute-start | bytes 811016 | tf_op jit(solution)/shard_map/ppermute | solution.py:18
  9.7 4.4 %attend.3 = (f32[32,4096]{1,0:T(8,128)S(1)}, bf16[32,4224]{1,0:T(8,128)(2,1)S(1)}, bf16[32,4096]{1,0:T(8,128)(2,1)S(1)}, bf16[32,4096]{1,0:T(8,128)(2,1)S(1)}, b...) custom-call(s32[1]{0:T(128)S(6)} %copy.16.len_hbm, bf16[64,4096]{1,0:T(8,128)(2,1)} %refs_0_.3, ...), custom_call_target="tpu_custom_call" | custom-call | flops 1 | bytes 14000000 | tf_op jit(solution)/shard_map/attend/pallas_call | solution.py:226
  14.1 0.9 collective-permute-done.3.refs_7_.refs_9_
  15.0 3.0 %collective-permute-start.8 = (bf16[32,4096]{1,0:T(8,128)(2,1)S(1)}, bf16[32,4096]{1,0:T(8,128)(2,1)S(1)}, u32[]{:S(2)}, u32[]{:S(2)}) collective-permute-start(bf16[32,4096]{1,0:T(8,128)(2,1)S(1)} %get-tuple-element.66), channel_id=1, source_target_pairs={{0,2},{1,3},{2,0},{3,1},{4,6},{5,7},{6,4},{7,5},{8,10},{9,11},{10,... | collective-permute-start | bytes 786440 | tf_op jit(solution)/shard_map/ppermute | solution.py:18
  18.0 2.6 %collective-permute-start.7 = (bf16[32,4224]{1,0:T(8,128)(2,1)S(1)}, bf16[32,4224]{1,0:T(8,128)(2,1)S(1)}, u32[]{:S(2)}, u32[]{:S(2)}) collective-permute-start(bf16[32,4224]{1,0:T(8,128)(2,1)S(1)} %get-tuple-element.65), channel_id=1, source_target_pairs={{0,8},{1,9},{2,10},{3,11},{4,12},{5,13},{6,14},{7,15},{8,0},{9,1},... | collective-permute-start | bytes 811016 | tf_op jit(solution)/shard_map/ppermute | solution.py:18
  20.6 1.6 %collective-permute-start.9 = (bf16[32,4096]{1,0:T(8,128)(2,1)S(1)}, bf16[32,4096]{1,0:T(8,128)(2,1)S(1)}, u32[]{:S(2)}, u32[]{:S(2)}) collective-permute-start(bf16[32,4096]{1,0:T(8,128)(2,1)S(1)} %get-tuple-element.67), channel_id=1, source_target_pairs={{0,4},{1,5},{2,6},{3,7},{4,0},{5,1},{6,2},{7,3},{8,12},{9,13},{10,... | collective-permute-start | bytes 786440 | tf_op jit(solution)/shard_map/ppermute | solution.py:18
  22.6 5.3 %collective-permute-done.rows_ref = bf16[32,4224]{1,0:T(8,128)(2,1)S(1)} collective-permute-done((bf16[32,4224]{1,0:T(8,128)(2,1)S(1)}, bf16[32,4224]{1,0:T(8,128)(2,1)S(1)}, u32[]{:S(2)}, u32[]{:S(2)}) %collective-permute-start) | collective-permute-done | bytes 270368 | tf_op jit(solution)/shard_map/ppermute | solution.py:18
  28.4 2.6 %collective-permute-start.4 = (bf16[16,4096]{1,0:T(8,128)(2,1)S(1)}, bf16[16,4096]{1,0:T(8,128)(2,1)S(1)}, u32[]{:S(2)}, u32[]{:S(2)}) collective-permute-start(bf16[16,4096]{1,0:T(8,128)(2,1)S(1)} %get-tuple-element.62), channel_id=1, source_target_pairs={{0,2},{1,3},{2,0},{3,1},{4,6},{5,7},{6,4},{7,5},{8,10},{9,11},{10,... | collective-permute-start | bytes 393224 | tf_op jit(solution)/shard_map/ppermute | solution.py:18
  31.0 2.9 %collective-permute-done.4.refs_5_.refs_1_ = bf16[16,4096]{1,0:T(8,128)(2,1)S(1)} collective-permute-done((bf16[16,4096]{1,0:T(8,128)(2,1)S(1)}, bf16[16,4096]{1,0:T(8,128)(2,1)S(1)}, u32[]{:S(2)}, u32[]{:S(2)}) %collective-permute-start.4) | collective-permute-done | bytes 131104 | tf_op jit(solution)/shard_map/ppermute | solution.py:18
  34.0 6.0 %collective-permute-start.5 = (bf16[16,4096]{1,0:T(8,128)(2,1)S(1)}, bf16[16,4096]{1,0:T(8,128)(2,1)S(1)}, u32[]{:S(2)}, u32[]{:S(2)}) collective-permute-start(bf16[16,4096]{1,0:T(8,128)(2,1)S(1)} %get-tuple-element.63), channel_id=1, source_target_pairs={{0,4},{1,5},{2,6},{3,7},{4,0},{5,1},{6,2},{7,3},{8,12},{9,13},{10,... | collective-permute-start | bytes 393224 | tf_op jit(solution)/shard_map/ppermute | solution.py:18
  39.9 1.4 %collective-permute-start.6 = (bf16[16,4096]{1,0:T(8,128)(2,1)S(1)}, bf16[16,4096]{1,0:T(8,128)(2,1)S(1)}, u32[]{:S(2)}, u32[]{:S(2)}) collective-permute-start(bf16[16,4096]{1,0:T(8,128)(2,1)S(1)} %get-tuple-element.64), channel_id=1, source_target_pairs={{0,6},{1,7},{2,4},{3,5},{4,2},{5,3},{6,0},{7,1},{8,14},{9,15},{10,... | collective-permute-start | bytes 393224 | tf_op jit(solution)/shard_map/ppermute | solution.py:18
  41.3 1.0 %collective-permute-done.10.refs_4_.refs_3_ = bf16[32,4096]{1,0:T(8,128)(2,1)S(1)} collective-permute-done((bf16[32,4096]{1,0:T(8,128)(2,1)S(1)}, bf16[32,4096]{1,0:T(8,128)(2,1)S(1)}, u32[]{:S(2)}, u32[]{:S(2)}) %collective-permute-start.10) | collective-permute-done | bytes 262176 | tf_op jit(solution)/shard_map/ppermute | solution.py:18
  44.0 2.4 %collective-permute-start.16 = (bf16[16,4096]{1,0:T(8,128)(2,1)S(1)}, bf16[16,4096]{1,0:T(8,128)(2,1)S(1)}, u32[]{:S(2)}, u32[]{:S(2)}) collective-permute-start(bf16[16,4096]{1,0:T(8,128)(2,1)S(1)} %get-tuple-element.76), channel_id=1, source_target_pairs={{0,6},{1,7},{2,4},{3,5},{4,2},{5,3},{6,0},{7,1},{8,14},{9,15},{10,... | collective-permute-start | bytes 393224 | tf_op jit(solution)/shard_map/ppermute | solution.py:18
  46.5 2.2 %collective-permute-done.6.refs_3_ = bf16[16,4096]{1,0:T(8,128)(2,1)S(1)} collective-permute-done((bf16[16,4096]{1,0:T(8,128)(2,1)S(1)}, bf16[16,4096]{1,0:T(8,128)(2,1)S(1)}, u32[]{:S(2)}, u32[]{:S(2)}) %collective-permute-start.6) | collective-permute-done | bytes 131104 | tf_op jit(solution)/shard_map/ppermute | solution.py:18
  48.7 3.4 %expert.3 = (bf16[16,4096]{1,0:T(8,128)(2,1)S(1)}, bf16[16,4096]{1,0:T(8,128)(2,1)S(1)}, bf16[16,4096]{1,0:T(8,128)(2,1)S(1)}, bf16[16,4096]{1,0:T(8,128)(2,1)S(1)}) custom-call(bf16[16,4096]{1,0:T(8,128)(2,1)S(1)} %get-tuple-element.61.refs_0_, bf16[16,4096]{1,0:T(8,128)(2,1)S(1)} %collective-permute-done.4.refs_5_.refs_1_, ...), custom_call_target="tpu_custom_call" | custom-call | flops 1 | bytes 35000 | tf_op jit(solution)/shard_map/expert/pallas_call | solution.py:343
  52.8 1.3 %collective-permute-start.12 = (bf16[16,4096]{1,0:T(8,128)(2,1)S(1)}, bf16[16,4096]{1,0:T(8,128)(2,1)S(1)}, u32[]{:S(2)}, u32[]{:S(2)}) collective-permute-start(bf16[16,4096]{1,0:T(8,128)(2,1)S(1)} %get-tuple-element.72), channel_id=1, source_target_pairs={{0,4},{1,5},{2,6},{3,7},{4,0},{5,1},{6,2},{7,3},{8,12},{9,13},{10,... | collective-permute-start | bytes 393224 | tf_op jit(solution)/shard_map/ppermute | solution.py:18
  54.1 1.5 %collective-permute-start.13 = (bf16[16,4096]{1,0:T(8,128)(2,1)S(1)}, bf16[16,4096]{1,0:T(8,128)(2,1)S(1)}, u32[]{:S(2)}, u32[]{:S(2)}) collective-permute-start(bf16[16,4096]{1,0:T(8,128)(2,1)S(1)} %get-tuple-element.73), channel_id=1, source_target_pairs={{0,6},{1,7},{2,4},{3,5},{4,2},{5,3},{6,0},{7,1},{8,14},{9,15},{10,... | collective-permute-start | bytes 393224 | tf_op jit(solution)/shard_map/ppermute | solution.py:18
  55.7 3.4 %expert.4 = (bf16[16,4096]{1,0:T(8,128)(2,1)S(1)}, bf16[16,4096]{1,0:T(8,128)(2,1)S(1)}, bf16[16,4096]{1,0:T(8,128)(2,1)S(1)}, bf16[16,4096]{1,0:T(8,128)(2,1)S(1)}) custom-call(bf16[16,4096]{1,0:T(8,128)(2,1)S(1)} %get-tuple-element.69.refs_10_.refs_0_, bf16[16,4096]{1,0:T(8,128)(2,1)S(1)} %collective-permute-done.14.refs_1_, ...), custom_call_target="tpu_custom_call" | custom-call | flops 1 | bytes 35000 | tf_op jit(solution)/shard_map/expert/pallas_call | solution.py:343
  59.1 0.9 %collective-permute-start.18 = (bf16[16,4096]{1,0:T(8,128)(2,1)S(1)}, bf16[16,4096]{1,0:T(8,128)(2,1)S(1)}, u32[]{:S(2)}, u32[]{:S(2)}) collective-permute-start(bf16[16,4096]{1,0:T(8,128)(2,1)S(1)} %get-tuple-element.82), channel_id=1, source_target_pairs={{0,2},{1,3},{2,0},{3,1},{4,6},{5,7},{6,4},{7,5},{8,10},{9,11},{10,... | collective-permute-start | bytes 393224 | tf_op jit(solution)/shard_map/ppermute | solution.py:18
  60.0 1.3 %collective-permute-start.19 = (bf16[16,4096]{1,0:T(8,128)(2,1)S(1)}, bf16[16,4096]{1,0:T(8,128)(2,1)S(1)}, u32[]{:S(2)}, u32[]{:S(2)}) collective-permute-start(bf16[16,4096]{1,0:T(8,128)(2,1)S(1)} %get-tuple-element.83), channel_id=1, source_target_pairs={{0,4},{1,5},{2,6},{3,7},{4,0},{5,1},{6,2},{7,3},{8,12},{9,13},{10,... | collective-permute-start | bytes 393224 | tf_op jit(solution)/shard_map/ppermute | solution.py:18
  61.3 1.5 %collective-permute-start.20 = (bf16[16,4096]{1,0:T(8,128)(2,1)S(1)}, bf16[16,4096]{1,0:T(8,128)(2,1)S(1)}, u32[]{:S(2)}, u32[]{:S(2)}) collective-permute-start(bf16[16,4096]{1,0:T(8,128)(2,1)S(1)} %get-tuple-element.84), channel_id=1, source_target_pairs={{0,6},{1,7},{2,4},{3,5},{4,2},{5,3},{6,0},{7,1},{8,14},{9,15},{10,... | collective-permute-start | bytes 393224 | tf_op jit(solution)/shard_map/ppermute | solution.py:18
  63.8 2.7 %expert.5 = (bf16[32,4096]{1,0:T(8,128)(2,1)S(1)}, bf16[32,4096]{1,0:T(8,128)(2,1)S(1)}, bf16[32,4096]{1,0:T(8,128)(2,1)S(1)}, bf16[32,4096]{1,0:T(8,128)(2,1)S(1)}) custom-call(bf16[32,4096]{1,0:T(8,128)(2,1)S(1)} %get-tuple-element.60.refs_0_.refs_1_, bf16[32,4096]{1,0:T(8,128)(2,1)S(1)} %collective-permute-done.8.refs_2_.refs_1_, ...), custom_call_target="tpu_custom_call" | custom-call | flops 1 | bytes 14000000 | tf_op jit(solution)/shard_map/expert/pallas_call | solution.py:343
  66.6 2.2 %collective-permute-done.20.refs_3_ = bf16[16,4096]{1,0:T(8,128)(2,1)S(1)} collective-permute-done((bf16[16,4096]{1,0:T(8,128)(2,1)S(1)}, bf16[16,4096]{1,0:T(8,128)(2,1)S(1)}, u32[]{:S(2)}, u32[]{:S(2)}) %collective-permute-start.20) | collective-permute-done | bytes 131104 | tf_op jit(solution)/shard_map/ppermute | solution.py:18
  69.9 1.9 %collective-permute-start.22 = (bf16[32,4096]{1,0:T(8,128)(2,1)S(1)}, bf16[32,4096]{1,0:T(8,128)(2,1)S(1)}, u32[]{:S(2)}, u32[]{:S(2)}) collective-permute-start(bf16[32,4096]{1,0:T(8,128)(2,1)S(1)} %get-tuple-element.87), channel_id=1, source_target_pairs={{0,4},{1,5},{2,6},{3,7},{4,0},{5,1},{6,2},{7,3},{8,12},{9,13},{10,... | collective-permute-start | bytes 786440 | tf_op jit(solution)/shard_map/ppermute | solution.py:18
  71.8 1.2 %collective-permute-start.23 = (bf16[32,4096]{1,0:T(8,128)(2,1)S(1)}, bf16[32,4096]{1,0:T(8,128)(2,1)S(1)}, u32[]{:S(2)}, u32[]{:S(2)}) collective-permute-start(bf16[32,4096]{1,0:T(8,128)(2,1)S(1)} %get-tuple-element.88), channel_id=1, source_target_pairs={{0,6},{1,7},{2,4},{3,5},{4,2},{5,3},{6,0},{7,1},{8,14},{9,15},{10,... | collective-permute-start | bytes 786440 | tf_op jit(solution)/shard_map/ppermute | solution.py:18
  73.0 1.8 %collective-permute-start.24 = (bf16[32,4096]{1,0:T(8,128)(2,1)S(1)}, bf16[32,4096]{1,0:T(8,128)(2,1)S(1)}, u32[]{:S(2)}, u32[]{:S(2)}) collective-permute-start(bf16[32,4096]{1,0:T(8,128)(2,1)S(1)} %relay_back.3.refs_4_), channel_id=1, source_target_pairs={{0,8},{1,9},{2,10},{3,11},{4,12},{5,13},{6,14},{7,15},{8,0},{9,1},... | collective-permute-start | bytes 786440 | tf_op jit(solution)/shard_map/ppermute | solution.py:18
  74.8 1.2 %collective-permute-done.17.refs_2_ = bf16[32,4096]{1,0:T(8,128)(2,1)S(1)} collective-permute-done((bf16[32,4096]{1,0:T(8,128)(2,1)S(1)}, bf16[32,4096]{1,0:T(8,128)(2,1)S(1)}, u32[]{:S(2)}, u32[]{:S(2)}) %collective-permute-start.17) | collective-permute-done | bytes 262176 | tf_op jit(solution)/shard_map/ppermute | solution.py:18
  76.0 9.4 %collective-permute-done.22.refs_5_ = bf16[32,4096]{1,0:T(8,128)(2,1)S(1)} collective-permute-done((bf16[32,4096]{1,0:T(8,128)(2,1)S(1)}, bf16[32,4096]{1,0:T(8,128)(2,1)S(1)}, u32[]{:S(2)}, u32[]{:S(2)}) %collective-permute-start.22) | collective-permute-done | bytes 262176 | tf_op jit(solution)/shard_map/ppermute | solution.py:18
  85.3 3.3 %collective-permute-done.23.refs_6_ = bf16[32,4096]{1,0:T(8,128)(2,1)S(1)} collective-permute-done((bf16[32,4096]{1,0:T(8,128)(2,1)S(1)}, bf16[32,4096]{1,0:T(8,128)(2,1)S(1)}, u32[]{:S(2)}, u32[]{:S(2)}) %collective-permute-start.23) | collective-permute-done | bytes 262176 | tf_op jit(solution)/shard_map/ppermute | solution.py:18
  88.6 0.9 %add_near.1.base_ref = f32[64,4096]{1,0:T(8,128)S(1)} custom-call(f32[4,64]{1,0:T(4,128)S(1)} %get-tuple-element.47.info_ref, f32[32,4096]{1,0:T(8,128)S(1)} %get-tuple-element.48.refs_0_, f32[32,4096]{1,0:T(8,128)S(1)} %get-tuple-element.53.refs_1_, bf16[32,4096]{1,0:T(8,128)(2,1)S(1)} %collective-permute-done.17.refs_2_, ...), custom_call_target="tpu_custom_call" | custom-call | flops 1 | bytes 14000000 | tf_op jit(solution)/shard_map/add_near/pallas_call | solution.py:397
  89.6 0.9 add_far.1
  (37 shorter events, 6.5 us)
Async XLA Ops:
  0.0 14.1 %collective-permute-start.1 = (bf16[4096,384]{1,0:T(8,128)(2,1)}, bf16[4096,384]{1,0:T(8,128)(2,1)S(1)}, u32[]{:S(2)}, u32[]{:S(2)}) collective-permute-start(bf16[4096,384]{1,0:T(8,128)(2,1)} %refs_4_.9), channel_id=1, source_target_pairs={{0,1},{1,0},{2,3},{3,2},{4,5},{5,4},{6,7},{7,6},{8,9},{9,8},{10,11... | collective-permute-start | bytes 9437192 | tf_op jit(solution)/shard_map/ppermute | solution.py:18
  0.5 13.6 %collective-permute-start.2 = (bf16[4096,384]{1,0:T(8,128)(2,1)}, bf16[4096,384]{1,0:T(8,128)(2,1)S(1)}, u32[]{:S(2)}, u32[]{:S(2)}) collective-permute-start(bf16[4096,384]{1,0:T(8,128)(2,1)} %refs_5_.9), channel_id=1, source_target_pairs={{0,1},{1,0},{2,3},{3,2},{4,5},{5,4},{6,7},{7,6},{8,9},{9,8},{10,11... | collective-permute-start | bytes 9437192 | tf_op jit(solution)/shard_map/ppermute | solution.py:18
  0.5 14.4 %collective-permute-start.3 = (bf16[384,4096]{1,0:T(8,128)(2,1)}, bf16[384,4096]{1,0:T(8,128)(2,1)S(1)}, u32[]{:S(2)}, u32[]{:S(2)}) collective-permute-start(bf16[384,4096]{1,0:T(8,128)(2,1)} %refs_6_.9), channel_id=1, source_target_pairs={{0,1},{1,0},{2,3},{3,2},{4,5},{5,4},{6,7},{7,6},{8,9},{9,8},{10,11... | collective-permute-start | bytes 9437192 | tf_op jit(solution)/shard_map/ppermute | solution.py:18
  6.0 21.9 %collective-permute-start = (bf16[32,4224]{1,0:T(8,128)(2,1)S(1)}, bf16[32,4224]{1,0:T(8,128)(2,1)S(1)}, u32[]{:S(2)}, u32[]{:S(2)}) collective-permute-start(bf16[32,4224]{1,0:T(8,128)(2,1)S(1)} %get-tuple-element.54), channel_id=1, source_target_pairs={{0,8},{1,9},{2,10},{3,11},{4,12},{5,13},{6,14},{7,15},{8,0},{9,1},... | collective-permute-start | bytes 811016 | tf_op jit(solution)/shard_map/ppermute | solution.py:18
  14.9 33.7 %copy-start = (bf16[4096,384]{1,0:T(8,128)(2,1)S(1)}, bf16[4096,384]{1,0:T(8,128)(2,1)}, u32[]{:S(2)}) copy-start(bf16[4096,384]{1,0:T(8,128)(2,1)} %refs_4_.9) | copy-start | bytes 9437188
  15.0 33.7 %copy-start.1 = (bf16[4096,384]{1,0:T(8,128)(2,1)S(1)}, bf16[4096,384]{1,0:T(8,128)(2,1)}, u32[]{:S(2)}) copy-start(bf16[4096,384]{1,0:T(8,128)(2,1)} %refs_5_.9) | copy-start | bytes 9437188
  15.0 33.7 %copy-start.2 = (bf16[384,4096]{1,0:T(8,128)(2,1)S(1)}, bf16[384,4096]{1,0:T(8,128)(2,1)}, u32[]{:S(2)}) copy-start(bf16[384,4096]{1,0:T(8,128)(2,1)} %refs_6_.9) | copy-start | bytes 9437188
  15.0 24.9 %collective-permute-start.8 = (bf16[32,4096]{1,0:T(8,128)(2,1)S(1)}, bf16[32,4096]{1,0:T(8,128)(2,1)S(1)}, u32[]{:S(2)}, u32[]{:S(2)}) collective-permute-start(bf16[32,4096]{1,0:T(8,128)(2,1)S(1)} %get-tuple-element.66), channel_id=1, source_target_pairs={{0,2},{1,3},{2,0},{3,1},{4,6},{5,7},{6,4},{7,5},{8,10},{9,11},{10,... | collective-permute-start | bytes 786440 | tf_op jit(solution)/shard_map/ppermute | solution.py:18
  18.0 24.4 %collective-permute-start.7 = (bf16[32,4224]{1,0:T(8,128)(2,1)S(1)}, bf16[32,4224]{1,0:T(8,128)(2,1)S(1)}, u32[]{:S(2)}, u32[]{:S(2)}) collective-permute-start(bf16[32,4224]{1,0:T(8,128)(2,1)S(1)} %get-tuple-element.65), channel_id=1, source_target_pairs={{0,8},{1,9},{2,10},{3,11},{4,12},{5,13},{6,14},{7,15},{8,0},{9,1},... | collective-permute-start | bytes 811016 | tf_op jit(solution)/shard_map/ppermute | solution.py:18
  20.6 20.8 %collective-permute-start.9 = (bf16[32,4096]{1,0:T(8,128)(2,1)S(1)}, bf16[32,4096]{1,0:T(8,128)(2,1)S(1)}, u32[]{:S(2)}, u32[]{:S(2)}) collective-permute-start(bf16[32,4096]{1,0:T(8,128)(2,1)S(1)} %get-tuple-element.67), channel_id=1, source_target_pairs={{0,4},{1,5},{2,6},{3,7},{4,0},{5,1},{6,2},{7,3},{8,12},{9,13},{10,... | collective-permute-start | bytes 786440 | tf_op jit(solution)/shard_map/ppermute | solution.py:18
  22.2 20.2 %collective-permute-start.10 = (bf16[32,4096]{1,0:T(8,128)(2,1)S(1)}, bf16[32,4096]{1,0:T(8,128)(2,1)S(1)}, u32[]{:S(2)}, u32[]{:S(2)}) collective-permute-start(bf16[32,4096]{1,0:T(8,128)(2,1)S(1)} %get-tuple-element.68), channel_id=1, source_target_pairs={{0,6},{1,7},{2,4},{3,5},{4,2},{5,3},{6,0},{7,1},{8,14},{9,15},{10,... | collective-permute-start | bytes 786440 | tf_op jit(solution)/shard_map/ppermute | solution.py:18
  28.4 5.6 %collective-permute-start.4 = (bf16[16,4096]{1,0:T(8,128)(2,1)S(1)}, bf16[16,4096]{1,0:T(8,128)(2,1)S(1)}, u32[]{:S(2)}, u32[]{:S(2)}) collective-permute-start(bf16[16,4096]{1,0:T(8,128)(2,1)S(1)} %get-tuple-element.62), channel_id=1, source_target_pairs={{0,2},{1,3},{2,0},{3,1},{4,6},{5,7},{6,4},{7,5},{8,10},{9,11},{10,... | collective-permute-start | bytes 393224 | tf_op jit(solution)/shard_map/ppermute | solution.py:18
  34.0 12.5 %collective-permute-start.5 = (bf16[16,4096]{1,0:T(8,128)(2,1)S(1)}, bf16[16,4096]{1,0:T(8,128)(2,1)S(1)}, u32[]{:S(2)}, u32[]{:S(2)}) collective-permute-start(bf16[16,4096]{1,0:T(8,128)(2,1)S(1)} %get-tuple-element.63), channel_id=1, source_target_pairs={{0,4},{1,5},{2,6},{3,7},{4,0},{5,1},{6,2},{7,3},{8,12},{9,13},{10,... | collective-permute-start | bytes 393224 | tf_op jit(solution)/shard_map/ppermute | solution.py:18
  39.9 8.7 %collective-permute-start.6 = (bf16[16,4096]{1,0:T(8,128)(2,1)S(1)}, bf16[16,4096]{1,0:T(8,128)(2,1)S(1)}, u32[]{:S(2)}, u32[]{:S(2)}) collective-permute-start(bf16[16,4096]{1,0:T(8,128)(2,1)S(1)} %get-tuple-element.64), channel_id=1, source_target_pairs={{0,6},{1,7},{2,4},{3,5},{4,2},{5,3},{6,0},{7,1},{8,14},{9,15},{10,... | collective-permute-start | bytes 393224 | tf_op jit(solution)/shard_map/ppermute | solution.py:18
  42.9 11.3 %collective-permute-start.14 = (bf16[16,4096]{1,0:T(8,128)(2,1)S(1)}, bf16[16,4096]{1,0:T(8,128)(2,1)S(1)}, u32[]{:S(2)}, u32[]{:S(2)}) collective-permute-start(bf16[16,4096]{1,0:T(8,128)(2,1)S(1)} %get-tuple-element.74), channel_id=1, source_target_pairs={{0,2},{1,3},{2,0},{3,1},{4,6},{5,7},{6,4},{7,5},{8,10},{9,11},{10,... | collective-permute-start | bytes 393224 | tf_op jit(solution)/shard_map/ppermute | solution.py:18
  43.4 12.2 %collective-permute-start.15 = (bf16[16,4096]{1,0:T(8,128)(2,1)S(1)}, bf16[16,4096]{1,0:T(8,128)(2,1)S(1)}, u32[]{:S(2)}, u32[]{:S(2)}) collective-permute-start(bf16[16,4096]{1,0:T(8,128)(2,1)S(1)} %get-tuple-element.75), channel_id=1, source_target_pairs={{0,4},{1,5},{2,6},{3,7},{4,0},{5,1},{6,2},{7,3},{8,12},{9,13},{10,... | collective-permute-start | bytes 393224 | tf_op jit(solution)/shard_map/ppermute | solution.py:18
  44.0 11.6 %collective-permute-start.16 = (bf16[16,4096]{1,0:T(8,128)(2,1)S(1)}, bf16[16,4096]{1,0:T(8,128)(2,1)S(1)}, u32[]{:S(2)}, u32[]{:S(2)}) collective-permute-start(bf16[16,4096]{1,0:T(8,128)(2,1)S(1)} %get-tuple-element.76), channel_id=1, source_target_pairs={{0,6},{1,7},{2,4},{3,5},{4,2},{5,3},{6,0},{7,1},{8,14},{9,15},{10,... | collective-permute-start | bytes 393224 | tf_op jit(solution)/shard_map/ppermute | solution.py:18
  52.1 9.2 %collective-permute-start.11 = (bf16[16,4096]{1,0:T(8,128)(2,1)S(1)}, bf16[16,4096]{1,0:T(8,128)(2,1)S(1)}, u32[]{:S(2)}, u32[]{:S(2)}) collective-permute-start(bf16[16,4096]{1,0:T(8,128)(2,1)S(1)} %get-tuple-element.71), channel_id=1, source_target_pairs={{0,2},{1,3},{2,0},{3,1},{4,6},{5,7},{6,4},{7,5},{8,10},{9,11},{10,... | collective-permute-start | bytes 393224 | tf_op jit(solution)/shard_map/ppermute | solution.py:18
  52.8 10.0 %collective-permute-start.12 = (bf16[16,4096]{1,0:T(8,128)(2,1)S(1)}, bf16[16,4096]{1,0:T(8,128)(2,1)S(1)}, u32[]{:S(2)}, u32[]{:S(2)}) collective-permute-start(bf16[16,4096]{1,0:T(8,128)(2,1)S(1)} %get-tuple-element.72), channel_id=1, source_target_pairs={{0,4},{1,5},{2,6},{3,7},{4,0},{5,1},{6,2},{7,3},{8,12},{9,13},{10,... | collective-permute-start | bytes 393224 | tf_op jit(solution)/shard_map/ppermute | solution.py:18
  54.1 8.7 %collective-permute-start.13 = (bf16[16,4096]{1,0:T(8,128)(2,1)S(1)}, bf16[16,4096]{1,0:T(8,128)(2,1)S(1)}, u32[]{:S(2)}, u32[]{:S(2)}) collective-permute-start(bf16[16,4096]{1,0:T(8,128)(2,1)S(1)} %get-tuple-element.73), channel_id=1, source_target_pairs={{0,6},{1,7},{2,4},{3,5},{4,2},{5,3},{6,0},{7,1},{8,14},{9,15},{10,... | collective-permute-start | bytes 393224 | tf_op jit(solution)/shard_map/ppermute | solution.py:18
  59.1 7.5 %collective-permute-start.18 = (bf16[16,4096]{1,0:T(8,128)(2,1)S(1)}, bf16[16,4096]{1,0:T(8,128)(2,1)S(1)}, u32[]{:S(2)}, u32[]{:S(2)}) collective-permute-start(bf16[16,4096]{1,0:T(8,128)(2,1)S(1)} %get-tuple-element.82), channel_id=1, source_target_pairs={{0,2},{1,3},{2,0},{3,1},{4,6},{5,7},{6,4},{7,5},{8,10},{9,11},{10,... | collective-permute-start | bytes 393224 | tf_op jit(solution)/shard_map/ppermute | solution.py:18
  60.0 6.5 %collective-permute-start.19 = (bf16[16,4096]{1,0:T(8,128)(2,1)S(1)}, bf16[16,4096]{1,0:T(8,128)(2,1)S(1)}, u32[]{:S(2)}, u32[]{:S(2)}) collective-permute-start(bf16[16,4096]{1,0:T(8,128)(2,1)S(1)} %get-tuple-element.83), channel_id=1, source_target_pairs={{0,4},{1,5},{2,6},{3,7},{4,0},{5,1},{6,2},{7,3},{8,12},{9,13},{10,... | collective-permute-start | bytes 393224 | tf_op jit(solution)/shard_map/ppermute | solution.py:18
  61.3 7.4 %collective-permute-start.20 = (bf16[16,4096]{1,0:T(8,128)(2,1)S(1)}, bf16[16,4096]{1,0:T(8,128)(2,1)S(1)}, u32[]{:S(2)}, u32[]{:S(2)}) collective-permute-start(bf16[16,4096]{1,0:T(8,128)(2,1)S(1)} %get-tuple-element.84), channel_id=1, source_target_pairs={{0,6},{1,7},{2,4},{3,5},{4,2},{5,3},{6,0},{7,1},{8,14},{9,15},{10,... | collective-permute-start | bytes 393224 | tf_op jit(solution)/shard_map/ppermute | solution.py:18
  63.4 12.5 %collective-permute-start.17 = (bf16[32,4096]{1,0:T(8,128)(2,1)S(1)}, bf16[32,4096]{1,0:T(8,128)(2,1)S(1)}, u32[]{:S(2)}, u32[]{:S(2)}) collective-permute-start(bf16[32,4096]{1,0:T(8,128)(2,1)S(1)} %relay_back.2.refs_10_), channel_id=1, source_target_pairs={{0,8},{1,9},{2,10},{3,11},{4,12},{5,13},{6,14},{7,15},{8,0},{9,1},... | collective-permute-start | bytes 786440 | tf_op jit(solution)/shard_map/ppermute | solution.py:18
  69.4 6.5 %collective-permute-start.21 = (bf16[32,4096]{1,0:T(8,128)(2,1)S(1)}, bf16[32,4096]{1,0:T(8,128)(2,1)S(1)}, u32[]{:S(2)}, u32[]{:S(2)}) collective-permute-start(bf16[32,4096]{1,0:T(8,128)(2,1)S(1)} %get-tuple-element.86), channel_id=1, source_target_pairs={{0,2},{1,3},{2,0},{3,1},{4,6},{5,7},{6,4},{7,5},{8,10},{9,11},{10,... | collective-permute-start | bytes 786440 | tf_op jit(solution)/shard_map/ppermute | solution.py:18
  69.9 15.4 %collective-permute-start.22 = (bf16[32,4096]{1,0:T(8,128)(2,1)S(1)}, bf16[32,4096]{1,0:T(8,128)(2,1)S(1)}, u32[]{:S(2)}, u32[]{:S(2)}) collective-permute-start(bf16[32,4096]{1,0:T(8,128)(2,1)S(1)} %get-tuple-element.87), channel_id=1, source_target_pairs={{0,4},{1,5},{2,6},{3,7},{4,0},{5,1},{6,2},{7,3},{8,12},{9,13},{10,... | collective-permute-start | bytes 786440 | tf_op jit(solution)/shard_map/ppermute | solution.py:18
  71.8 16.8 %collective-permute-start.23 = (bf16[32,4096]{1,0:T(8,128)(2,1)S(1)}, bf16[32,4096]{1,0:T(8,128)(2,1)S(1)}, u32[]{:S(2)}, u32[]{:S(2)}) collective-permute-start(bf16[32,4096]{1,0:T(8,128)(2,1)S(1)} %get-tuple-element.88), channel_id=1, source_target_pairs={{0,6},{1,7},{2,4},{3,5},{4,2},{5,3},{6,0},{7,1},{8,14},{9,15},{10,... | collective-permute-start | bytes 786440 | tf_op jit(solution)/shard_map/ppermute | solution.py:18
  73.0 16.6 %collective-permute-start.24 = (bf16[32,4096]{1,0:T(8,128)(2,1)S(1)}, bf16[32,4096]{1,0:T(8,128)(2,1)S(1)}, u32[]{:S(2)}, u32[]{:S(2)}) collective-permute-start(bf16[32,4096]{1,0:T(8,128)(2,1)S(1)} %relay_back.3.refs_4_), channel_id=1, source_target_pairs={{0,8},{1,9},{2,10},{3,11},{4,12},{5,13},{6,14},{7,15},{8,0},{9,1},... | collective-permute-start | bytes 786440 | tf_op jit(solution)/shard_map/ppermute | solution.py:18

commit v5 on v4

--- a/solution.py
+++ b/solution.py
@@ -302,7 +302,8 @@
     rows, width = ins[0].shape
     total = len(ins) * rows
     hidden = weights[0].shape[1]
-    block = min(total, 128)
+    block = 128
+    held = -(-total // block) * block
     part = 1024
     back = total // outs
     out = [jax.ShapeDtypeStruct((back, width), jnp.bfloat16)] * outs
@@ -313,6 +314,9 @@
         out_refs, (x_ref, y_ref) = refs[:outs], refs[outs:]
         for i in range(len(ins)):
             x_ref[i * rows : (i + 1) * rows, :] = in_refs[i][...]
+
+        if held > total:
+            x_ref[total:, :] = jnp.zeros((held - total, width), jnp.bfloat16)
 
         def rows_of(span):
             inners = []
@@ -328,11 +332,11 @@
                     jnp.bfloat16
                 )
 
-        if total == block:
+        if held == block:
             rows_of(slice(0, block))
         else:
 
-            @pl.loop(0, total // block)
+            @pl.loop(0, held // block)
             def _(r):
                 rows_of(pl.ds(pl.multiple_of(r * block, block), block))
 
@@ -345,7 +349,7 @@
             out_shape=out,
             in_specs=[whole(x) for x in ins] + [whole(w) for w in weights] + unread(after),
             out_specs=[whole(o) for o in out],
-            scratch_shapes=[VMEM((total, width), jnp.bfloat16)] * 2,
+            scratch_shapes=[VMEM((held, width), jnp.bfloat16)] * 2,
             compiler_params=params(24),
             cost_estimate=taking(microseconds),
             name="expert",
@@ -481,31 +485,37 @@
         resid.append(residual)
         normed.append(rows_c)
     far_rows = [exchange(normed[0], ep // 2)]
-    gate = passed(outgoing + normed[1:], list(weights[3:]), 0.3)
-    near = around(gate[:half])
-    far_rows += [exchange(x, ep // 2) for x in gate[half:]]
+    gate = passed(outgoing, list(weights[3:]), 0.3)
+    near = around(gate)
+    after = gate[:1]
+    for c in range(1, chunks):
+        after = passed([normed[c]], after, 0.3)
+        far_rows.append(exchange(after[0], ep // 2))
 
     placed = []
-    after = [gate[0]]
     for c in range(chunks):
         slotted, _ = relay(far_rows[c], top, half, cap, [], after, 0.5)
         placed.append(around(slotted))
-        after = [slotted[0], *near, placed[0][1]]
+        after = [slotted[0], *near]
     returned, after = [], after[:1]
     for c in range(chunks):
         outs = expert(placed[c], weights, half, after, 0.01)
         returned.append(around(outs))
         after = outs[:1]
-    far_back, near_out = [], None
+    far_back, near_back = [], [None] * half
     for c in range(chunks):
         if c == chunks - 1:
             near_out = expert(near, weights, half, after, 4)
-            after = near_out[:1]
+            near_back[0] = near_out[0]
+            after = passed(near_out[half - 1 :], near_out[:1], 0.1)
+            near_back[half - 1] = exchange(after[0], 2 * (half - 1))
         back = relay_back(returned[c], far_rows[c], top, cap, after, 0.6)
         far_back.append(exchange(back, ep // 2))
         after = [back]
-    near_back = around(passed(near_out, after, 0.1))
-    base = add_near(resid, far_back[:-1], near_back, info, cap, [], 4)
+    rest = passed(near_out[1 : half - 1], after, 0.1)
+    for d in range(1, half - 1):
+        near_back[d] = exchange(rest[d - 1], 2 * d)
+    base = add_near(resid, far_back[:-1], near_back, info, cap, rest[:1], 4)
     return add_far(base, far_back[-1])
 
 

time: 90.6 us -> 87.8 us (0.969)
  starting transfers between devices: 38.7 us -> 30.7 us
  waiting for transfers between devices: 28.4 us -> 34.8 us
  Pallas kernels: 22.5 us -> 21.3 us
    ppermute x25, starting transfers between devices: 38.7 us -> 30.7 us  [exchange(): lax.ppermute(value, 'ep', [(i, i ^ distance) for i in range(lax.axis_size...]
    ppermute x25, waiting for transfers between devices: 28.4 us -> 34.8 us  [exchange(): lax.ppermute(value, 'ep', [(i, i ^ distance) for i in range(lax.axis_size...]
    pallas_call x3, Pallas kernels: 9.62 us -> 8.4 us  [expert(): pl.pallas_call(body, out_shape=out, in_specs=[whole(x) for x in ins] + [w...]
  transfers between devices with their start and end apart: 25 -> 25, of which waited for: 9 -> 8; matrix products, arithmetic and copies ran while one was open for 0% -> 0% of each run, Pallas kernels for 24% -> 23%
where the time goes in v5:
time: 87.8 us; the launch traced here: 87.7 us
  waiting for transfers between devices  34.8 us (40%)
  starting transfers between devices  30.7 us (35%)
  Pallas kernels  21.3 us (24%)
    ppermute x25, waiting for transfers between devices, exchange(): lax.ppermute(value, 'ep', [(i, i ^ distance) for i in range(lax.axis_size...  34.8 us
    ppermute x25, starting transfers between devices, exchange(): lax.ppermute(value, 'ep', [(i, i ^ distance) for i in range(lax.axis_size...  30.7 us
    pallas_call x2, Pallas kernels, attend(): pl.pallas_call(body, out_shape=out_shape, in_specs=[pl.BlockSpec(memory_s...  8.77 us
    pallas_call x3, Pallas kernels, expert(): pl.pallas_call(body, out_shape=out, in_specs=[whole(x) for x in ins] + [w...  8.4 us
  transfers between devices with their start and end apart: 25, of which 8 were waited for; matrix products, arithmetic and copies ran while one was open for 0% of the time, Pallas kernels for 23%

profile of v5, /device:TPU:0, one launch (start us, length us, event | category | flops | bytes accessed | tf_op | source)
XLA Modules:
  0.0 87.7 jit_solution(1141344784767068386)
XLA Ops:
  1.6 4.4 %attend.2 = (f32[32,4096]{1,0:T(8,128)S(1)}, bf16[32,4224]{1,0:T(8,128)(2,1)S(1)}, bf16[16,4096]{1,0:T(8,128)(2,1)S(1)}, bf16[16,4096]{1,0:T(8,128)(2,1)S(1)}, b...) custom-call(s32[1]{0:T(128)S(6)} %copy.16.len_hbm, bf16[64,4096]{1,0:T(8,128)(2,1)} %refs_0_.3, ...), custom_call_target="tpu_custom_call" | custom-call | flops 1 | bytes 14000000 | tf_op jit(solution)/shard_map/attend/pallas_call | solution.py:226
  6.0 3.7 %collective-permute-start = (bf16[32,4224]{1,0:T(8,128)(2,1)S(1)}, bf16[32,4224]{1,0:T(8,128)(2,1)S(1)}, u32[]{:S(2)}, u32[]{:S(2)}) collective-permute-start(bf16[32,4224]{1,0:T(8,128)(2,1)S(1)} %get-tuple-element.51), channel_id=1, source_target_pairs={{0,8},{1,9},{2,10},{3,11},{4,12},{5,13},{6,14},{7,15},{8,0},{9,1},... | collective-permute-start | bytes 811016 | tf_op jit(solution)/shard_map/ppermute | solution.py:18
  9.7 4.4 %attend.3 = (f32[32,4096]{1,0:T(8,128)S(1)}, bf16[32,4224]{1,0:T(8,128)(2,1)S(1)}, bf16[32,4096]{1,0:T(8,128)(2,1)S(1)}, bf16[32,4096]{1,0:T(8,128)(2,1)S(1)}, b...) custom-call(s32[1]{0:T(128)S(6)} %copy.16.len_hbm, bf16[64,4096]{1,0:T(8,128)(2,1)} %refs_0_.3, ...), custom_call_target="tpu_custom_call" | custom-call | flops 1 | bytes 14000000 | tf_op jit(solution)/shard_map/attend/pallas_call | solution.py:226
  14.1 0.9 collective-permute-done.3.refs_6_.refs_9_
  15.0 3.0 %collective-permute-start.8 = (bf16[32,4096]{1,0:T(8,128)(2,1)S(1)}, bf16[32,4096]{1,0:T(8,128)(2,1)S(1)}, u32[]{:S(2)}, u32[]{:S(2)}) collective-permute-start(bf16[32,4096]{1,0:T(8,128)(2,1)S(1)} %get-tuple-element.62), channel_id=1, source_target_pairs={{0,2},{1,3},{2,0},{3,1},{4,6},{5,7},{6,4},{7,5},{8,10},{9,11},{10,... | collective-permute-start | bytes 786440 | tf_op jit(solution)/shard_map/ppermute | solution.py:18
  18.0 1.6 %collective-permute-start.9 = (bf16[32,4096]{1,0:T(8,128)(2,1)S(1)}, bf16[32,4096]{1,0:T(8,128)(2,1)S(1)}, u32[]{:S(2)}, u32[]{:S(2)}) collective-permute-start(bf16[32,4096]{1,0:T(8,128)(2,1)S(1)} %get-tuple-element.63), channel_id=1, source_target_pairs={{0,4},{1,5},{2,6},{3,7},{4,0},{5,1},{6,2},{7,3},{8,12},{9,13},{10,... | collective-permute-start | bytes 786440 | tf_op jit(solution)/shard_map/ppermute | solution.py:18
  19.6 2.7 %collective-permute-start.7 = (bf16[32,4224]{1,0:T(8,128)(2,1)S(1)}, bf16[32,4224]{1,0:T(8,128)(2,1)S(1)}, u32[]{:S(2)}, u32[]{:S(2)}) collective-permute-start(bf16[32,4224]{1,0:T(8,128)(2,1)S(1)} %passed.5.refs_0_), channel_id=1, source_target_pairs={{0,8},{1,9},{2,10},{3,11},{4,12},{5,13},{6,14},{7,15},{8,0},{9,1},... | collective-permute-start | bytes 811016 | tf_op jit(solution)/shard_map/ppermute | solution.py:18
  22.7 0.5 relay.2
  23.2 2.0 %collective-permute-start.4 = (bf16[16,4096]{1,0:T(8,128)(2,1)S(1)}, bf16[16,4096]{1,0:T(8,128)(2,1)S(1)}, u32[]{:S(2)}, u32[]{:S(2)}) collective-permute-start(bf16[16,4096]{1,0:T(8,128)(2,1)S(1)} %get-tuple-element.59), channel_id=1, source_target_pairs={{0,2},{1,3},{2,0},{3,1},{4,6},{5,7},{6,4},{7,5},{8,10},{9,11},{10,... | collective-permute-start | bytes 393224 | tf_op jit(solution)/shard_map/ppermute | solution.py:18
  25.2 1.2 %collective-permute-start.5 = (bf16[16,4096]{1,0:T(8,128)(2,1)S(1)}, bf16[16,4096]{1,0:T(8,128)(2,1)S(1)}, u32[]{:S(2)}, u32[]{:S(2)}) collective-permute-start(bf16[16,4096]{1,0:T(8,128)(2,1)S(1)} %get-tuple-element.60), channel_id=1, source_target_pairs={{0,4},{1,5},{2,6},{3,7},{4,0},{5,1},{6,2},{7,3},{8,12},{9,13},{10,... | collective-permute-start | bytes 393224 | tf_op jit(solution)/shard_map/ppermute | solution.py:18
  26.4 7.7 %collective-permute-done.9.refs_3_.refs_2_ = bf16[32,4096]{1,0:T(8,128)(2,1)S(1)} collective-permute-done((bf16[32,4096]{1,0:T(8,128)(2,1)S(1)}, bf16[32,4096]{1,0:T(8,128)(2,1)S(1)}, u32[]{:S(2)}, u32[]{:S(2)}) %collective-permute-start.9) | collective-permute-done | bytes 262176 | tf_op jit(solution)/shard_map/ppermute | solution.py:18
  34.1 6.6 %collective-permute-done.10.refs_4_.refs_3_ = bf16[32,4096]{1,0:T(8,128)(2,1)S(1)} collective-permute-done((bf16[32,4096]{1,0:T(8,128)(2,1)S(1)}, bf16[32,4096]{1,0:T(8,128)(2,1)S(1)}, u32[]{:S(2)}, u32[]{:S(2)}) %collective-permute-start.10) | collective-permute-done | bytes 262176 | tf_op jit(solution)/shard_map/ppermute | solution.py:18
  40.7 0.5 relay.3
  41.2 0.5 collective-permute-start.14
  42.3 2.5 %collective-permute-start.16 = (bf16[16,4096]{1,0:T(8,128)(2,1)S(1)}, bf16[16,4096]{1,0:T(8,128)(2,1)S(1)}, u32[]{:S(2)}, u32[]{:S(2)}) collective-permute-start(bf16[16,4096]{1,0:T(8,128)(2,1)S(1)} %get-tuple-element.72), channel_id=1, source_target_pairs={{0,6},{1,7},{2,4},{3,5},{4,2},{5,3},{6,0},{7,1},{8,14},{9,15},{10,... | collective-permute-start | bytes 393224 | tf_op jit(solution)/shard_map/ppermute | solution.py:18
  44.8 1.6 %collective-permute-done.6.refs_3_ = bf16[16,4096]{1,0:T(8,128)(2,1)S(1)} collective-permute-done((bf16[16,4096]{1,0:T(8,128)(2,1)S(1)}, bf16[16,4096]{1,0:T(8,128)(2,1)S(1)}, u32[]{:S(2)}, u32[]{:S(2)}) %collective-permute-start.6) | collective-permute-done | bytes 131104 | tf_op jit(solution)/shard_map/ppermute | solution.py:18
  46.4 2.7 %expert.3 = (bf16[16,4096]{1,0:T(8,128)(2,1)S(1)}, bf16[16,4096]{1,0:T(8,128)(2,1)S(1)}, bf16[16,4096]{1,0:T(8,128)(2,1)S(1)}, bf16[16,4096]{1,0:T(8,128)(2,1)S(1)}) custom-call(bf16[16,4096]{1,0:T(8,128)(2,1)S(1)} %get-tuple-element.58.refs_0_, bf16[16,4096]{1,0:T(8,128)(2,1)S(1)} %collective-permute-done.4.refs_1_, ...), custom_call_target="tpu_custom_call" | custom-call | flops 1 | bytes 35000 | tf_op jit(solution)/shard_map/expert/pallas_call | solution.py:347
  49.1 0.5 collective-permute-start.11
  49.7 3.0 %collective-permute-start.13 = (bf16[16,4096]{1,0:T(8,128)(2,1)S(1)}, bf16[16,4096]{1,0:T(8,128)(2,1)S(1)}, u32[]{:S(2)}, u32[]{:S(2)}) collective-permute-start(bf16[16,4096]{1,0:T(8,128)(2,1)S(1)} %get-tuple-element.69), channel_id=1, source_target_pairs={{0,6},{1,7},{2,4},{3,5},{4,2},{5,3},{6,0},{7,1},{8,14},{9,15},{10,... | collective-permute-start | bytes 393224 | tf_op jit(solution)/shard_map/ppermute | solution.py:18
  52.7 2.9 %expert.4 = (bf16[16,4096]{1,0:T(8,128)(2,1)S(1)}, bf16[16,4096]{1,0:T(8,128)(2,1)S(1)}, bf16[16,4096]{1,0:T(8,128)(2,1)S(1)}, bf16[16,4096]{1,0:T(8,128)(2,1)S(1)}) custom-call(bf16[16,4096]{1,0:T(8,128)(2,1)S(1)} %get-tuple-element.65.refs_10_.refs_0_, bf16[16,4096]{1,0:T(8,128)(2,1)S(1)} %collective-permute-done.14.refs_1_, ...), custom_call_target="tpu_custom_call" | custom-call | flops 1 | bytes 35000 | tf_op jit(solution)/shard_map/expert/pallas_call | solution.py:347
  55.6 0.5 collective-permute-start.18
  56.3 2.9 %collective-permute-start.20 = (bf16[16,4096]{1,0:T(8,128)(2,1)S(1)}, bf16[16,4096]{1,0:T(8,128)(2,1)S(1)}, u32[]{:S(2)}, u32[]{:S(2)}) collective-permute-start(bf16[16,4096]{1,0:T(8,128)(2,1)S(1)} %get-tuple-element.79), channel_id=1, source_target_pairs={{0,6},{1,7},{2,4},{3,5},{4,2},{5,3},{6,0},{7,1},{8,14},{9,15},{10,... | collective-permute-start | bytes 393224 | tf_op jit(solution)/shard_map/ppermute | solution.py:18
  59.2 0.6 relay_back.2.refs_10_
  59.8 2.1 %collective-permute-start.17 = (bf16[32,4096]{1,0:T(8,128)(2,1)S(1)}, bf16[32,4096]{1,0:T(8,128)(2,1)S(1)}, u32[]{:S(2)}, u32[]{:S(2)}) collective-permute-start(bf16[32,4096]{1,0:T(8,128)(2,1)S(1)} %relay_back.2.refs_10_), channel_id=1, source_target_pairs={{0,8},{1,9},{2,10},{3,11},{4,12},{5,13},{6,14},{7,15},{8,0},{9,1},... | collective-permute-start | bytes 786440 | tf_op jit(solution)/shard_map/ppermute | solution.py:18
  61.9 2.7 %expert.5 = (bf16[32,4096]{1,0:T(8,128)(2,1)S(1)}, bf16[32,4096]{1,0:T(8,128)(2,1)S(1)}, bf16[32,4096]{1,0:T(8,128)(2,1)S(1)}, bf16[32,4096]{1,0:T(8,128)(2,1)S(1)}) custom-call(bf16[32,4096]{1,0:T(8,128)(2,1)S(1)} %get-tuple-element.57.refs_1_.refs_0_, bf16[32,4096]{1,0:T(8,128)(2,1)S(1)} %collective-permute-done.8.refs_2_.refs_1_, ...), custom_call_target="tpu_custom_call" | custom-call | flops 1 | bytes 14000000 | tf_op jit(solution)/shard_map/expert/pallas_call | solution.py:347
  64.7 2.1 %collective-permute-start.23 = (bf16[32,4096]{1,0:T(8,128)(2,1)S(1)}, bf16[32,4096]{1,0:T(8,128)(2,1)S(1)}, u32[]{:S(2)}, u32[]{:S(2)}) collective-permute-start(bf16[32,4096]{1,0:T(8,128)(2,1)S(1)} %passed.6.refs_4_), channel_id=1, source_target_pairs={{0,6},{1,7},{2,4},{3,5},{4,2},{5,3},{6,0},{7,1},{8,14},{9,15},{10,... | collective-permute-start | bytes 786440 | tf_op jit(solution)/shard_map/ppermute | solution.py:18
  66.7 3.7 %collective-permute-done.20.refs_3_ = bf16[16,4096]{1,0:T(8,128)(2,1)S(1)} collective-permute-done((bf16[16,4096]{1,0:T(8,128)(2,1)S(1)}, bf16[16,4096]{1,0:T(8,128)(2,1)S(1)}, u32[]{:S(2)}, u32[]{:S(2)}) %collective-permute-start.20) | collective-permute-done | bytes 131104 | tf_op jit(solution)/shard_map/ppermute | solution.py:18
  70.5 0.6 relay_back.3.refs_2_
  71.7 11.0 %collective-permute-done.23.refs_6_ = bf16[32,4096]{1,0:T(8,128)(2,1)S(1)} collective-permute-done((bf16[32,4096]{1,0:T(8,128)(2,1)S(1)}, bf16[32,4096]{1,0:T(8,128)(2,1)S(1)}, u32[]{:S(2)}, u32[]{:S(2)}) %collective-permute-start.23) | collective-permute-done | bytes 262176 | tf_op jit(solution)/shard_map/ppermute | solution.py:18
  82.7 3.1 %collective-permute-done.22.refs_5_ = bf16[32,4096]{1,0:T(8,128)(2,1)S(1)} collective-permute-done((bf16[32,4096]{1,0:T(8,128)(2,1)S(1)}, bf16[32,4096]{1,0:T(8,128)(2,1)S(1)}, u32[]{:S(2)}, u32[]{:S(2)}) %collective-permute-start.22) | collective-permute-done | bytes 262176 | tf_op jit(solution)/shard_map/ppermute | solution.py:18
  85.8 0.9 %add_near.1.base_ref = f32[64,4096]{1,0:T(8,128)S(1)} custom-call(f32[4,64]{1,0:T(4,128)S(1)} %get-tuple-element.44.info_ref, f32[32,4096]{1,0:T(8,128)S(1)} %get-tuple-element.45.refs_0_, f32[32,4096]{1,0:T(8,128)S(1)} %get-tuple-element.50.refs_1_, bf16[32,4096]{1,0:T(8,128)(2,1)S(1)} %collective-permute-done.17.refs_2_, ...), custom_call_target="tpu_custom_call" | custom-call | flops 1 | bytes 14000000 | tf_op jit(solution)/shard_map/add_near/pallas_call | solution.py:401
  86.8 0.9 %add_far.1 = bf16[64,4096]{1,0:T(8,128)(2,1)} custom-call(f32[64,4096]{1,0:T(8,128)S(1)} %add_near.1.base_ref, bf16[32,4096]{1,0:T(8,128)(2,1)S(1)} %collective-permute-done.24.far_ref), custom_call_target="tpu_custom_call" | custom-call | flops 1 | bytes 3500000 | tf_op jit(solution)/shard_map/add_far/pallas_call | solution.py:423
  (39 shorter events, 2.8 us)
Async XLA Ops:
  0.0 14.1 %collective-permute-start.1 = (bf16[4096,384]{1,0:T(8,128)(2,1)}, bf16[4096,384]{1,0:T(8,128)(2,1)S(1)}, u32[]{:S(2)}, u32[]{:S(2)}) collective-permute-start(bf16[4096,384]{1,0:T(8,128)(2,1)} %refs_4_.9), channel_id=1, source_target_pairs={{0,1},{1,0},{2,3},{3,2},{4,5},{5,4},{6,7},{7,6},{8,9},{9,8},{10,11... | collective-permute-start | bytes 9437192 | tf_op jit(solution)/shard_map/ppermute | solution.py:18
  0.5 13.6 %collective-permute-start.2 = (bf16[4096,384]{1,0:T(8,128)(2,1)}, bf16[4096,384]{1,0:T(8,128)(2,1)S(1)}, u32[]{:S(2)}, u32[]{:S(2)}) collective-permute-start(bf16[4096,384]{1,0:T(8,128)(2,1)} %refs_5_.9), channel_id=1, source_target_pairs={{0,1},{1,0},{2,3},{3,2},{4,5},{5,4},{6,7},{7,6},{8,9},{9,8},{10,11... | collective-permute-start | bytes 9437192 | tf_op jit(solution)/shard_map/ppermute | solution.py:18
  0.5 14.4 %collective-permute-start.3 = (bf16[384,4096]{1,0:T(8,128)(2,1)}, bf16[384,4096]{1,0:T(8,128)(2,1)S(1)}, u32[]{:S(2)}, u32[]{:S(2)}) collective-permute-start(bf16[384,4096]{1,0:T(8,128)(2,1)} %refs_6_.9), channel_id=1, source_target_pairs={{0,1},{1,0},{2,3},{3,2},{4,5},{5,4},{6,7},{7,6},{8,9},{9,8},{10,11... | collective-permute-start | bytes 9437192 | tf_op jit(solution)/shard_map/ppermute | solution.py:18
  6.0 16.7 %collective-permute-start = (bf16[32,4224]{1,0:T(8,128)(2,1)S(1)}, bf16[32,4224]{1,0:T(8,128)(2,1)S(1)}, u32[]{:S(2)}, u32[]{:S(2)}) collective-permute-start(bf16[32,4224]{1,0:T(8,128)(2,1)S(1)} %get-tuple-element.51), channel_id=1, source_target_pairs={{0,8},{1,9},{2,10},{3,11},{4,12},{5,13},{6,14},{7,15},{8,0},{9,1},... | collective-permute-start | bytes 811016 | tf_op jit(solution)/shard_map/ppermute | solution.py:18
  14.9 31.4 %copy-start = (bf16[4096,384]{1,0:T(8,128)(2,1)S(1)}, bf16[4096,384]{1,0:T(8,128)(2,1)}, u32[]{:S(2)}) copy-start(bf16[4096,384]{1,0:T(8,128)(2,1)} %refs_4_.9) | copy-start | bytes 9437188
  15.0 31.4 %copy-start.1 = (bf16[4096,384]{1,0:T(8,128)(2,1)S(1)}, bf16[4096,384]{1,0:T(8,128)(2,1)}, u32[]{:S(2)}) copy-start(bf16[4096,384]{1,0:T(8,128)(2,1)} %refs_5_.9) | copy-start | bytes 9437188
  15.0 31.4 %copy-start.2 = (bf16[384,4096]{1,0:T(8,128)(2,1)S(1)}, bf16[384,4096]{1,0:T(8,128)(2,1)}, u32[]{:S(2)}) copy-start(bf16[384,4096]{1,0:T(8,128)(2,1)} %refs_6_.9) | copy-start | bytes 9437188
  15.0 10.2 %collective-permute-start.8 = (bf16[32,4096]{1,0:T(8,128)(2,1)S(1)}, bf16[32,4096]{1,0:T(8,128)(2,1)S(1)}, u32[]{:S(2)}, u32[]{:S(2)}) collective-permute-start(bf16[32,4096]{1,0:T(8,128)(2,1)S(1)} %get-tuple-element.62), channel_id=1, source_target_pairs={{0,2},{1,3},{2,0},{3,1},{4,6},{5,7},{6,4},{7,5},{8,10},{9,11},{10,... | collective-permute-start | bytes 786440 | tf_op jit(solution)/shard_map/ppermute | solution.py:18
  18.0 16.1 %collective-permute-start.9 = (bf16[32,4096]{1,0:T(8,128)(2,1)S(1)}, bf16[32,4096]{1,0:T(8,128)(2,1)S(1)}, u32[]{:S(2)}, u32[]{:S(2)}) collective-permute-start(bf16[32,4096]{1,0:T(8,128)(2,1)S(1)} %get-tuple-element.63), channel_id=1, source_target_pairs={{0,4},{1,5},{2,6},{3,7},{4,0},{5,1},{6,2},{7,3},{8,12},{9,13},{10,... | collective-permute-start | bytes 786440 | tf_op jit(solution)/shard_map/ppermute | solution.py:18
  19.6 21.1 %collective-permute-start.7 = (bf16[32,4224]{1,0:T(8,128)(2,1)S(1)}, bf16[32,4224]{1,0:T(8,128)(2,1)S(1)}, u32[]{:S(2)}, u32[]{:S(2)}) collective-permute-start(bf16[32,4224]{1,0:T(8,128)(2,1)S(1)} %passed.5.refs_0_), channel_id=1, source_target_pairs={{0,8},{1,9},{2,10},{3,11},{4,12},{5,13},{6,14},{7,15},{8,0},{9,1},... | collective-permute-start | bytes 811016 | tf_op jit(solution)/shard_map/ppermute | solution.py:18
  22.2 18.5 %collective-permute-start.10 = (bf16[32,4096]{1,0:T(8,128)(2,1)S(1)}, bf16[32,4096]{1,0:T(8,128)(2,1)S(1)}, u32[]{:S(2)}, u32[]{:S(2)}) collective-permute-start(bf16[32,4096]{1,0:T(8,128)(2,1)S(1)} %get-tuple-element.64), channel_id=1, source_target_pairs={{0,6},{1,7},{2,4},{3,5},{4,2},{5,3},{6,0},{7,1},{8,14},{9,15},{10,... | collective-permute-start | bytes 786440 | tf_op jit(solution)/shard_map/ppermute | solution.py:18
  23.2 19.0 %collective-permute-start.4 = (bf16[16,4096]{1,0:T(8,128)(2,1)S(1)}, bf16[16,4096]{1,0:T(8,128)(2,1)S(1)}, u32[]{:S(2)}, u32[]{:S(2)}) collective-permute-start(bf16[16,4096]{1,0:T(8,128)(2,1)S(1)} %get-tuple-element.59), channel_id=1, source_target_pairs={{0,2},{1,3},{2,0},{3,1},{4,6},{5,7},{6,4},{7,5},{8,10},{9,11},{10,... | collective-permute-start | bytes 393224 | tf_op jit(solution)/shard_map/ppermute | solution.py:18
  25.2 19.6 %collective-permute-start.5 = (bf16[16,4096]{1,0:T(8,128)(2,1)S(1)}, bf16[16,4096]{1,0:T(8,128)(2,1)S(1)}, u32[]{:S(2)}, u32[]{:S(2)}) collective-permute-start(bf16[16,4096]{1,0:T(8,128)(2,1)S(1)} %get-tuple-element.60), channel_id=1, source_target_pairs={{0,4},{1,5},{2,6},{3,7},{4,0},{5,1},{6,2},{7,3},{8,12},{9,13},{10,... | collective-permute-start | bytes 393224 | tf_op jit(solution)/shard_map/ppermute | solution.py:18
  34.1 12.3 %collective-permute-start.6 = (bf16[16,4096]{1,0:T(8,128)(2,1)S(1)}, bf16[16,4096]{1,0:T(8,128)(2,1)S(1)}, u32[]{:S(2)}, u32[]{:S(2)}) collective-permute-start(bf16[16,4096]{1,0:T(8,128)(2,1)S(1)} %get-tuple-element.61), channel_id=1, source_target_pairs={{0,6},{1,7},{2,4},{3,5},{4,2},{5,3},{6,0},{7,1},{8,14},{9,15},{10,... | collective-permute-start | bytes 393224 | tf_op jit(solution)/shard_map/ppermute | solution.py:18
  41.2 8.5 %collective-permute-start.14 = (bf16[16,4096]{1,0:T(8,128)(2,1)S(1)}, bf16[16,4096]{1,0:T(8,128)(2,1)S(1)}, u32[]{:S(2)}, u32[]{:S(2)}) collective-permute-start(bf16[16,4096]{1,0:T(8,128)(2,1)S(1)} %get-tuple-element.70), channel_id=1, source_target_pairs={{0,2},{1,3},{2,0},{3,1},{4,6},{5,7},{6,4},{7,5},{8,10},{9,11},{10,... | collective-permute-start | bytes 393224 | tf_op jit(solution)/shard_map/ppermute | solution.py:18
  41.8 10.9 %collective-permute-start.15 = (bf16[16,4096]{1,0:T(8,128)(2,1)S(1)}, bf16[16,4096]{1,0:T(8,128)(2,1)S(1)}, u32[]{:S(2)}, u32[]{:S(2)}) collective-permute-start(bf16[16,4096]{1,0:T(8,128)(2,1)S(1)} %get-tuple-element.71), channel_id=1, source_target_pairs={{0,4},{1,5},{2,6},{3,7},{4,0},{5,1},{6,2},{7,3},{8,12},{9,13},{10,... | collective-permute-start | bytes 393224 | tf_op jit(solution)/shard_map/ppermute | solution.py:18
  42.3 10.4 %collective-permute-start.16 = (bf16[16,4096]{1,0:T(8,128)(2,1)S(1)}, bf16[16,4096]{1,0:T(8,128)(2,1)S(1)}, u32[]{:S(2)}, u32[]{:S(2)}) collective-permute-start(bf16[16,4096]{1,0:T(8,128)(2,1)S(1)} %get-tuple-element.72), channel_id=1, source_target_pairs={{0,6},{1,7},{2,4},{3,5},{4,2},{5,3},{6,0},{7,1},{8,14},{9,15},{10,... | collective-permute-start | bytes 393224 | tf_op jit(solution)/shard_map/ppermute | solution.py:18
  49.1 7.2 %collective-permute-start.11 = (bf16[16,4096]{1,0:T(8,128)(2,1)S(1)}, bf16[16,4096]{1,0:T(8,128)(2,1)S(1)}, u32[]{:S(2)}, u32[]{:S(2)}) collective-permute-start(bf16[16,4096]{1,0:T(8,128)(2,1)S(1)} %get-tuple-element.67), channel_id=1, source_target_pairs={{0,2},{1,3},{2,0},{3,1},{4,6},{5,7},{6,4},{7,5},{8,10},{9,11},{10,... | collective-permute-start | bytes 393224 | tf_op jit(solution)/shard_map/ppermute | solution.py:18
  49.7 9.5 %collective-permute-start.12 = (bf16[16,4096]{1,0:T(8,128)(2,1)S(1)}, bf16[16,4096]{1,0:T(8,128)(2,1)S(1)}, u32[]{:S(2)}, u32[]{:S(2)}) collective-permute-start(bf16[16,4096]{1,0:T(8,128)(2,1)S(1)} %get-tuple-element.68), channel_id=1, source_target_pairs={{0,4},{1,5},{2,6},{3,7},{4,0},{5,1},{6,2},{7,3},{8,12},{9,13},{10,... | collective-permute-start | bytes 393224 | tf_op jit(solution)/shard_map/ppermute | solution.py:18
  49.7 9.5 %collective-permute-start.13 = (bf16[16,4096]{1,0:T(8,128)(2,1)S(1)}, bf16[16,4096]{1,0:T(8,128)(2,1)S(1)}, u32[]{:S(2)}, u32[]{:S(2)}) collective-permute-start(bf16[16,4096]{1,0:T(8,128)(2,1)S(1)} %get-tuple-element.69), channel_id=1, source_target_pairs={{0,6},{1,7},{2,4},{3,5},{4,2},{5,3},{6,0},{7,1},{8,14},{9,15},{10,... | collective-permute-start | bytes 393224 | tf_op jit(solution)/shard_map/ppermute | solution.py:18
  55.6 11.1 %collective-permute-start.18 = (bf16[16,4096]{1,0:T(8,128)(2,1)S(1)}, bf16[16,4096]{1,0:T(8,128)(2,1)S(1)}, u32[]{:S(2)}, u32[]{:S(2)}) collective-permute-start(bf16[16,4096]{1,0:T(8,128)(2,1)S(1)} %get-tuple-element.77), channel_id=1, source_target_pairs={{0,2},{1,3},{2,0},{3,1},{4,6},{5,7},{6,4},{7,5},{8,10},{9,11},{10,... | collective-permute-start | bytes 393224 | tf_op jit(solution)/shard_map/ppermute | solution.py:18
  56.2 10.6 %collective-permute-start.19 = (bf16[16,4096]{1,0:T(8,128)(2,1)S(1)}, bf16[16,4096]{1,0:T(8,128)(2,1)S(1)}, u32[]{:S(2)}, u32[]{:S(2)}) collective-permute-start(bf16[16,4096]{1,0:T(8,128)(2,1)S(1)} %get-tuple-element.78), channel_id=1, source_target_pairs={{0,4},{1,5},{2,6},{3,7},{4,0},{5,1},{6,2},{7,3},{8,12},{9,13},{10,... | collective-permute-start | bytes 393224 | tf_op jit(solution)/shard_map/ppermute | solution.py:18
  56.3 14.2 %collective-permute-start.20 = (bf16[16,4096]{1,0:T(8,128)(2,1)S(1)}, bf16[16,4096]{1,0:T(8,128)(2,1)S(1)}, u32[]{:S(2)}, u32[]{:S(2)}) collective-permute-start(bf16[16,4096]{1,0:T(8,128)(2,1)S(1)} %get-tuple-element.79), channel_id=1, source_target_pairs={{0,6},{1,7},{2,4},{3,5},{4,2},{5,3},{6,0},{7,1},{8,14},{9,15},{10,... | collective-permute-start | bytes 393224 | tf_op jit(solution)/shard_map/ppermute | solution.py:18
  59.8 22.9 %collective-permute-start.17 = (bf16[32,4096]{1,0:T(8,128)(2,1)S(1)}, bf16[32,4096]{1,0:T(8,128)(2,1)S(1)}, u32[]{:S(2)}, u32[]{:S(2)}) collective-permute-start(bf16[32,4096]{1,0:T(8,128)(2,1)S(1)} %relay_back.2.refs_10_), channel_id=1, source_target_pairs={{0,8},{1,9},{2,10},{3,11},{4,12},{5,13},{6,14},{7,15},{8,0},{9,1},... | collective-permute-start | bytes 786440 | tf_op jit(solution)/shard_map/ppermute | solution.py:18
  64.7 18.0 %collective-permute-start.23 = (bf16[32,4096]{1,0:T(8,128)(2,1)S(1)}, bf16[32,4096]{1,0:T(8,128)(2,1)S(1)}, u32[]{:S(2)}, u32[]{:S(2)}) collective-permute-start(bf16[32,4096]{1,0:T(8,128)(2,1)S(1)} %passed.6.refs_4_), channel_id=1, source_target_pairs={{0,6},{1,7},{2,4},{3,5},{4,2},{5,3},{6,0},{7,1},{8,14},{9,15},{10,... | collective-permute-start | bytes 786440 | tf_op jit(solution)/shard_map/ppermute | solution.py:18
  71.1 14.7 %collective-permute-start.22 = (bf16[32,4096]{1,0:T(8,128)(2,1)S(1)}, bf16[32,4096]{1,0:T(8,128)(2,1)S(1)}, u32[]{:S(2)}, u32[]{:S(2)}) collective-permute-start(bf16[32,4096]{1,0:T(8,128)(2,1)S(1)} %get-tuple-element.82), channel_id=1, source_target_pairs={{0,4},{1,5},{2,6},{3,7},{4,0},{5,1},{6,2},{7,3},{8,12},{9,13},{10,... | collective-permute-start | bytes 786440 | tf_op jit(solution)/shard_map/ppermute | solution.py:18
  71.2 14.6 %collective-permute-start.21 = (bf16[32,4096]{1,0:T(8,128)(2,1)S(1)}, bf16[32,4096]{1,0:T(8,128)(2,1)S(1)}, u32[]{:S(2)}, u32[]{:S(2)}) collective-permute-start(bf16[32,4096]{1,0:T(8,128)(2,1)S(1)} %get-tuple-element.81.refs_7_), channel_id=1, source_target_pairs={{0,2},{1,3},{2,0},{3,1},{4,6},{5,7},{6,4},{7,5},{8,10},{9,11},{10,... | collective-permute-start | bytes 786440 | tf_op jit(solution)/shard_map/ppermute | solution.py:18
  71.3 15.5 %collective-permute-start.24 = (bf16[32,4096]{1,0:T(8,128)(2,1)S(1)}, bf16[32,4096]{1,0:T(8,128)(2,1)S(1)}, u32[]{:S(2)}, u32[]{:S(2)}) collective-permute-start(bf16[32,4096]{1,0:T(8,128)(2,1)S(1)} %relay_back.3.refs_2_), channel_id=1, source_target_pairs={{0,8},{1,9},{2,10},{3,11},{4,12},{5,13},{6,14},{7,15},{8,0},{9,1},... | collective-permute-start | bytes 786440 | tf_op jit(solution)/shard_map/ppermute | solution.py:18

commit v6 on v5

--- a/solution.py
+++ b/solution.py
@@ -133,12 +133,12 @@
     mine = pl.ds(chunk * rows, rows)
     per = max(1, min(group, 256 // rows))
     block = per * rows
-    near_rows = cap * chunks if last else cap
     out_shape = [
         jax.ShapeDtypeStruct((rows, width), jnp.float32),
         jax.ShapeDtypeStruct((rows, width + ROUTE), jnp.bfloat16),
     ]
-    out_shape += [jax.ShapeDtypeStruct((near_rows, width), jnp.bfloat16)] * half
+    if last:
+        out_shape += [jax.ShapeDtypeStruct((cap * chunks, width), jnp.bfloat16)] * half
     if first:
         out_shape.append(jax.ShapeDtypeStruct((2 * top, token_rows), jnp.float32))
 
@@ -148,7 +148,7 @@
         outs, scratch = refs[: len(out_shape)], refs[len(out_shape) :]
         (q_ref, hid_ref, sk_ref, sv_ref, tk_ref, tv_ref, qg_ref, kg_ref, ng_ref, ids_ref, gates_ref) = scratch[:11]
         kn_ref, vx_ref, qs_ref, info_ref, len_ref, sems = scratch[11:]
-        resid_ref, normed_ref, out_refs = outs[0], outs[1], outs[2 : 2 + half]
+        resid_ref, normed_ref, out_refs = outs[0], outs[1], outs[2 : 2 + half] if last else []
         copies = []
         for i in range(11):
             source = hbm[i].at[mine, :] if i < 2 else hbm[i]
@@ -218,10 +218,14 @@
         route = info_ref[:, chunk * rows : (chunk + 1) * rows]
         normed_ref[:, :width] = normed
         normed_ref[:, width:] = pack_route(route, ROUTE)
-        tail = slice(near_rows - cap, near_rows)
-        spread_rows(route, normed, [o.at[tail, :] for o in out_refs], cap)
-        for i in range(len(before)):
-            out_refs[i][: near_rows - cap, :] = carried[i][...]
+        if last:
+            for c in range(chunks):
+                spread_rows(
+                    info_ref[:, c * rows : (c + 1) * rows],
+                    carried[c][:, :width] if c < len(carried) else normed,
+                    [o.at[c * cap : (c + 1) * cap, :] for o in out_refs],
+                    cap,
+                )
 
     results = pl.pallas_call(
         body,
@@ -253,7 +257,7 @@
         cost_estimate=taking(4),
         name="attend",
     )(cache_len, *arrays, *before)
-    return results[0], results[1], list(results[2 : 2 + half]), (results[-1] if first else None)
+    return results[0], results[1], list(results[2 : 2 + half]) if last else [], (results[-1] if first else None)
 
 
 def relay(rows_in, top, half, cap, carried, after, microseconds):
@@ -480,7 +484,7 @@
 
     resid, normed, outgoing, info = [], [], [], None
     for c in range(chunks):
-        residual, rows_c, outgoing, packed = attend(cache_len, arrays, outgoing, c, chunks, half, cap)
+        residual, rows_c, outgoing, packed = attend(cache_len, arrays, normed, c, chunks, half, cap)
         info = packed if c == 0 else info
         resid.append(residual)
         normed.append(rows_c)

time: 87.8 us -> 87.4 us (level)
  transfers between devices with their start and end apart: 25 -> 25, of which waited for: 8 -> 7; matrix products, arithmetic and copies ran while one was open for 0% -> 0% of each run, Pallas kernels for 23% -> 23%
where the time goes in v6:
time: 87.4 us; the launch traced here: 87.3 us
  waiting for transfers between devices  34.8 us (40%)
  starting transfers between devices  30.9 us (35%)
  Pallas kernels  20.8 us (24%)
    ppermute x25, waiting for transfers between devices, exchange(): lax.ppermute(value, 'ep', [(i, i ^ distance) for i in range(lax.axis_size...  34.8 us
    ppermute x25, starting transfers between devices, exchange(): lax.ppermute(value, 'ep', [(i, i ^ distance) for i in range(lax.axis_size...  30.9 us
    pallas_call x3, Pallas kernels, expert(): pl.pallas_call(body, out_shape=out, in_specs=[whole(x) for x in ins] + [w...  8.32 us
    pallas_call x2, Pallas kernels, attend(): pl.pallas_call(body, out_shape=out_shape, in_specs=[pl.BlockSpec(memory_s...  8.3 us
  transfers between devices with their start and end apart: 25, of which 7 were waited for; matrix products, arithmetic and copies ran while one was open for 0% of the time, Pallas kernels for 23%

profile of v6, /device:TPU:0, one launch (start us, length us, event | category | flops | bytes accessed | tf_op | source)
XLA Modules:
  0.0 87.3 jit_solution(18046029885602852057)
XLA Ops:
  1.6 4.0 %attend.2 = (f32[32,4096]{1,0:T(8,128)S(1)}, bf16[32,4224]{1,0:T(8,128)(2,1)S(1)}, f32[4,64]{1,0:T(4,128)S(1)}) custom-call(s32[1]{0:T(128)S(6)} %copy.16.len_hbm, bf16[64,4096]{1,0:T(8,128)(2,1)} %refs_0_.3, bf16[64,4096]{1,0:T(8,128)(2,1)} %refs_1_.3, bf16[1024,256]{1,0:T(8,128)(2,1)} %refs_2_.3, bf16[1024,256]{1,0:T(8,128)(2,1)} %refs_3_.3, ...), custom_call_target="tpu_custom_call" | custom-call | flops 1 | bytes 14000000 | tf_op jit(solution)/shard_map/attend/pallas_call | solution.py:230
  5.7 3.7 %collective-permute-start = (bf16[32,4224]{1,0:T(8,128)(2,1)S(1)}, bf16[32,4224]{1,0:T(8,128)(2,1)S(1)}, u32[]{:S(2)}, u32[]{:S(2)}) collective-permute-start(bf16[32,4224]{1,0:T(8,128)(2,1)S(1)} %get-tuple-element.42.refs_11_), channel_id=1, source_target_pairs={{0,8},{1,9},{2,10},{3,11},{4,12},{5,13},{6,14},{7,15},{8,0},{9,1},... | collective-permute-start | bytes 811016 | tf_op jit(solution)/shard_map/ppermute | solution.py:18
  9.3 4.3 %attend.3 = (f32[32,4096]{1,0:T(8,128)S(1)}, bf16[32,4224]{1,0:T(8,128)(2,1)S(1)}, bf16[32,4096]{1,0:T(8,128)(2,1)S(1)}, bf16[32,4096]{1,0:T(8,128)(2,1)S(1)}, b...) custom-call(s32[1]{0:T(128)S(6)} %copy.16.len_hbm, bf16[64,4096]{1,0:T(8,128)(2,1)} %refs_0_.3, ...), custom_call_target="tpu_custom_call" | custom-call | flops 1 | bytes 14000000 | tf_op jit(solution)/shard_map/attend/pallas_call | solution.py:230
  13.6 1.3 %collective-permute-done.3.refs_6_.refs_9_ = bf16[384,4096]{1,0:T(8,128)(2,1)S(1)} collective-permute-done((bf16[384,4096]{1,0:T(8,128)(2,1)}, bf16[384,4096]{1,0:T(8,128)(2,1)S(1)}, u32[]{:S(2)}, u32[]{:S(2)}) %collective-permute-start.3) | collective-permute-done | bytes 3145760 | tf_op jit(solution)/shard_map/ppermute | solution.py:18
  15.0 3.0 %collective-permute-start.8 = (bf16[32,4096]{1,0:T(8,128)(2,1)S(1)}, bf16[32,4096]{1,0:T(8,128)(2,1)S(1)}, u32[]{:S(2)}, u32[]{:S(2)}) collective-permute-start(bf16[32,4096]{1,0:T(8,128)(2,1)S(1)} %get-tuple-element.54), channel_id=1, source_target_pairs={{0,2},{1,3},{2,0},{3,1},{4,6},{5,7},{6,4},{7,5},{8,10},{9,11},{10,... | collective-permute-start | bytes 786440 | tf_op jit(solution)/shard_map/ppermute | solution.py:18
  18.0 1.6 %collective-permute-start.9 = (bf16[32,4096]{1,0:T(8,128)(2,1)S(1)}, bf16[32,4096]{1,0:T(8,128)(2,1)S(1)}, u32[]{:S(2)}, u32[]{:S(2)}) collective-permute-start(bf16[32,4096]{1,0:T(8,128)(2,1)S(1)} %get-tuple-element.55), channel_id=1, source_target_pairs={{0,4},{1,5},{2,6},{3,7},{4,0},{5,1},{6,2},{7,3},{8,12},{9,13},{10,... | collective-permute-start | bytes 786440 | tf_op jit(solution)/shard_map/ppermute | solution.py:18
  19.6 2.7 %collective-permute-start.7 = (bf16[32,4224]{1,0:T(8,128)(2,1)S(1)}, bf16[32,4224]{1,0:T(8,128)(2,1)S(1)}, u32[]{:S(2)}, u32[]{:S(2)}) collective-permute-start(bf16[32,4224]{1,0:T(8,128)(2,1)S(1)} %passed.5.refs_0_), channel_id=1, source_target_pairs={{0,8},{1,9},{2,10},{3,11},{4,12},{5,13},{6,14},{7,15},{8,0},{9,1},... | collective-permute-start | bytes 811016 | tf_op jit(solution)/shard_map/ppermute | solution.py:18
  23.1 1.7 %collective-permute-start.4 = (bf16[16,4096]{1,0:T(8,128)(2,1)S(1)}, bf16[16,4096]{1,0:T(8,128)(2,1)S(1)}, u32[]{:S(2)}, u32[]{:S(2)}) collective-permute-start(bf16[16,4096]{1,0:T(8,128)(2,1)S(1)} %get-tuple-element.51), channel_id=1, source_target_pairs={{0,2},{1,3},{2,0},{3,1},{4,6},{5,7},{6,4},{7,5},{8,10},{9,11},{10,... | collective-permute-start | bytes 393224 | tf_op jit(solution)/shard_map/ppermute | solution.py:18
  24.9 1.5 %collective-permute-start.5 = (bf16[16,4096]{1,0:T(8,128)(2,1)S(1)}, bf16[16,4096]{1,0:T(8,128)(2,1)S(1)}, u32[]{:S(2)}, u32[]{:S(2)}) collective-permute-start(bf16[16,4096]{1,0:T(8,128)(2,1)S(1)} %get-tuple-element.52), channel_id=1, source_target_pairs={{0,4},{1,5},{2,6},{3,7},{4,0},{5,1},{6,2},{7,3},{8,12},{9,13},{10,... | collective-permute-start | bytes 393224 | tf_op jit(solution)/shard_map/ppermute | solution.py:18
  26.4 7.4 %collective-permute-done.9.refs_3_.refs_2_ = bf16[32,4096]{1,0:T(8,128)(2,1)S(1)} collective-permute-done((bf16[32,4096]{1,0:T(8,128)(2,1)S(1)}, bf16[32,4096]{1,0:T(8,128)(2,1)S(1)}, u32[]{:S(2)}, u32[]{:S(2)}) %collective-permute-start.9) | collective-permute-done | bytes 262176 | tf_op jit(solution)/shard_map/ppermute | solution.py:18
  33.9 6.4 %collective-permute-done.10.refs_4_.refs_3_ = bf16[32,4096]{1,0:T(8,128)(2,1)S(1)} collective-permute-done((bf16[32,4096]{1,0:T(8,128)(2,1)S(1)}, bf16[32,4096]{1,0:T(8,128)(2,1)S(1)}, u32[]{:S(2)}, u32[]{:S(2)}) %collective-permute-start.10) | collective-permute-done | bytes 262176 | tf_op jit(solution)/shard_map/ppermute | solution.py:18
  40.4 0.5 relay.3
  40.9 0.5 collective-permute-start.14
  41.4 0.8 collective-permute-start.15
  42.3 2.2 %collective-permute-start.16 = (bf16[16,4096]{1,0:T(8,128)(2,1)S(1)}, bf16[16,4096]{1,0:T(8,128)(2,1)S(1)}, u32[]{:S(2)}, u32[]{:S(2)}) collective-permute-start(bf16[16,4096]{1,0:T(8,128)(2,1)S(1)} %get-tuple-element.64), channel_id=1, source_target_pairs={{0,6},{1,7},{2,4},{3,5},{4,2},{5,3},{6,0},{7,1},{8,14},{9,15},{10,... | collective-permute-start | bytes 393224 | tf_op jit(solution)/shard_map/ppermute | solution.py:18
  44.4 1.6 %collective-permute-done.6.refs_3_ = bf16[16,4096]{1,0:T(8,128)(2,1)S(1)} collective-permute-done((bf16[16,4096]{1,0:T(8,128)(2,1)S(1)}, bf16[16,4096]{1,0:T(8,128)(2,1)S(1)}, u32[]{:S(2)}, u32[]{:S(2)}) %collective-permute-start.6) | collective-permute-done | bytes 131104 | tf_op jit(solution)/shard_map/ppermute | solution.py:18
  46.0 2.7 %expert.3 = (bf16[16,4096]{1,0:T(8,128)(2,1)S(1)}, bf16[16,4096]{1,0:T(8,128)(2,1)S(1)}, bf16[16,4096]{1,0:T(8,128)(2,1)S(1)}, bf16[16,4096]{1,0:T(8,128)(2,1)S(1)}) custom-call(bf16[16,4096]{1,0:T(8,128)(2,1)S(1)} %get-tuple-element.50.refs_0_, bf16[16,4096]{1,0:T(8,128)(2,1)S(1)} %collective-permute-done.4.refs_1_, ...), custom_call_target="tpu_custom_call" | custom-call | flops 1 | bytes 35000 | tf_op jit(solution)/shard_map/expert/pallas_call | solution.py:351
  48.8 0.5 collective-permute-start.11
  49.7 2.6 %collective-permute-start.13 = (bf16[16,4096]{1,0:T(8,128)(2,1)S(1)}, bf16[16,4096]{1,0:T(8,128)(2,1)S(1)}, u32[]{:S(2)}, u32[]{:S(2)}) collective-permute-start(bf16[16,4096]{1,0:T(8,128)(2,1)S(1)} %get-tuple-element.61), channel_id=1, source_target_pairs={{0,6},{1,7},{2,4},{3,5},{4,2},{5,3},{6,0},{7,1},{8,14},{9,15},{10,... | collective-permute-start | bytes 393224 | tf_op jit(solution)/shard_map/ppermute | solution.py:18
  52.3 2.9 %expert.4 = (bf16[16,4096]{1,0:T(8,128)(2,1)S(1)}, bf16[16,4096]{1,0:T(8,128)(2,1)S(1)}, bf16[16,4096]{1,0:T(8,128)(2,1)S(1)}, bf16[16,4096]{1,0:T(8,128)(2,1)S(1)}) custom-call(bf16[16,4096]{1,0:T(8,128)(2,1)S(1)} %get-tuple-element.57.refs_10_.refs_0_, bf16[16,4096]{1,0:T(8,128)(2,1)S(1)} %collective-permute-done.14.refs_1_, ...), custom_call_target="tpu_custom_call" | custom-call | flops 1 | bytes 35000 | tf_op jit(solution)/shard_map/expert/pallas_call | solution.py:351
  55.2 0.5 collective-permute-start.18
  56.2 2.6 %collective-permute-start.20 = (bf16[16,4096]{1,0:T(8,128)(2,1)S(1)}, bf16[16,4096]{1,0:T(8,128)(2,1)S(1)}, u32[]{:S(2)}, u32[]{:S(2)}) collective-permute-start(bf16[16,4096]{1,0:T(8,128)(2,1)S(1)} %get-tuple-element.71), channel_id=1, source_target_pairs={{0,6},{1,7},{2,4},{3,5},{4,2},{5,3},{6,0},{7,1},{8,14},{9,15},{10,... | collective-permute-start | bytes 393224 | tf_op jit(solution)/shard_map/ppermute | solution.py:18
  58.8 0.6 relay_back.2.refs_10_
  59.4 2.1 %collective-permute-start.17 = (bf16[32,4096]{1,0:T(8,128)(2,1)S(1)}, bf16[32,4096]{1,0:T(8,128)(2,1)S(1)}, u32[]{:S(2)}, u32[]{:S(2)}) collective-permute-start(bf16[32,4096]{1,0:T(8,128)(2,1)S(1)} %relay_back.2.refs_10_), channel_id=1, source_target_pairs={{0,8},{1,9},{2,10},{3,11},{4,12},{5,13},{6,14},{7,15},{8,0},{9,1},... | collective-permute-start | bytes 786440 | tf_op jit(solution)/shard_map/ppermute | solution.py:18
  61.5 2.7 %expert.5 = (bf16[32,4096]{1,0:T(8,128)(2,1)S(1)}, bf16[32,4096]{1,0:T(8,128)(2,1)S(1)}, bf16[32,4096]{1,0:T(8,128)(2,1)S(1)}, bf16[32,4096]{1,0:T(8,128)(2,1)S(1)}) custom-call(bf16[32,4096]{1,0:T(8,128)(2,1)S(1)} %get-tuple-element.49.refs_1_.refs_0_, bf16[32,4096]{1,0:T(8,128)(2,1)S(1)} %collective-permute-done.8.refs_2_.refs_1_, ...), custom_call_target="tpu_custom_call" | custom-call | flops 1 | bytes 14000000 | tf_op jit(solution)/shard_map/expert/pallas_call | solution.py:351
  64.2 2.0 %collective-permute-start.23 = (bf16[32,4096]{1,0:T(8,128)(2,1)S(1)}, bf16[32,4096]{1,0:T(8,128)(2,1)S(1)}, u32[]{:S(2)}, u32[]{:S(2)}) collective-permute-start(bf16[32,4096]{1,0:T(8,128)(2,1)S(1)} %passed.6.refs_4_), channel_id=1, source_target_pairs={{0,6},{1,7},{2,4},{3,5},{4,2},{5,3},{6,0},{7,1},{8,14},{9,15},{10,... | collective-permute-start | bytes 786440 | tf_op jit(solution)/shard_map/ppermute | solution.py:18
  66.3 3.9 %collective-permute-done.20.refs_3_ = bf16[16,4096]{1,0:T(8,128)(2,1)S(1)} collective-permute-done((bf16[16,4096]{1,0:T(8,128)(2,1)S(1)}, bf16[16,4096]{1,0:T(8,128)(2,1)S(1)}, u32[]{:S(2)}, u32[]{:S(2)}) %collective-permute-start.20) | collective-permute-done | bytes 131104 | tf_op jit(solution)/shard_map/ppermute | solution.py:18
  70.2 0.6 relay_back.3.refs_2_
  71.3 11.0 %collective-permute-done.23.refs_6_ = bf16[32,4096]{1,0:T(8,128)(2,1)S(1)} collective-permute-done((bf16[32,4096]{1,0:T(8,128)(2,1)S(1)}, bf16[32,4096]{1,0:T(8,128)(2,1)S(1)}, u32[]{:S(2)}, u32[]{:S(2)}) %collective-permute-start.23) | collective-permute-done | bytes 262176 | tf_op jit(solution)/shard_map/ppermute | solution.py:18
  82.4 3.1 %collective-permute-done.22.refs_5_ = bf16[32,4096]{1,0:T(8,128)(2,1)S(1)} collective-permute-done((bf16[32,4096]{1,0:T(8,128)(2,1)S(1)}, bf16[32,4096]{1,0:T(8,128)(2,1)S(1)}, u32[]{:S(2)}, u32[]{:S(2)}) %collective-permute-start.22) | collective-permute-done | bytes 262176 | tf_op jit(solution)/shard_map/ppermute | solution.py:18
  85.4 1.0 %add_near.1.base_ref = f32[64,4096]{1,0:T(8,128)S(1)} custom-call(f32[4,64]{1,0:T(4,128)S(1)} %get-tuple-element.40.info_ref, f32[32,4096]{1,0:T(8,128)S(1)} %get-tuple-element.41.refs_0_, f32[32,4096]{1,0:T(8,128)S(1)} %get-tuple-element.43.refs_1_, bf16[32,4096]{1,0:T(8,128)(2,1)S(1)} %collective-permute-done.17.refs_2_, ...), custom_call_target="tpu_custom_call" | custom-call | flops 1 | bytes 14000000 | tf_op jit(solution)/shard_map/add_near/pallas_call | solution.py:405
  86.4 0.9 %add_far.1 = bf16[64,4096]{1,0:T(8,128)(2,1)} custom-call(f32[64,4096]{1,0:T(8,128)S(1)} %add_near.1.base_ref, bf16[32,4096]{1,0:T(8,128)(2,1)S(1)} %collective-permute-done.24.far_ref), custom_call_target="tpu_custom_call" | custom-call | flops 1 | bytes 3500000 | tf_op jit(solution)/shard_map/add_far/pallas_call | solution.py:427
  (39 shorter events, 3.5 us)
Async XLA Ops:
  0.0 13.6 %collective-permute-start.1 = (bf16[4096,384]{1,0:T(8,128)(2,1)}, bf16[4096,384]{1,0:T(8,128)(2,1)S(1)}, u32[]{:S(2)}, u32[]{:S(2)}) collective-permute-start(bf16[4096,384]{1,0:T(8,128)(2,1)} %refs_4_.9), channel_id=1, source_target_pairs={{0,1},{1,0},{2,3},{3,2},{4,5},{5,4},{6,7},{7,6},{8,9},{9,8},{10,11... | collective-permute-start | bytes 9437192 | tf_op jit(solution)/shard_map/ppermute | solution.py:18
  0.5 13.1 %collective-permute-start.2 = (bf16[4096,384]{1,0:T(8,128)(2,1)}, bf16[4096,384]{1,0:T(8,128)(2,1)S(1)}, u32[]{:S(2)}, u32[]{:S(2)}) collective-permute-start(bf16[4096,384]{1,0:T(8,128)(2,1)} %refs_5_.9), channel_id=1, source_target_pairs={{0,1},{1,0},{2,3},{3,2},{4,5},{5,4},{6,7},{7,6},{8,9},{9,8},{10,11... | collective-permute-start | bytes 9437192 | tf_op jit(solution)/shard_map/ppermute | solution.py:18
  0.5 14.4 %collective-permute-start.3 = (bf16[384,4096]{1,0:T(8,128)(2,1)}, bf16[384,4096]{1,0:T(8,128)(2,1)S(1)}, u32[]{:S(2)}, u32[]{:S(2)}) collective-permute-start(bf16[384,4096]{1,0:T(8,128)(2,1)} %refs_6_.9), channel_id=1, source_target_pairs={{0,1},{1,0},{2,3},{3,2},{4,5},{5,4},{6,7},{7,6},{8,9},{9,8},{10,11... | collective-permute-start | bytes 9437192 | tf_op jit(solution)/shard_map/ppermute | solution.py:18
  5.7 17.0 %collective-permute-start = (bf16[32,4224]{1,0:T(8,128)(2,1)S(1)}, bf16[32,4224]{1,0:T(8,128)(2,1)S(1)}, u32[]{:S(2)}, u32[]{:S(2)}) collective-permute-start(bf16[32,4224]{1,0:T(8,128)(2,1)S(1)} %get-tuple-element.42.refs_11_), channel_id=1, source_target_pairs={{0,8},{1,9},{2,10},{3,11},{4,12},{5,13},{6,14},{7,15},{8,0},{9,1},... | collective-permute-start | bytes 811016 | tf_op jit(solution)/shard_map/ppermute | solution.py:18
  14.9 31.1 %copy-start = (bf16[4096,384]{1,0:T(8,128)(2,1)S(1)}, bf16[4096,384]{1,0:T(8,128)(2,1)}, u32[]{:S(2)}) copy-start(bf16[4096,384]{1,0:T(8,128)(2,1)} %refs_4_.9) | copy-start | bytes 9437188
  15.0 31.1 %copy-start.1 = (bf16[4096,384]{1,0:T(8,128)(2,1)S(1)}, bf16[4096,384]{1,0:T(8,128)(2,1)}, u32[]{:S(2)}) copy-start(bf16[4096,384]{1,0:T(8,128)(2,1)} %refs_5_.9) | copy-start | bytes 9437188
  15.0 31.1 %copy-start.2 = (bf16[384,4096]{1,0:T(8,128)(2,1)S(1)}, bf16[384,4096]{1,0:T(8,128)(2,1)}, u32[]{:S(2)}) copy-start(bf16[384,4096]{1,0:T(8,128)(2,1)} %refs_6_.9) | copy-start | bytes 9437188
  15.0 9.9 %collective-permute-start.8 = (bf16[32,4096]{1,0:T(8,128)(2,1)S(1)}, bf16[32,4096]{1,0:T(8,128)(2,1)S(1)}, u32[]{:S(2)}, u32[]{:S(2)}) collective-permute-start(bf16[32,4096]{1,0:T(8,128)(2,1)S(1)} %get-tuple-element.54), channel_id=1, source_target_pairs={{0,2},{1,3},{2,0},{3,1},{4,6},{5,7},{6,4},{7,5},{8,10},{9,11},{10,... | collective-permute-start | bytes 786440 | tf_op jit(solution)/shard_map/ppermute | solution.py:18
  18.0 15.8 %collective-permute-start.9 = (bf16[32,4096]{1,0:T(8,128)(2,1)S(1)}, bf16[32,4096]{1,0:T(8,128)(2,1)S(1)}, u32[]{:S(2)}, u32[]{:S(2)}) collective-permute-start(bf16[32,4096]{1,0:T(8,128)(2,1)S(1)} %get-tuple-element.55), channel_id=1, source_target_pairs={{0,4},{1,5},{2,6},{3,7},{4,0},{5,1},{6,2},{7,3},{8,12},{9,13},{10,... | collective-permute-start | bytes 786440 | tf_op jit(solution)/shard_map/ppermute | solution.py:18
  19.6 20.8 %collective-permute-start.7 = (bf16[32,4224]{1,0:T(8,128)(2,1)S(1)}, bf16[32,4224]{1,0:T(8,128)(2,1)S(1)}, u32[]{:S(2)}, u32[]{:S(2)}) collective-permute-start(bf16[32,4224]{1,0:T(8,128)(2,1)S(1)} %passed.5.refs_0_), channel_id=1, source_target_pairs={{0,8},{1,9},{2,10},{3,11},{4,12},{5,13},{6,14},{7,15},{8,0},{9,1},... | collective-permute-start | bytes 811016 | tf_op jit(solution)/shard_map/ppermute | solution.py:18
  22.2 18.1 %collective-permute-start.10 = (bf16[32,4096]{1,0:T(8,128)(2,1)S(1)}, bf16[32,4096]{1,0:T(8,128)(2,1)S(1)}, u32[]{:S(2)}, u32[]{:S(2)}) collective-permute-start(bf16[32,4096]{1,0:T(8,128)(2,1)S(1)} %get-tuple-element.56), channel_id=1, source_target_pairs={{0,6},{1,7},{2,4},{3,5},{4,2},{5,3},{6,0},{7,1},{8,14},{9,15},{10,... | collective-permute-start | bytes 786440 | tf_op jit(solution)/shard_map/ppermute | solution.py:18
  23.1 19.1 %collective-permute-start.4 = (bf16[16,4096]{1,0:T(8,128)(2,1)S(1)}, bf16[16,4096]{1,0:T(8,128)(2,1)S(1)}, u32[]{:S(2)}, u32[]{:S(2)}) collective-permute-start(bf16[16,4096]{1,0:T(8,128)(2,1)S(1)} %get-tuple-element.51), channel_id=1, source_target_pairs={{0,2},{1,3},{2,0},{3,1},{4,6},{5,7},{6,4},{7,5},{8,10},{9,11},{10,... | collective-permute-start | bytes 393224 | tf_op jit(solution)/shard_map/ppermute | solution.py:18
  24.9 19.6 %collective-permute-start.5 = (bf16[16,4096]{1,0:T(8,128)(2,1)S(1)}, bf16[16,4096]{1,0:T(8,128)(2,1)S(1)}, u32[]{:S(2)}, u32[]{:S(2)}) collective-permute-start(bf16[16,4096]{1,0:T(8,128)(2,1)S(1)} %get-tuple-element.52), channel_id=1, source_target_pairs={{0,4},{1,5},{2,6},{3,7},{4,0},{5,1},{6,2},{7,3},{8,12},{9,13},{10,... | collective-permute-start | bytes 393224 | tf_op jit(solution)/shard_map/ppermute | solution.py:18
  33.8 12.3 %collective-permute-start.6 = (bf16[16,4096]{1,0:T(8,128)(2,1)S(1)}, bf16[16,4096]{1,0:T(8,128)(2,1)S(1)}, u32[]{:S(2)}, u32[]{:S(2)}) collective-permute-start(bf16[16,4096]{1,0:T(8,128)(2,1)S(1)} %get-tuple-element.53), channel_id=1, source_target_pairs={{0,6},{1,7},{2,4},{3,5},{4,2},{5,3},{6,0},{7,1},{8,14},{9,15},{10,... | collective-permute-start | bytes 393224 | tf_op jit(solution)/shard_map/ppermute | solution.py:18
  40.9 8.8 %collective-permute-start.14 = (bf16[16,4096]{1,0:T(8,128)(2,1)S(1)}, bf16[16,4096]{1,0:T(8,128)(2,1)S(1)}, u32[]{:S(2)}, u32[]{:S(2)}) collective-permute-start(bf16[16,4096]{1,0:T(8,128)(2,1)S(1)} %get-tuple-element.62), channel_id=1, source_target_pairs={{0,2},{1,3},{2,0},{3,1},{4,6},{5,7},{6,4},{7,5},{8,10},{9,11},{10,... | collective-permute-start | bytes 393224 | tf_op jit(solution)/shard_map/ppermute | solution.py:18
  41.4 10.9 %collective-permute-start.15 = (bf16[16,4096]{1,0:T(8,128)(2,1)S(1)}, bf16[16,4096]{1,0:T(8,128)(2,1)S(1)}, u32[]{:S(2)}, u32[]{:S(2)}) collective-permute-start(bf16[16,4096]{1,0:T(8,128)(2,1)S(1)} %get-tuple-element.63), channel_id=1, source_target_pairs={{0,4},{1,5},{2,6},{3,7},{4,0},{5,1},{6,2},{7,3},{8,12},{9,13},{10,... | collective-permute-start | bytes 393224 | tf_op jit(solution)/shard_map/ppermute | solution.py:18
  42.3 10.1 %collective-permute-start.16 = (bf16[16,4096]{1,0:T(8,128)(2,1)S(1)}, bf16[16,4096]{1,0:T(8,128)(2,1)S(1)}, u32[]{:S(2)}, u32[]{:S(2)}) collective-permute-start(bf16[16,4096]{1,0:T(8,128)(2,1)S(1)} %get-tuple-element.64), channel_id=1, source_target_pairs={{0,6},{1,7},{2,4},{3,5},{4,2},{5,3},{6,0},{7,1},{8,14},{9,15},{10,... | collective-permute-start | bytes 393224 | tf_op jit(solution)/shard_map/ppermute | solution.py:18
  48.8 7.4 %collective-permute-start.11 = (bf16[16,4096]{1,0:T(8,128)(2,1)S(1)}, bf16[16,4096]{1,0:T(8,128)(2,1)S(1)}, u32[]{:S(2)}, u32[]{:S(2)}) collective-permute-start(bf16[16,4096]{1,0:T(8,128)(2,1)S(1)} %get-tuple-element.59), channel_id=1, source_target_pairs={{0,2},{1,3},{2,0},{3,1},{4,6},{5,7},{6,4},{7,5},{8,10},{9,11},{10,... | collective-permute-start | bytes 393224 | tf_op jit(solution)/shard_map/ppermute | solution.py:18
  49.3 9.5 %collective-permute-start.12 = (bf16[16,4096]{1,0:T(8,128)(2,1)S(1)}, bf16[16,4096]{1,0:T(8,128)(2,1)S(1)}, u32[]{:S(2)}, u32[]{:S(2)}) collective-permute-start(bf16[16,4096]{1,0:T(8,128)(2,1)S(1)} %get-tuple-element.60), channel_id=1, source_target_pairs={{0,4},{1,5},{2,6},{3,7},{4,0},{5,1},{6,2},{7,3},{8,12},{9,13},{10,... | collective-permute-start | bytes 393224 | tf_op jit(solution)/shard_map/ppermute | solution.py:18
  49.7 9.1 %collective-permute-start.13 = (bf16[16,4096]{1,0:T(8,128)(2,1)S(1)}, bf16[16,4096]{1,0:T(8,128)(2,1)S(1)}, u32[]{:S(2)}, u32[]{:S(2)}) collective-permute-start(bf16[16,4096]{1,0:T(8,128)(2,1)S(1)} %get-tuple-element.61), channel_id=1, source_target_pairs={{0,6},{1,7},{2,4},{3,5},{4,2},{5,3},{6,0},{7,1},{8,14},{9,15},{10,... | collective-permute-start | bytes 393224 | tf_op jit(solution)/shard_map/ppermute | solution.py:18
  55.2 11.0 %collective-permute-start.18 = (bf16[16,4096]{1,0:T(8,128)(2,1)S(1)}, bf16[16,4096]{1,0:T(8,128)(2,1)S(1)}, u32[]{:S(2)}, u32[]{:S(2)}) collective-permute-start(bf16[16,4096]{1,0:T(8,128)(2,1)S(1)} %get-tuple-element.69), channel_id=1, source_target_pairs={{0,2},{1,3},{2,0},{3,1},{4,6},{5,7},{6,4},{7,5},{8,10},{9,11},{10,... | collective-permute-start | bytes 393224 | tf_op jit(solution)/shard_map/ppermute | solution.py:18
  55.8 10.5 %collective-permute-start.19 = (bf16[16,4096]{1,0:T(8,128)(2,1)S(1)}, bf16[16,4096]{1,0:T(8,128)(2,1)S(1)}, u32[]{:S(2)}, u32[]{:S(2)}) collective-permute-start(bf16[16,4096]{1,0:T(8,128)(2,1)S(1)} %get-tuple-element.70), channel_id=1, source_target_pairs={{0,4},{1,5},{2,6},{3,7},{4,0},{5,1},{6,2},{7,3},{8,12},{9,13},{10,... | collective-permute-start | bytes 393224 | tf_op jit(solution)/shard_map/ppermute | solution.py:18
  56.2 14.0 %collective-permute-start.20 = (bf16[16,4096]{1,0:T(8,128)(2,1)S(1)}, bf16[16,4096]{1,0:T(8,128)(2,1)S(1)}, u32[]{:S(2)}, u32[]{:S(2)}) collective-permute-start(bf16[16,4096]{1,0:T(8,128)(2,1)S(1)} %get-tuple-element.71), channel_id=1, source_target_pairs={{0,6},{1,7},{2,4},{3,5},{4,2},{5,3},{6,0},{7,1},{8,14},{9,15},{10,... | collective-permute-start | bytes 393224 | tf_op jit(solution)/shard_map/ppermute | solution.py:18
  59.4 23.0 %collective-permute-start.17 = (bf16[32,4096]{1,0:T(8,128)(2,1)S(1)}, bf16[32,4096]{1,0:T(8,128)(2,1)S(1)}, u32[]{:S(2)}, u32[]{:S(2)}) collective-permute-start(bf16[32,4096]{1,0:T(8,128)(2,1)S(1)} %relay_back.2.refs_10_), channel_id=1, source_target_pairs={{0,8},{1,9},{2,10},{3,11},{4,12},{5,13},{6,14},{7,15},{8,0},{9,1},... | collective-permute-start | bytes 786440 | tf_op jit(solution)/shard_map/ppermute | solution.py:18
  64.2 18.1 %collective-permute-start.23 = (bf16[32,4096]{1,0:T(8,128)(2,1)S(1)}, bf16[32,4096]{1,0:T(8,128)(2,1)S(1)}, u32[]{:S(2)}, u32[]{:S(2)}) collective-permute-start(bf16[32,4096]{1,0:T(8,128)(2,1)S(1)} %passed.6.refs_4_), channel_id=1, source_target_pairs={{0,6},{1,7},{2,4},{3,5},{4,2},{5,3},{6,0},{7,1},{8,14},{9,15},{10,... | collective-permute-start | bytes 786440 | tf_op jit(solution)/shard_map/ppermute | solution.py:18
  70.8 14.6 %collective-permute-start.22 = (bf16[32,4096]{1,0:T(8,128)(2,1)S(1)}, bf16[32,4096]{1,0:T(8,128)(2,1)S(1)}, u32[]{:S(2)}, u32[]{:S(2)}) collective-permute-start(bf16[32,4096]{1,0:T(8,128)(2,1)S(1)} %get-tuple-element.74), channel_id=1, source_target_pairs={{0,4},{1,5},{2,6},{3,7},{4,0},{5,1},{6,2},{7,3},{8,12},{9,13},{10,... | collective-permute-start | bytes 786440 | tf_op jit(solution)/shard_map/ppermute | solution.py:18
  70.9 14.6 %collective-permute-start.21 = (bf16[32,4096]{1,0:T(8,128)(2,1)S(1)}, bf16[32,4096]{1,0:T(8,128)(2,1)S(1)}, u32[]{:S(2)}, u32[]{:S(2)}) collective-permute-start(bf16[32,4096]{1,0:T(8,128)(2,1)S(1)} %get-tuple-element.73.refs_7_), channel_id=1, source_target_pairs={{0,2},{1,3},{2,0},{3,1},{4,6},{5,7},{6,4},{7,5},{8,10},{9,11},{10,... | collective-permute-start | bytes 786440 | tf_op jit(solution)/shard_map/ppermute | solution.py:18
  71.0 15.4 %collective-permute-start.24 = (bf16[32,4096]{1,0:T(8,128)(2,1)S(1)}, bf16[32,4096]{1,0:T(8,128)(2,1)S(1)}, u32[]{:S(2)}, u32[]{:S(2)}) collective-permute-start(bf16[32,4096]{1,0:T(8,128)(2,1)S(1)} %relay_back.3.refs_2_), channel_id=1, source_target_pairs={{0,8},{1,9},{2,10},{3,11},{4,12},{5,13},{6,14},{7,15},{8,0},{9,1},... | collective-permute-start | bytes 786440 | tf_op jit(solution)/shard_map/ppermute | solution.py:18

commit v7 on v6

--- a/solution.py
+++ b/solution.py
@@ -107,9 +107,9 @@
     low = (weight - high.astype(jnp.float32)).astype(jnp.bfloat16)
     values = joined[...]
     first = (((0,), (0,)), ((), ()))
-    return lax.dot_general(high, values, first, preferred_element_type=jnp.float32) + lax.dot_general(
-        low, values, first, preferred_element_type=jnp.float32
-    )
+    both = jnp.concatenate([high, low], axis=0)
+    twice = jnp.concatenate([values, values], axis=0)
+    return lax.dot_general(both, twice, first, preferred_element_type=jnp.float32)
 
 
 def unit_rows(values, gain, ones):

time: 87.4 us -> 87.4 us (level)
  no operation moved by 1% of the time
where the time goes in v7:
time: 87.4 us; the launch traced here: 87.2 us
  waiting for transfers between devices  34.9 us (40%)
  starting transfers between devices  30.8 us (35%)
  Pallas kernels  20.6 us (24%)
    ppermute x25, waiting for transfers between devices, exchange(): lax.ppermute(value, 'ep', [(i, i ^ distance) for i in range(lax.axis_size...  34.9 us
    ppermute x25, starting transfers between devices, exchange(): lax.ppermute(value, 'ep', [(i, i ^ distance) for i in range(lax.axis_size...  30.8 us
    pallas_call x3, Pallas kernels, expert(): pl.pallas_call(body, out_shape=out, in_specs=[whole(x) for x in ins] + [w...  8.31 us
    pallas_call x2, Pallas kernels, attend(): pl.pallas_call(body, out_shape=out_shape, in_specs=[pl.BlockSpec(memory_s...  8.3 us
  transfers between devices with their start and end apart: 25, of which 7 were waited for; matrix products, arithmetic and copies ran while one was open for 0% of the time, Pallas kernels for 23%

profile of v7, /device:TPU:0, one launch (start us, length us, event | category | flops | bytes accessed | tf_op | source)
XLA Modules:
  0.0 87.2 jit_solution(15794884883030930160)
XLA Ops:
  1.6 4.0 %attend.2 = (f32[32,4096]{1,0:T(8,128)S(1)}, bf16[32,4224]{1,0:T(8,128)(2,1)S(1)}, f32[4,64]{1,0:T(4,128)S(1)}) custom-call(s32[1]{0:T(128)S(6)} %copy.16.len_hbm, bf16[64,4096]{1,0:T(8,128)(2,1)} %refs_0_.3, bf16[64,4096]{1,0:T(8,128)(2,1)} %refs_1_.3, bf16[1024,256]{1,0:T(8,128)(2,1)} %refs_2_.3, bf16[1024,256]{1,0:T(8,128)(2,1)} %refs_3_.3, ...), custom_call_target="tpu_custom_call" | custom-call | flops 1 | bytes 14000000 | tf_op jit(solution)/shard_map/attend/pallas_call | solution.py:230
  5.7 3.7 %collective-permute-start = (bf16[32,4224]{1,0:T(8,128)(2,1)S(1)}, bf16[32,4224]{1,0:T(8,128)(2,1)S(1)}, u32[]{:S(2)}, u32[]{:S(2)}) collective-permute-start(bf16[32,4224]{1,0:T(8,128)(2,1)S(1)} %get-tuple-element.42.refs_11_), channel_id=1, source_target_pairs={{0,8},{1,9},{2,10},{3,11},{4,12},{5,13},{6,14},{7,15},{8,0},{9,1},... | collective-permute-start | bytes 811016 | tf_op jit(solution)/shard_map/ppermute | solution.py:18
  9.3 4.3 %attend.3 = (f32[32,4096]{1,0:T(8,128)S(1)}, bf16[32,4224]{1,0:T(8,128)(2,1)S(1)}, bf16[32,4096]{1,0:T(8,128)(2,1)S(1)}, bf16[32,4096]{1,0:T(8,128)(2,1)S(1)}, b...) custom-call(s32[1]{0:T(128)S(6)} %copy.16.len_hbm, bf16[64,4096]{1,0:T(8,128)(2,1)} %refs_0_.3, ...), custom_call_target="tpu_custom_call" | custom-call | flops 1 | bytes 14000000 | tf_op jit(solution)/shard_map/attend/pallas_call | solution.py:230
  13.6 1.3 %collective-permute-done.3.refs_6_.refs_9_ = bf16[384,4096]{1,0:T(8,128)(2,1)S(1)} collective-permute-done((bf16[384,4096]{1,0:T(8,128)(2,1)}, bf16[384,4096]{1,0:T(8,128)(2,1)S(1)}, u32[]{:S(2)}, u32[]{:S(2)}) %collective-permute-start.3) | collective-permute-done | bytes 3145760 | tf_op jit(solution)/shard_map/ppermute | solution.py:18
  15.0 3.0 %collective-permute-start.8 = (bf16[32,4096]{1,0:T(8,128)(2,1)S(1)}, bf16[32,4096]{1,0:T(8,128)(2,1)S(1)}, u32[]{:S(2)}, u32[]{:S(2)}) collective-permute-start(bf16[32,4096]{1,0:T(8,128)(2,1)S(1)} %get-tuple-element.54), channel_id=1, source_target_pairs={{0,2},{1,3},{2,0},{3,1},{4,6},{5,7},{6,4},{7,5},{8,10},{9,11},{10,... | collective-permute-start | bytes 786440 | tf_op jit(solution)/shard_map/ppermute | solution.py:18
  18.0 1.6 %collective-permute-start.9 = (bf16[32,4096]{1,0:T(8,128)(2,1)S(1)}, bf16[32,4096]{1,0:T(8,128)(2,1)S(1)}, u32[]{:S(2)}, u32[]{:S(2)}) collective-permute-start(bf16[32,4096]{1,0:T(8,128)(2,1)S(1)} %get-tuple-element.55), channel_id=1, source_target_pairs={{0,4},{1,5},{2,6},{3,7},{4,0},{5,1},{6,2},{7,3},{8,12},{9,13},{10,... | collective-permute-start | bytes 786440 | tf_op jit(solution)/shard_map/ppermute | solution.py:18
  19.6 2.7 %collective-permute-start.7 = (bf16[32,4224]{1,0:T(8,128)(2,1)S(1)}, bf16[32,4224]{1,0:T(8,128)(2,1)S(1)}, u32[]{:S(2)}, u32[]{:S(2)}) collective-permute-start(bf16[32,4224]{1,0:T(8,128)(2,1)S(1)} %passed.5.refs_0_), channel_id=1, source_target_pairs={{0,8},{1,9},{2,10},{3,11},{4,12},{5,13},{6,14},{7,15},{8,0},{9,1},... | collective-permute-start | bytes 811016 | tf_op jit(solution)/shard_map/ppermute | solution.py:18
  23.1 1.7 %collective-permute-start.4 = (bf16[16,4096]{1,0:T(8,128)(2,1)S(1)}, bf16[16,4096]{1,0:T(8,128)(2,1)S(1)}, u32[]{:S(2)}, u32[]{:S(2)}) collective-permute-start(bf16[16,4096]{1,0:T(8,128)(2,1)S(1)} %get-tuple-element.51), channel_id=1, source_target_pairs={{0,2},{1,3},{2,0},{3,1},{4,6},{5,7},{6,4},{7,5},{8,10},{9,11},{10,... | collective-permute-start | bytes 393224 | tf_op jit(solution)/shard_map/ppermute | solution.py:18
  24.9 1.5 %collective-permute-start.5 = (bf16[16,4096]{1,0:T(8,128)(2,1)S(1)}, bf16[16,4096]{1,0:T(8,128)(2,1)S(1)}, u32[]{:S(2)}, u32[]{:S(2)}) collective-permute-start(bf16[16,4096]{1,0:T(8,128)(2,1)S(1)} %get-tuple-element.52), channel_id=1, source_target_pairs={{0,4},{1,5},{2,6},{3,7},{4,0},{5,1},{6,2},{7,3},{8,12},{9,13},{10,... | collective-permute-start | bytes 393224 | tf_op jit(solution)/shard_map/ppermute | solution.py:18
  26.4 7.4 %collective-permute-done.9.refs_3_.refs_2_ = bf16[32,4096]{1,0:T(8,128)(2,1)S(1)} collective-permute-done((bf16[32,4096]{1,0:T(8,128)(2,1)S(1)}, bf16[32,4096]{1,0:T(8,128)(2,1)S(1)}, u32[]{:S(2)}, u32[]{:S(2)}) %collective-permute-start.9) | collective-permute-done | bytes 262176 | tf_op jit(solution)/shard_map/ppermute | solution.py:18
  33.9 6.4 %collective-permute-done.10.refs_4_.refs_3_ = bf16[32,4096]{1,0:T(8,128)(2,1)S(1)} collective-permute-done((bf16[32,4096]{1,0:T(8,128)(2,1)S(1)}, bf16[32,4096]{1,0:T(8,128)(2,1)S(1)}, u32[]{:S(2)}, u32[]{:S(2)}) %collective-permute-start.10) | collective-permute-done | bytes 262176 | tf_op jit(solution)/shard_map/ppermute | solution.py:18
  40.4 0.5 relay.3
  40.9 0.5 collective-permute-start.14
  41.4 0.8 collective-permute-start.15
  42.3 2.2 %collective-permute-start.16 = (bf16[16,4096]{1,0:T(8,128)(2,1)S(1)}, bf16[16,4096]{1,0:T(8,128)(2,1)S(1)}, u32[]{:S(2)}, u32[]{:S(2)}) collective-permute-start(bf16[16,4096]{1,0:T(8,128)(2,1)S(1)} %get-tuple-element.64), channel_id=1, source_target_pairs={{0,6},{1,7},{2,4},{3,5},{4,2},{5,3},{6,0},{7,1},{8,14},{9,15},{10,... | collective-permute-start | bytes 393224 | tf_op jit(solution)/shard_map/ppermute | solution.py:18
  44.4 1.6 %collective-permute-done.6.refs_3_ = bf16[16,4096]{1,0:T(8,128)(2,1)S(1)} collective-permute-done((bf16[16,4096]{1,0:T(8,128)(2,1)S(1)}, bf16[16,4096]{1,0:T(8,128)(2,1)S(1)}, u32[]{:S(2)}, u32[]{:S(2)}) %collective-permute-start.6) | collective-permute-done | bytes 131104 | tf_op jit(solution)/shard_map/ppermute | solution.py:18
  46.0 2.7 %expert.3 = (bf16[16,4096]{1,0:T(8,128)(2,1)S(1)}, bf16[16,4096]{1,0:T(8,128)(2,1)S(1)}, bf16[16,4096]{1,0:T(8,128)(2,1)S(1)}, bf16[16,4096]{1,0:T(8,128)(2,1)S(1)}) custom-call(bf16[16,4096]{1,0:T(8,128)(2,1)S(1)} %get-tuple-element.50.refs_0_, bf16[16,4096]{1,0:T(8,128)(2,1)S(1)} %collective-permute-done.4.refs_1_, ...), custom_call_target="tpu_custom_call" | custom-call | flops 1 | bytes 35000 | tf_op jit(solution)/shard_map/expert/pallas_call | solution.py:351
  48.8 0.5 collective-permute-start.11
  49.7 2.6 %collective-permute-start.13 = (bf16[16,4096]{1,0:T(8,128)(2,1)S(1)}, bf16[16,4096]{1,0:T(8,128)(2,1)S(1)}, u32[]{:S(2)}, u32[]{:S(2)}) collective-permute-start(bf16[16,4096]{1,0:T(8,128)(2,1)S(1)} %get-tuple-element.61), channel_id=1, source_target_pairs={{0,6},{1,7},{2,4},{3,5},{4,2},{5,3},{6,0},{7,1},{8,14},{9,15},{10,... | collective-permute-start | bytes 393224 | tf_op jit(solution)/shard_map/ppermute | solution.py:18
  52.3 2.9 %expert.4 = (bf16[16,4096]{1,0:T(8,128)(2,1)S(1)}, bf16[16,4096]{1,0:T(8,128)(2,1)S(1)}, bf16[16,4096]{1,0:T(8,128)(2,1)S(1)}, bf16[16,4096]{1,0:T(8,128)(2,1)S(1)}) custom-call(bf16[16,4096]{1,0:T(8,128)(2,1)S(1)} %get-tuple-element.57.refs_10_.refs_0_, bf16[16,4096]{1,0:T(8,128)(2,1)S(1)} %collective-permute-done.14.refs_1_, ...), custom_call_target="tpu_custom_call" | custom-call | flops 1 | bytes 35000 | tf_op jit(solution)/shard_map/expert/pallas_call | solution.py:351
  55.2 0.5 collective-permute-start.18
  56.2 2.6 %collective-permute-start.20 = (bf16[16,4096]{1,0:T(8,128)(2,1)S(1)}, bf16[16,4096]{1,0:T(8,128)(2,1)S(1)}, u32[]{:S(2)}, u32[]{:S(2)}) collective-permute-start(bf16[16,4096]{1,0:T(8,128)(2,1)S(1)} %get-tuple-element.71), channel_id=1, source_target_pairs={{0,6},{1,7},{2,4},{3,5},{4,2},{5,3},{6,0},{7,1},{8,14},{9,15},{10,... | collective-permute-start | bytes 393224 | tf_op jit(solution)/shard_map/ppermute | solution.py:18
  58.8 0.5 relay_back.2.refs_10_
  59.3 2.1 %collective-permute-start.17 = (bf16[32,4096]{1,0:T(8,128)(2,1)S(1)}, bf16[32,4096]{1,0:T(8,128)(2,1)S(1)}, u32[]{:S(2)}, u32[]{:S(2)}) collective-permute-start(bf16[32,4096]{1,0:T(8,128)(2,1)S(1)} %relay_back.2.refs_10_), channel_id=1, source_target_pairs={{0,8},{1,9},{2,10},{3,11},{4,12},{5,13},{6,14},{7,15},{8,0},{9,1},... | collective-permute-start | bytes 786440 | tf_op jit(solution)/shard_map/ppermute | solution.py:18
  61.5 2.7 %expert.5 = (bf16[32,4096]{1,0:T(8,128)(2,1)S(1)}, bf16[32,4096]{1,0:T(8,128)(2,1)S(1)}, bf16[32,4096]{1,0:T(8,128)(2,1)S(1)}, bf16[32,4096]{1,0:T(8,128)(2,1)S(1)}) custom-call(bf16[32,4096]{1,0:T(8,128)(2,1)S(1)} %get-tuple-element.49.refs_1_.refs_0_, bf16[32,4096]{1,0:T(8,128)(2,1)S(1)} %collective-permute-done.8.refs_2_.refs_1_, ...), custom_call_target="tpu_custom_call" | custom-call | flops 1 | bytes 14000000 | tf_op jit(solution)/shard_map/expert/pallas_call | solution.py:351
  64.2 2.0 %collective-permute-start.23 = (bf16[32,4096]{1,0:T(8,128)(2,1)S(1)}, bf16[32,4096]{1,0:T(8,128)(2,1)S(1)}, u32[]{:S(2)}, u32[]{:S(2)}) collective-permute-start(bf16[32,4096]{1,0:T(8,128)(2,1)S(1)} %passed.6.refs_4_), channel_id=1, source_target_pairs={{0,6},{1,7},{2,4},{3,5},{4,2},{5,3},{6,0},{7,1},{8,14},{9,15},{10,... | collective-permute-start | bytes 786440 | tf_op jit(solution)/shard_map/ppermute | solution.py:18
  66.2 4.1 %collective-permute-done.20.refs_3_ = bf16[16,4096]{1,0:T(8,128)(2,1)S(1)} collective-permute-done((bf16[16,4096]{1,0:T(8,128)(2,1)S(1)}, bf16[16,4096]{1,0:T(8,128)(2,1)S(1)}, u32[]{:S(2)}, u32[]{:S(2)}) %collective-permute-start.20) | collective-permute-done | bytes 131104 | tf_op jit(solution)/shard_map/ppermute | solution.py:18
  70.3 0.5 relay_back.3.refs_2_
  71.4 11.1 %collective-permute-done.23.refs_6_ = bf16[32,4096]{1,0:T(8,128)(2,1)S(1)} collective-permute-done((bf16[32,4096]{1,0:T(8,128)(2,1)S(1)}, bf16[32,4096]{1,0:T(8,128)(2,1)S(1)}, u32[]{:S(2)}, u32[]{:S(2)}) %collective-permute-start.23) | collective-permute-done | bytes 262176 | tf_op jit(solution)/shard_map/ppermute | solution.py:18
  82.4 3.0 %collective-permute-done.22.refs_5_ = bf16[32,4096]{1,0:T(8,128)(2,1)S(1)} collective-permute-done((bf16[32,4096]{1,0:T(8,128)(2,1)S(1)}, bf16[32,4096]{1,0:T(8,128)(2,1)S(1)}, u32[]{:S(2)}, u32[]{:S(2)}) %collective-permute-start.22) | collective-permute-done | bytes 262176 | tf_op jit(solution)/shard_map/ppermute | solution.py:18
  85.4 0.9 %add_near.1.base_ref = f32[64,4096]{1,0:T(8,128)S(1)} custom-call(f32[4,64]{1,0:T(4,128)S(1)} %get-tuple-element.40.info_ref, f32[32,4096]{1,0:T(8,128)S(1)} %get-tuple-element.41.refs_0_, f32[32,4096]{1,0:T(8,128)S(1)} %get-tuple-element.43.refs_1_, bf16[32,4096]{1,0:T(8,128)(2,1)S(1)} %collective-permute-done.17.refs_2_, ...), custom_call_target="tpu_custom_call" | custom-call | flops 1 | bytes 14000000 | tf_op jit(solution)/shard_map/add_near/pallas_call | solution.py:405
  86.3 0.9 %add_far.1 = bf16[64,4096]{1,0:T(8,128)(2,1)} custom-call(f32[64,4096]{1,0:T(8,128)S(1)} %add_near.1.base_ref, bf16[32,4096]{1,0:T(8,128)(2,1)S(1)} %collective-permute-done.24.far_ref), custom_call_target="tpu_custom_call" | custom-call | flops 1 | bytes 3500000 | tf_op jit(solution)/shard_map/add_far/pallas_call | solution.py:427
  (39 shorter events, 3.4 us)
Async XLA Ops:
  0.0 13.6 %collective-permute-start.1 = (bf16[4096,384]{1,0:T(8,128)(2,1)}, bf16[4096,384]{1,0:T(8,128)(2,1)S(1)}, u32[]{:S(2)}, u32[]{:S(2)}) collective-permute-start(bf16[4096,384]{1,0:T(8,128)(2,1)} %refs_4_.9), channel_id=1, source_target_pairs={{0,1},{1,0},{2,3},{3,2},{4,5},{5,4},{6,7},{7,6},{8,9},{9,8},{10,11... | collective-permute-start | bytes 9437192 | tf_op jit(solution)/shard_map/ppermute | solution.py:18
  0.5 13.1 %collective-permute-start.2 = (bf16[4096,384]{1,0:T(8,128)(2,1)}, bf16[4096,384]{1,0:T(8,128)(2,1)S(1)}, u32[]{:S(2)}, u32[]{:S(2)}) collective-permute-start(bf16[4096,384]{1,0:T(8,128)(2,1)} %refs_5_.9), channel_id=1, source_target_pairs={{0,1},{1,0},{2,3},{3,2},{4,5},{5,4},{6,7},{7,6},{8,9},{9,8},{10,11... | collective-permute-start | bytes 9437192 | tf_op jit(solution)/shard_map/ppermute | solution.py:18
  0.5 14.4 %collective-permute-start.3 = (bf16[384,4096]{1,0:T(8,128)(2,1)}, bf16[384,4096]{1,0:T(8,128)(2,1)S(1)}, u32[]{:S(2)}, u32[]{:S(2)}) collective-permute-start(bf16[384,4096]{1,0:T(8,128)(2,1)} %refs_6_.9), channel_id=1, source_target_pairs={{0,1},{1,0},{2,3},{3,2},{4,5},{5,4},{6,7},{7,6},{8,9},{9,8},{10,11... | collective-permute-start | bytes 9437192 | tf_op jit(solution)/shard_map/ppermute | solution.py:18
  5.7 17.0 %collective-permute-start = (bf16[32,4224]{1,0:T(8,128)(2,1)S(1)}, bf16[32,4224]{1,0:T(8,128)(2,1)S(1)}, u32[]{:S(2)}, u32[]{:S(2)}) collective-permute-start(bf16[32,4224]{1,0:T(8,128)(2,1)S(1)} %get-tuple-element.42.refs_11_), channel_id=1, source_target_pairs={{0,8},{1,9},{2,10},{3,11},{4,12},{5,13},{6,14},{7,15},{8,0},{9,1},... | collective-permute-start | bytes 811016 | tf_op jit(solution)/shard_map/ppermute | solution.py:18
  14.9 31.1 %copy-start = (bf16[4096,384]{1,0:T(8,128)(2,1)S(1)}, bf16[4096,384]{1,0:T(8,128)(2,1)}, u32[]{:S(2)}) copy-start(bf16[4096,384]{1,0:T(8,128)(2,1)} %refs_4_.9) | copy-start | bytes 9437188
  15.0 31.1 %copy-start.1 = (bf16[4096,384]{1,0:T(8,128)(2,1)S(1)}, bf16[4096,384]{1,0:T(8,128)(2,1)}, u32[]{:S(2)}) copy-start(bf16[4096,384]{1,0:T(8,128)(2,1)} %refs_5_.9) | copy-start | bytes 9437188
  15.0 31.1 %copy-start.2 = (bf16[384,4096]{1,0:T(8,128)(2,1)S(1)}, bf16[384,4096]{1,0:T(8,128)(2,1)}, u32[]{:S(2)}) copy-start(bf16[384,4096]{1,0:T(8,128)(2,1)} %refs_6_.9) | copy-start | bytes 9437188
  15.0 9.9 %collective-permute-start.8 = (bf16[32,4096]{1,0:T(8,128)(2,1)S(1)}, bf16[32,4096]{1,0:T(8,128)(2,1)S(1)}, u32[]{:S(2)}, u32[]{:S(2)}) collective-permute-start(bf16[32,4096]{1,0:T(8,128)(2,1)S(1)} %get-tuple-element.54), channel_id=1, source_target_pairs={{0,2},{1,3},{2,0},{3,1},{4,6},{5,7},{6,4},{7,5},{8,10},{9,11},{10,... | collective-permute-start | bytes 786440 | tf_op jit(solution)/shard_map/ppermute | solution.py:18
  18.0 15.8 %collective-permute-start.9 = (bf16[32,4096]{1,0:T(8,128)(2,1)S(1)}, bf16[32,4096]{1,0:T(8,128)(2,1)S(1)}, u32[]{:S(2)}, u32[]{:S(2)}) collective-permute-start(bf16[32,4096]{1,0:T(8,128)(2,1)S(1)} %get-tuple-element.55), channel_id=1, source_target_pairs={{0,4},{1,5},{2,6},{3,7},{4,0},{5,1},{6,2},{7,3},{8,12},{9,13},{10,... | collective-permute-start | bytes 786440 | tf_op jit(solution)/shard_map/ppermute | solution.py:18
  19.6 20.8 %collective-permute-start.7 = (bf16[32,4224]{1,0:T(8,128)(2,1)S(1)}, bf16[32,4224]{1,0:T(8,128)(2,1)S(1)}, u32[]{:S(2)}, u32[]{:S(2)}) collective-permute-start(bf16[32,4224]{1,0:T(8,128)(2,1)S(1)} %passed.5.refs_0_), channel_id=1, source_target_pairs={{0,8},{1,9},{2,10},{3,11},{4,12},{5,13},{6,14},{7,15},{8,0},{9,1},... | collective-permute-start | bytes 811016 | tf_op jit(solution)/shard_map/ppermute | solution.py:18
  22.2 18.1 %collective-permute-start.10 = (bf16[32,4096]{1,0:T(8,128)(2,1)S(1)}, bf16[32,4096]{1,0:T(8,128)(2,1)S(1)}, u32[]{:S(2)}, u32[]{:S(2)}) collective-permute-start(bf16[32,4096]{1,0:T(8,128)(2,1)S(1)} %get-tuple-element.56), channel_id=1, source_target_pairs={{0,6},{1,7},{2,4},{3,5},{4,2},{5,3},{6,0},{7,1},{8,14},{9,15},{10,... | collective-permute-start | bytes 786440 | tf_op jit(solution)/shard_map/ppermute | solution.py:18
  23.1 19.1 %collective-permute-start.4 = (bf16[16,4096]{1,0:T(8,128)(2,1)S(1)}, bf16[16,4096]{1,0:T(8,128)(2,1)S(1)}, u32[]{:S(2)}, u32[]{:S(2)}) collective-permute-start(bf16[16,4096]{1,0:T(8,128)(2,1)S(1)} %get-tuple-element.51), channel_id=1, source_target_pairs={{0,2},{1,3},{2,0},{3,1},{4,6},{5,7},{6,4},{7,5},{8,10},{9,11},{10,... | collective-permute-start | bytes 393224 | tf_op jit(solution)/shard_map/ppermute | solution.py:18
  24.9 19.6 %collective-permute-start.5 = (bf16[16,4096]{1,0:T(8,128)(2,1)S(1)}, bf16[16,4096]{1,0:T(8,128)(2,1)S(1)}, u32[]{:S(2)}, u32[]{:S(2)}) collective-permute-start(bf16[16,4096]{1,0:T(8,128)(2,1)S(1)} %get-tuple-element.52), channel_id=1, source_target_pairs={{0,4},{1,5},{2,6},{3,7},{4,0},{5,1},{6,2},{7,3},{8,12},{9,13},{10,... | collective-permute-start | bytes 393224 | tf_op jit(solution)/shard_map/ppermute | solution.py:18
  33.8 12.3 %collective-permute-start.6 = (bf16[16,4096]{1,0:T(8,128)(2,1)S(1)}, bf16[16,4096]{1,0:T(8,128)(2,1)S(1)}, u32[]{:S(2)}, u32[]{:S(2)}) collective-permute-start(bf16[16,4096]{1,0:T(8,128)(2,1)S(1)} %get-tuple-element.53), channel_id=1, source_target_pairs={{0,6},{1,7},{2,4},{3,5},{4,2},{5,3},{6,0},{7,1},{8,14},{9,15},{10,... | collective-permute-start | bytes 393224 | tf_op jit(solution)/shard_map/ppermute | solution.py:18
  40.9 8.8 %collective-permute-start.14 = (bf16[16,4096]{1,0:T(8,128)(2,1)S(1)}, bf16[16,4096]{1,0:T(8,128)(2,1)S(1)}, u32[]{:S(2)}, u32[]{:S(2)}) collective-permute-start(bf16[16,4096]{1,0:T(8,128)(2,1)S(1)} %get-tuple-element.62), channel_id=1, source_target_pairs={{0,2},{1,3},{2,0},{3,1},{4,6},{5,7},{6,4},{7,5},{8,10},{9,11},{10,... | collective-permute-start | bytes 393224 | tf_op jit(solution)/shard_map/ppermute | solution.py:18
  41.4 10.9 %collective-permute-start.15 = (bf16[16,4096]{1,0:T(8,128)(2,1)S(1)}, bf16[16,4096]{1,0:T(8,128)(2,1)S(1)}, u32[]{:S(2)}, u32[]{:S(2)}) collective-permute-start(bf16[16,4096]{1,0:T(8,128)(2,1)S(1)} %get-tuple-element.63), channel_id=1, source_target_pairs={{0,4},{1,5},{2,6},{3,7},{4,0},{5,1},{6,2},{7,3},{8,12},{9,13},{10,... | collective-permute-start | bytes 393224 | tf_op jit(solution)/shard_map/ppermute | solution.py:18
  42.3 10.1 %collective-permute-start.16 = (bf16[16,4096]{1,0:T(8,128)(2,1)S(1)}, bf16[16,4096]{1,0:T(8,128)(2,1)S(1)}, u32[]{:S(2)}, u32[]{:S(2)}) collective-permute-start(bf16[16,4096]{1,0:T(8,128)(2,1)S(1)} %get-tuple-element.64), channel_id=1, source_target_pairs={{0,6},{1,7},{2,4},{3,5},{4,2},{5,3},{6,0},{7,1},{8,14},{9,15},{10,... | collective-permute-start | bytes 393224 | tf_op jit(solution)/shard_map/ppermute | solution.py:18
  48.8 7.4 %collective-permute-start.11 = (bf16[16,4096]{1,0:T(8,128)(2,1)S(1)}, bf16[16,4096]{1,0:T(8,128)(2,1)S(1)}, u32[]{:S(2)}, u32[]{:S(2)}) collective-permute-start(bf16[16,4096]{1,0:T(8,128)(2,1)S(1)} %get-tuple-element.59), channel_id=1, source_target_pairs={{0,2},{1,3},{2,0},{3,1},{4,6},{5,7},{6,4},{7,5},{8,10},{9,11},{10,... | collective-permute-start | bytes 393224 | tf_op jit(solution)/shard_map/ppermute | solution.py:18
  49.3 9.5 %collective-permute-start.12 = (bf16[16,4096]{1,0:T(8,128)(2,1)S(1)}, bf16[16,4096]{1,0:T(8,128)(2,1)S(1)}, u32[]{:S(2)}, u32[]{:S(2)}) collective-permute-start(bf16[16,4096]{1,0:T(8,128)(2,1)S(1)} %get-tuple-element.60), channel_id=1, source_target_pairs={{0,4},{1,5},{2,6},{3,7},{4,0},{5,1},{6,2},{7,3},{8,12},{9,13},{10,... | collective-permute-start | bytes 393224 | tf_op jit(solution)/shard_map/ppermute | solution.py:18
  49.7 9.1 %collective-permute-start.13 = (bf16[16,4096]{1,0:T(8,128)(2,1)S(1)}, bf16[16,4096]{1,0:T(8,128)(2,1)S(1)}, u32[]{:S(2)}, u32[]{:S(2)}) collective-permute-start(bf16[16,4096]{1,0:T(8,128)(2,1)S(1)} %get-tuple-element.61), channel_id=1, source_target_pairs={{0,6},{1,7},{2,4},{3,5},{4,2},{5,3},{6,0},{7,1},{8,14},{9,15},{10,... | collective-permute-start | bytes 393224 | tf_op jit(solution)/shard_map/ppermute | solution.py:18
  55.2 11.0 %collective-permute-start.18 = (bf16[16,4096]{1,0:T(8,128)(2,1)S(1)}, bf16[16,4096]{1,0:T(8,128)(2,1)S(1)}, u32[]{:S(2)}, u32[]{:S(2)}) collective-permute-start(bf16[16,4096]{1,0:T(8,128)(2,1)S(1)} %get-tuple-element.69), channel_id=1, source_target_pairs={{0,2},{1,3},{2,0},{3,1},{4,6},{5,7},{6,4},{7,5},{8,10},{9,11},{10,... | collective-permute-start | bytes 393224 | tf_op jit(solution)/shard_map/ppermute | solution.py:18
  55.8 10.5 %collective-permute-start.19 = (bf16[16,4096]{1,0:T(8,128)(2,1)S(1)}, bf16[16,4096]{1,0:T(8,128)(2,1)S(1)}, u32[]{:S(2)}, u32[]{:S(2)}) collective-permute-start(bf16[16,4096]{1,0:T(8,128)(2,1)S(1)} %get-tuple-element.70), channel_id=1, source_target_pairs={{0,4},{1,5},{2,6},{3,7},{4,0},{5,1},{6,2},{7,3},{8,12},{9,13},{10,... | collective-permute-start | bytes 393224 | tf_op jit(solution)/shard_map/ppermute | solution.py:18
  56.2 14.2 %collective-permute-start.20 = (bf16[16,4096]{1,0:T(8,128)(2,1)S(1)}, bf16[16,4096]{1,0:T(8,128)(2,1)S(1)}, u32[]{:S(2)}, u32[]{:S(2)}) collective-permute-start(bf16[16,4096]{1,0:T(8,128)(2,1)S(1)} %get-tuple-element.71), channel_id=1, source_target_pairs={{0,6},{1,7},{2,4},{3,5},{4,2},{5,3},{6,0},{7,1},{8,14},{9,15},{10,... | collective-permute-start | bytes 393224 | tf_op jit(solution)/shard_map/ppermute | solution.py:18
  59.3 23.1 %collective-permute-start.17 = (bf16[32,4096]{1,0:T(8,128)(2,1)S(1)}, bf16[32,4096]{1,0:T(8,128)(2,1)S(1)}, u32[]{:S(2)}, u32[]{:S(2)}) collective-permute-start(bf16[32,4096]{1,0:T(8,128)(2,1)S(1)} %relay_back.2.refs_10_), channel_id=1, source_target_pairs={{0,8},{1,9},{2,10},{3,11},{4,12},{5,13},{6,14},{7,15},{8,0},{9,1},... | collective-permute-start | bytes 786440 | tf_op jit(solution)/shard_map/ppermute | solution.py:18
  64.2 18.2 %collective-permute-start.23 = (bf16[32,4096]{1,0:T(8,128)(2,1)S(1)}, bf16[32,4096]{1,0:T(8,128)(2,1)S(1)}, u32[]{:S(2)}, u32[]{:S(2)}) collective-permute-start(bf16[32,4096]{1,0:T(8,128)(2,1)S(1)} %passed.6.refs_4_), channel_id=1, source_target_pairs={{0,6},{1,7},{2,4},{3,5},{4,2},{5,3},{6,0},{7,1},{8,14},{9,15},{10,... | collective-permute-start | bytes 786440 | tf_op jit(solution)/shard_map/ppermute | solution.py:18
  70.9 14.5 %collective-permute-start.22 = (bf16[32,4096]{1,0:T(8,128)(2,1)S(1)}, bf16[32,4096]{1,0:T(8,128)(2,1)S(1)}, u32[]{:S(2)}, u32[]{:S(2)}) collective-permute-start(bf16[32,4096]{1,0:T(8,128)(2,1)S(1)} %get-tuple-element.74), channel_id=1, source_target_pairs={{0,4},{1,5},{2,6},{3,7},{4,0},{5,1},{6,2},{7,3},{8,12},{9,13},{10,... | collective-permute-start | bytes 786440 | tf_op jit(solution)/shard_map/ppermute | solution.py:18
  71.0 14.4 %collective-permute-start.21 = (bf16[32,4096]{1,0:T(8,128)(2,1)S(1)}, bf16[32,4096]{1,0:T(8,128)(2,1)S(1)}, u32[]{:S(2)}, u32[]{:S(2)}) collective-permute-start(bf16[32,4096]{1,0:T(8,128)(2,1)S(1)} %get-tuple-element.73.refs_7_), channel_id=1, source_target_pairs={{0,2},{1,3},{2,0},{3,1},{4,6},{5,7},{6,4},{7,5},{8,10},{9,11},{10,... | collective-permute-start | bytes 786440 | tf_op jit(solution)/shard_map/ppermute | solution.py:18
  71.1 15.2 %collective-permute-start.24 = (bf16[32,4096]{1,0:T(8,128)(2,1)S(1)}, bf16[32,4096]{1,0:T(8,128)(2,1)S(1)}, u32[]{:S(2)}, u32[]{:S(2)}) collective-permute-start(bf16[32,4096]{1,0:T(8,128)(2,1)S(1)} %relay_back.3.refs_2_), channel_id=1, source_target_pairs={{0,8},{1,9},{2,10},{3,11},{4,12},{5,13},{6,14},{7,15},{8,0},{9,1},... | collective-permute-start | bytes 786440 | tf_op jit(solution)/shard_map/ppermute | solution.py:18
